TPU v7x, 32 devices: a whole 2x2x4 slice. The times are simulated.
32 devices in a mesh: strip: 8 (over y, x, core), branch: 4 (over z).
Axes of the slice: x: 2, y: 2, z: 4, core: 2. Of those that a mesh axis runs over, the one named last changes fastest.
Arguments:
- features: bfloat16 [64, 192, 512], P('strip'), may hold values from -6 to 6
- cotangent: bfloat16 [64, 192, 256], P('strip', None, 'branch'), may hold values from -6 to 6
- depth_weight: bfloat16 [4, 9, 512], P('branch'), may hold values from -2 to 2
- point_weight: bfloat16 [4, 512, 256], P('branch'), may hold values from -0.25 to 0.25
- joining_weight: bfloat16 [1024, 256], P('branch'), may hold values from -0.25 to 0.25
- branch_mask: int32 [4], replicated, may hold values from 0 to 1, as said below
Outputs:
- output: bfloat16 [64, 192, 256], P('strip', None, 'branch')
- joining_grad: float32 [1024, 256], P('branch')
- point_grad: float32 [4, 512, 256], P('branch')
- depth_grad: float32 [4, 9, 512], P('branch')
Inputs may be any that keep to these rules, and one draw needn't show every extreme that they name: `branch_mask`: 1 marks an active branch; at least one branch is active and at least one is not.
All inputs are finite; a program needn't handle non-finite values.
Results may differ from a plain program's by a relative error of at most 0.014.
Values may be sent and summed in bfloat16 or wider, within the bound.
No kernel may reach another device: no remote copies, remote signals or barrier semaphores. Data moves between devices by JAX's collectives and lax.ppermute only.
A program may use at most 64 MiB of HBM per device.

v0:
```python
import math

import jax
import jax.numpy as jnp
from jax import lax
from jax.sharding import PartitionSpec as P

DILATION_STEP = 6


tanh_coef = 0.7978845608
cubic_coef = 0.044715
slope_coef = 0.134145


def shifted(value, axis, steps):
    count = lax.axis_size(axis)
    leading, last = (max(0, -steps), min(count, count - steps))
    return lax.ppermute(value, axis, [(source, source + steps) for source in range(leading, last)])


def gelu_tanh(values):
    inner = jnp.tanh(tanh_coef * (values + cubic_coef * values * values * values))
    return 0.5 * values * (1.0 + inner)


def gelu_slope(values):
    inner = jnp.tanh(tanh_coef * (values + cubic_coef * values * values * values))
    return 0.5 * (1.0 + inner) + 0.5 * values * (1.0 - inner * inner) * tanh_coef * (
        1.0 + slope_coef * values * values
    )


def contract_rows(left, right):
    return lax.dot_general(
        left, right, (((0,), (0,)), ((), ())), preferred_element_type=jnp.float32
    )


def contract_cols(left, right):
    return lax.dot_general(
        left, right, (((1,), (1,)), ((), ())), preferred_element_type=jnp.float32
    )


def tap_piece(padded, border_rows, dilation_rate, tap_index, row_count, col_count, chan_count):
    row_start = border_rows + (tap_index // 3 - 1) * dilation_rate
    col_start = border_rows + (tap_index % 3 - 1) * dilation_rate
    return lax.dynamic_slice(padded, (row_start, col_start, 0), (row_count, col_count, chan_count))


def strip_from(features, offset):
    return shifted(features, "strip", offset)


def per_device(features, cotangent, depth_weight, point_weight, joining_weight, branch_mask):
    row_count, col_count, chan_count = features.shape
    pixel_count = row_count * col_count
    strip_count = lax.axis_size("strip")
    branch_total = lax.axis_size("branch")
    local_branch = lax.axis_index("branch")
    dilation_rate = (local_branch + 1) * DILATION_STEP
    border_rows = branch_total * DILATION_STEP
    hop_count = (border_rows + row_count - 1) // row_count
    pixel_scale = 1.0 / math.sqrt(pixel_count * strip_count)
    active = jnp.sum(
        jnp.where(jnp.arange(branch_mask.shape[0]) == local_branch, branch_mask, 0)
    ).astype(jnp.float32)
    above = [strip_from(features, hop) for hop in range(hop_count, 0, -1)]
    below = [strip_from(features, -hop) for hop in range(1, hop_count + 1)]
    stacked = jnp.concatenate(above + [features] + below, 0)
    first_row = hop_count * row_count - border_rows
    padded = stacked
    padded = jnp.pad(padded, ((0, 0), (border_rows, border_rows), (0, 0)))
    kernel = depth_weight[0].astype(jnp.float32)
    summed = jnp.zeros(features.shape, jnp.float32)
    for tap_index in range(9):
        piece = tap_piece(
            padded, border_rows, dilation_rate, tap_index, row_count, col_count, chan_count
        )
        summed = summed + piece.astype(jnp.float32) * kernel[tap_index]
    dw_out = summed.astype(jnp.bfloat16).reshape(pixel_count, chan_count)
    pre_act = jnp.dot(dw_out, point_weight[0], preferred_element_type=jnp.float32)
    branch_out = (gelu_tanh(pre_act) * active).astype(jnp.bfloat16)
    own_width = cotangent.shape[2]
    partial_sum = jnp.dot(branch_out, joining_weight, preferred_element_type=jnp.float32)
    joined_sum = lax.psum_scatter(
        partial_sum.astype(jnp.bfloat16), "branch", scatter_dimension=1, tiled=True
    ).astype(jnp.float32)
    output = gelu_tanh(joined_sum).astype(jnp.bfloat16).reshape(row_count, col_count, own_width)
    grad_joined = (
        cotangent.reshape(pixel_count, own_width).astype(jnp.float32) * gelu_slope(joined_sum)
    ).astype(jnp.bfloat16)
    full_grad = lax.all_gather(grad_joined, "branch", axis=1, tiled=True)
    joining_part = contract_rows(branch_out, full_grad) * pixel_scale
    grad_branch = contract_cols(full_grad, joining_weight) * active
    grad_pre = (grad_branch * gelu_slope(pre_act)).astype(jnp.bfloat16)
    point_part = contract_rows(dw_out, grad_pre) * pixel_scale
    depthwise_gradient = contract_cols(grad_pre, point_weight[0]).reshape(
        row_count, col_count, chan_count
    )
    tap_sums = []
    for tap_index in range(9):
        piece = tap_piece(
            padded, border_rows, dilation_rate, tap_index, row_count, col_count, chan_count
        )
        tap_sums.append(
            jnp.sum(depthwise_gradient * piece.astype(jnp.float32), axis=(0, 1)) * pixel_scale
        )
    depth_part = jnp.stack(tap_sums)
    joining_total, point_total, depth_total = lax.psum(
        (joining_part, point_part, depth_part), "strip"
    )
    return (output, joining_total, point_total[None], depth_total[None])


def solution(mesh):
    placed = (
        P("strip", None, None),
        P("strip", None, "branch"),
        P("branch", None, None),
        P("branch", None, None),
        P("branch", None),
        P(),
    )
    return jax.shard_map(
        per_device,
        mesh=mesh,
        in_specs=placed,
        out_specs=(
            P("strip", None, "branch"),
            P("branch", None),
            P("branch", None, None),
            P("branch", None, None),
        ),
        check_vma=False,
    )
```

profile of v0, /device:TPU:0, one launch (start us, length us, event | category | flops | bytes accessed | tf_op | source)
XLA Modules:
  0.0 281.9 jit_solution(13430187530830106846)
XLA Ops:
  7.2 5.6 %collective-permute-start = (bf16[8,192,512]{2,1,0:T(8,128)(2,1)}, bf16[8,192,512]{2,1,0:T(8,128)(2,1)}, u32[]{:S(2)}, u32[]{:S(2)}) collective-permute-start(bf16[8,192,512]{2,1,0:T(8,128)(2,1)} %param.6), channel_id=1, source_target_pairs={{0,12},{4,16},{8,20},{12,24},{16,28},{1,13},{5,17},{9,21},{13,25},... | collective-permute-start | bytes 4718600 | tf_op jit(solution)/shard_map/ppermute | solution.py:19
  12.8 3.5 %collective-permute-start.1 = (bf16[8,192,512]{2,1,0:T(8,128)(2,1)}, bf16[8,192,512]{2,1,0:T(8,128)(2,1)S(1)}, u32[]{:S(2)}, u32[]{:S(2)}) collective-permute-start(bf16[8,192,512]{2,1,0:T(8,128)(2,1)} %param.6), channel_id=1, source_target_pairs={{0,8},{4,12},{8,16},{12,20},{16,24},{20,28},{1,9},{5,13},{9,17},{1... | collective-permute-start | bytes 4718600 | tf_op jit(solution)/shard_map/ppermute | solution.py:19
  16.3 2.4 collective-permute-start.2
  21.3 22.2 %collective-permute-done = bf16[8,192,512]{2,1,0:T(8,128)(2,1)} collective-permute-done((bf16[8,192,512]{2,1,0:T(8,128)(2,1)}, bf16[8,192,512]{2,1,0:T(8,128)(2,1)}, u32[]{:S(2)}, u32[]{:S(2)}) %collective-permute-start) | collective-permute-done | bytes 1572896 | tf_op jit(solution)/shard_map/ppermute | solution.py:19
  47.8 1.5 constant_dynamic-update-slice_fusion.6
  49.3 27.9 %collective-permute-done.1 = bf16[8,192,512]{2,1,0:T(8,128)(2,1)S(1)} collective-permute-done((bf16[8,192,512]{2,1,0:T(8,128)(2,1)}, bf16[8,192,512]{2,1,0:T(8,128)(2,1)S(1)}, u32[]{:S(2)}, u32[]{:S(2)}) %collective-permute-start.1) | collective-permute-done | bytes 1572896 | tf_op jit(solution)/shard_map/ppermute | solution.py:19
  77.4 1.6 constant_dynamic-update-slice_fusion.4
  79.5 1.5 constant_dynamic-update-slice_fusion.2
  81.0 66.8 %collective-permute-done.4 = bf16[8,192,512]{2,1,0:T(8,128)(2,1)S(1)} collective-permute-done((bf16[8,192,512]{2,1,0:T(8,128)(2,1)}, bf16[8,192,512]{2,1,0:T(8,128)(2,1)S(1)}, u32[]{:S(2)}, u32[]{:S(2)}) %collective-permute-start.4) | collective-permute-done | bytes 1572896 | tf_op jit(solution)/shard_map/ppermute | solution.py:19
  147.9 1.9 collective-permute-done.5
  149.8 1.5 constant_dynamic-update-slice_fusion
  151.4 5.1 %fusion.8 = bf16[8,192,512]{2,1,0:T(8,128)(2,1)S(1)} fusion(bf16[8,192,512]{2,1,0:T(8,128)(2,1)S(1)} %copy-done.2, f32[512]{0:T(512)S(1)} %bitcast.52, f32[512]{0:T(512)S(1)} %bitcast.51, f32[512]{0:T(512)S(1)} %bitcast.50, f32[512]{0:T(512)S(1)} %bitcast.49, f32[512]{0:T(512)S(1)} %bitcast.48, f32[512]{0:T(512)S(1)} %bitcast.47, f32[512]{0:T(512)S(1)} %bitcast.46, ...), kind=kLoop, calls=%fused_computation.34 | loop fusion | flops 21233664 | bytes 14174224 | tf_op jit(solution)/shard_map/convert_element_type | solution.py:82
  158.3 1.7 convolution_convert_fusion
  160.1 1.9 copy.10
  162.0 2.0 reshape.130
  164.0 19.8 %reduce-scatter.2.cloned.1.call-done = bf16[1536,64]{0,1:T(8,128)(2,1)} async-done(((bf16[1536,256]{0,1:T(8,128)(2,1)}), bf16[1536,64]{0,1:T(8,128)(2,1)}) %reduce-scatter.2.cloned.1.call-update) | async-done | bytes 196624 | tf_op jit(solution)/shard_map/reduce_scatter | solution.py:87
  183.7 2.1 fusion.33
  185.8 18.1 %all_gather.3 = bf16[1536,256]{0,1:T(8,128)(2,1)S(1)} all-gather(bf16[1536,64]{0,1:T(8,128)(2,1)S(1)} %get-tuple-element.19), channel_id=1, replica_groups=mesh['strip'=8,'branch'=4] {'branch'}, dimensions={1}, use_global_device_ids=true | all-gather | bytes 983040 | tf_op jit(solution)/shard_map/all_gather | solution.py:94
  205.2 1.4 convolution_multiply_fusion.2
  208.0 8.7 %fusion.17 = (f32[512]{0:T(512)S(1)}, f32[512]{0:T(512)S(1)}, f32[512]{0:T(512)S(1)}, f32[512]{0:T(512)S(1)}, f32[512]{0:T(512)S(1)}, /*index=5*/f32[512]{0:T(51...) fusion(s32[]{:T(128)S(6)} %select_n.15, s32[]{:T(128)S(6)} %select_n.14, bf16[56,192,512]{2,1,0:T(8,128)(2,1)} %copy-done.1, ...), kind=kOutput, calls=%fused_computation.43 | convolution fusion | flops 423882240 | bytes 13649936 | tf_op jit(solution)/shard_map/dot_general | solution.py:41
  217.9 22.9 %psum.23 = f32[1,9,512]{2,0,1:T(1,128)} all-reduce(f32[1,9,512]{2,0,1:T(1,128)S(1)} %broadcast_in_dim.12), channel_id=1, replica_groups=mesh['strip'=8,'branch'=4] {'strip'}, use_global_device_ids=true, to_apply=%region_13.14 | all-reduce | flops 4608 | bytes 36864 | tf_op jit(solution)/shard_map/psum | solution.py:111
  240.9 30.7 %all-reduce.4.cloned.1.call-done = (f32[256,256]{1,0:T(8,128)}, f32[1,512,256]{2,1,0:T(8,128)}) async-done(((f32[256,256]{1,0:T(8,128)}, f32[1,512,256]{2,1,0:T(8,128)}), (f32[256,256]{1,0:T(8,128)}, f32[1,512,256]{2,1,0:T(8,128)})) %all-reduce.4.cloned.1.call-update) | async-done | bytes 786448 | tf_op jit(solution)/shard_map/psum | solution.py:111
  271.6 1.7 copy.20
  273.2 1.9 copy.21
  (42 shorter events, 12.4 us)
Async XLA Ops:
  7.2 149.4 %copy-start = (bf16[1,512,256]{2,1,0:T(8,128)(2,1)S(1)}, bf16[1,512,256]{2,1,0:T(8,128)(2,1)}, u32[]{:S(2)}) copy-start(bf16[1,512,256]{2,1,0:T(8,128)(2,1)} %param.9) | copy-start | bytes 786436
  7.2 176.5 %reduce-scatter.2.cloned.1.call-start = ((), (), s32[]{:S(2)}) async-start(), calls=%async_computation.1 | async-start | bytes 983040 | tf_op jit(solution)/shard_map/reduce_scatter | solution.py:87
  7.2 36.3 %collective-permute-start = (bf16[8,192,512]{2,1,0:T(8,128)(2,1)}, bf16[8,192,512]{2,1,0:T(8,128)(2,1)}, u32[]{:S(2)}, u32[]{:S(2)}) collective-permute-start(bf16[8,192,512]{2,1,0:T(8,128)(2,1)} %param.6), channel_id=1, source_target_pairs={{0,12},{4,16},{8,20},{12,24},{16,28},{1,13},{5,17},{9,21},{13,25},... | collective-permute-start | bytes 4718600 | tf_op jit(solution)/shard_map/ppermute | solution.py:19
  12.8 64.4 %collective-permute-start.1 = (bf16[8,192,512]{2,1,0:T(8,128)(2,1)}, bf16[8,192,512]{2,1,0:T(8,128)(2,1)S(1)}, u32[]{:S(2)}, u32[]{:S(2)}) collective-permute-start(bf16[8,192,512]{2,1,0:T(8,128)(2,1)} %param.6), channel_id=1, source_target_pairs={{0,8},{4,12},{8,16},{12,20},{16,24},{20,28},{1,9},{5,13},{9,17},{1... | collective-permute-start | bytes 4718600 | tf_op jit(solution)/shard_map/ppermute | solution.py:19
  16.3 61.1 %collective-permute-start.2 = (bf16[8,192,512]{2,1,0:T(8,128)(2,1)}, bf16[8,192,512]{2,1,0:T(8,128)(2,1)}, u32[]{:S(2)}, u32[]{:S(2)}) collective-permute-start(bf16[8,192,512]{2,1,0:T(8,128)(2,1)} %param.6), channel_id=1, source_target_pairs={{0,4},{4,8},{8,12},{12,16},{16,20},{20,24},{24,28},{1,5},{5,9},{9,... | collective-permute-start | bytes 4718600 | tf_op jit(solution)/shard_map/ppermute | solution.py:19
  18.7 60.7 %collective-permute-start.3 = (bf16[8,192,512]{2,1,0:T(8,128)(2,1)}, bf16[8,192,512]{2,1,0:T(8,128)(2,1)}, u32[]{:S(2)}, u32[]{:S(2)}) collective-permute-start(bf16[8,192,512]{2,1,0:T(8,128)(2,1)} %param.6), channel_id=1, source_target_pairs={{4,0},{8,4},{12,8},{16,12},{20,16},{24,20},{28,24},{5,1},{9,5},{13... | collective-permute-start | bytes 4718600 | tf_op jit(solution)/shard_map/ppermute | solution.py:19
  20.0 127.7 %collective-permute-start.4 = (bf16[8,192,512]{2,1,0:T(8,128)(2,1)}, bf16[8,192,512]{2,1,0:T(8,128)(2,1)S(1)}, u32[]{:S(2)}, u32[]{:S(2)}) collective-permute-start(bf16[8,192,512]{2,1,0:T(8,128)(2,1)} %param.6), channel_id=1, source_target_pairs={{8,0},{12,4},{16,8},{20,12},{24,16},{28,20},{9,1},{13,5},{17,9},{2... | collective-permute-start | bytes 4718600 | tf_op jit(solution)/shard_map/ppermute | solution.py:19
  43.5 106.3 %collective-permute-start.5 = (bf16[8,192,512]{2,1,0:T(8,128)(2,1)}, bf16[8,192,512]{2,1,0:T(8,128)(2,1)}, u32[]{:S(2)}, u32[]{:S(2)}) collective-permute-start(bf16[8,192,512]{2,1,0:T(8,128)(2,1)} %param.6), channel_id=1, source_target_pairs={{12,0},{16,4},{20,8},{24,12},{28,16},{13,1},{17,5},{21,9},{25,13},... | collective-permute-start | bytes 4718600 | tf_op jit(solution)/shard_map/ppermute | solution.py:19
  77.4 1.9 copy-start.2
  151.4 5.2 %copy-start.1 = (bf16[56,192,512]{2,1,0:T(8,128)(2,1)}, bf16[56,192,512]{2,1,0:T(8,128)(2,1)S(1)}, u32[]{:S(2)}) copy-start(bf16[56,192,512]{2,1,0:T(8,128)(2,1)S(1)} %constant_dynamic-update-slice_fusion) | copy-start | bytes 33030148
  156.5 1.7 copy-start.6
  157.1 1.1 copy-start.3
  160.0 111.5 %all-reduce.4.cloned.1.call-start = ((), (), s32[]{:S(2)}) async-start(), calls=%async_computation.2 | async-start | bytes 1572864 | tf_op jit(solution)/shard_map/psum | solution.py:111
  183.7 20.3 %copy-start.4 = (f32[1536,256]{1,0:T(8,128)S(1)}, f32[1536,256]{1,0:T(8,128)}, u32[]{:S(2)}) copy-start(f32[1536,256]{1,0:T(8,128)} %copy-done.3) | copy-start | bytes 4718596
  205.2 1.4 copy-start.7
  208.0 8.9 %copy-start.5 = (bf16[1536,64]{0,1:T(8,128)(2,1)S(1)}, bf16[1536,64]{0,1:T(8,128)(2,1)}, u32[]{:S(2)}) copy-start(bf16[1536,64]{0,1:T(8,128)(2,1)} %get-tuple-element.20) | copy-start | bytes 589828
Sparse Core Ops, SparseCore 0:
  160.1 23.5 reduce-scatter.1
  217.0 54.5 all-reduce.3
where the time goes:
time: 283 us; the launch traced here: 282 us
  waiting for transfers between devices  169 us (60%)
  blocking collectives  41.1 us (15%)
  local copies, waits for them, and re-layouts  17.5 us (6%)
  starting transfers between devices  15.4 us (5%)
  matrix products  15.1 us (5%)
  between operations  14.9 us (5%)
  other arithmetic  8.57 us (3%)
    ppermute x6, waiting for transfers between devices, shifted(): lax.ppermute(value, axis, [(source, source + steps) for source in range(l...  119 us
    psum x1, waiting for transfers between devices, per_device(): lax.psum((joining_part, point_part, depth_part), 'strip')  30.7 us
    psum x1, blocking collectives, per_device(): lax.psum((joining_part, point_part, depth_part), 'strip')  22.9 us
    reduce_scatter x1, waiting for transfers between devices, per_device(): lax.psum_scatter(partial_sum.astype(jnp.bfloat16), 'branch', scatter_dime...  19.8 us
    all_gather x1, blocking collectives, per_device(): full_grad = lax.all_gather(grad_joined, 'branch', axis=1, tiled=True)  18.1 us
    ppermute x6, starting transfers between devices, shifted(): lax.ppermute(value, axis, [(source, source + steps) for source in range(l...  15.4 us
    unnamed x25, local copies, waits for them, and re-layouts  10.8 us
    dot_general x2, matrix products, contract_cols(): lax.dot_general(left, right, (((1,), (1,)), ((), ())), preferred_element_...  9.93 us
  transfers between devices with their start and end apart: 8, of which 6 were waited for; matrix products, arithmetic and copies ran while one was open for 4% of the time, Pallas kernels for 0%

commit v1 on v0

v1 whole, which is shorter than its diff:
```python
import functools
import math

import jax
import jax.numpy as jnp
from jax import lax
from jax.experimental import pallas as pl
from jax.experimental.pallas import tpu as pltpu
from jax.sharding import PartitionSpec as P

DILATION_STEP = 6
GROUP = 8
CHIPS = 4
SLOTS = 3

tanh_coef = 0.7978845608
cubic_coef = 0.044715
slope_coef = 0.134145

f32, bf16, i32 = jnp.float32, jnp.bfloat16, jnp.int32
VMEM = pl.BlockSpec(memory_space=pltpu.VMEM)
SMEM = pl.BlockSpec(memory_space=pltpu.SMEM)
ANY = pl.BlockSpec(memory_space=pl.ANY)


def gelu_both(values):
    square = values * values
    inner = jnp.tanh(tanh_coef * (values + cubic_coef * values * square))
    half = 0.5 * (1.0 + inner)
    slope = half + 0.5 * values * (1.0 - inner * inner) * tanh_coef * (1.0 + slope_coef * square)
    return values * half, slope


def dot(left, right, dims=((1,), (0,))):
    return lax.dot_general(left, right, (dims, ((), ())), preferred_element_type=f32)


def iota(shape, dim):
    return lax.broadcasted_iota(i32, shape, dim)


def one_hot(mask):
    return jnp.where(mask, 1.0, 0.0).astype(bf16)


class Plan:
    def __init__(self, row_count, col_count, chan_count, width, branches):
        self.rows, self.cols, self.chans, self.width, self.branches = row_count, col_count, chan_count, width, branches
        self.classes = DILATION_STEP
        self.run = col_count // DILATION_STEP
        self.work = col_count // (branches * CHIPS)
        self.taps_t = row_count // 2
        self.sub_rows = GROUP * self.taps_t
        self.pixels = self.sub_rows * self.work
        self.lanes = chan_count // 128
        self.window = max(self.segments(m)[5] for m in range(branches * CHIPS))
        self.piece = self.window * self.taps_t
        self.part = width // branches
        self.step_rows = DILATION_STEP // 2
        self.pad = -(-self.step_rows * branches // 16) * 16
        self.tall = self.pad + self.sub_rows + self.pad
        self.grad_rows = (width + chan_count) // GROUP
        self.join_rows = width // GROUP
        self.point_rows = chan_count // GROUP
        self.tile = 2 * self.work

    def segments(self, m):
        smaller, larger = (min, max) if isinstance(m, int) else (jnp.minimum, jnp.maximum)
        first = m * self.work
        klass = first // self.run
        start = first - klass * self.run
        length = smaller(self.work, self.run - start)
        low = larger(0, start - self.branches)
        size = smaller(self.run, start + length + self.branches) - low
        rest = self.work - length
        if isinstance(m, int):
            total = size + (min(self.run, rest + self.branches) if rest else 0)
        else:
            total = size + jnp.where(rest > 0, jnp.minimum(self.run, rest + self.branches), 0)
        return klass, start, length, low, size, total

    def column(self, m, w):
        klass, start, length, _, _, _ = self.segments(m)
        return jnp.where(w < length, self.classes * (start + w) + klass, self.classes * (w - length) + klass + 1)

    def window_column(self, m, j):
        klass, _, _, low, size, total = self.segments(m)
        inside = jnp.where(j < size, self.classes * (low + j) + klass, self.classes * (j - size) + klass + 1)
        return jnp.where(j < total, inside, -(1 << 20))

    def neighbour(self, segments, w, shift):
        _, start, length, low, size, _ = segments
        first = w < length
        place = jnp.where(first, start + w, w - length) + shift
        found = jnp.where(first, place - low, size + place)
        return jnp.where(jnp.logical_and(place >= 0, place < self.run), found, self.window)


def whereabouts():
    strip = lax.axis_index("strip") % GROUP
    return lax.axis_index("branch"), strip, strip // 2, strip % 2


def slots_of(mask_ref, branches):
    slots, count = [], 0
    for branch in range(branches):
        slots.append(jnp.minimum(count, SLOTS - 1) + 0 * mask_ref[branch])
        count = count + mask_ref[branch]
    return slots, count


def pick(values, index):
    result = values[0]
    for place in range(1, len(values)):
        result = jnp.where(index == place, values[place], result)
    return result


def spread_kernel(plan, features_ref, *out_refs):
    plane, _, chip, core = whereabouts()
    depth = plan.taps_t * plan.cols
    targets = []
    for hop in range(CHIPS):
        m = plane * CHIPS + (chip ^ hop)
        row = iota((plan.piece, 128), 0)
        column = plan.window_column(m, row // plan.taps_t)
        targets.append(column + (row % plan.taps_t) * plan.cols)
    target = jnp.concatenate(targets, 0)
    lane = iota(target.shape, 1)
    chosen = jnp.concatenate([one_hot(target == lane + 128 * k) for k in range(depth // 128)], 1)
    for flip in range(2):
        parity = core ^ flip
        rows = jnp.concatenate([features_ref[2 * t + parity] for t in range(plan.taps_t)], 0)
        found = dot(chosen, rows).astype(bf16)
        for hop in range(CHIPS):
            out_refs[2 * hop + flip][...] = found[hop * plan.piece:(hop + 1) * plan.piece]


def spread_features(plan, features):
    return pl.pallas_call(
        functools.partial(spread_kernel, plan),
        out_shape=[jax.ShapeDtypeStruct((plan.piece, plan.chans), bf16)] * GROUP,
        in_specs=[VMEM],
        out_specs=[VMEM] * GROUP,
        compiler_params=pltpu.CompilerParams(vmem_limit_bytes=40 << 20),
        name="spread_features",
    )(features)


def tile_columns(plan):
    blocks = []
    for chip in range(CHIPS):
        for plane in range(plan.branches):
            row = iota((plan.tile, 128), 0)
            column = plan.column(plane * CHIPS + chip, row // 2)
            blocks.append(column + (row % 2) * plan.cols)
    return jnp.concatenate(blocks, 0)


def tile_selector(plan):
    target = tile_columns(plan)
    lane = iota(target.shape, 1)
    return jnp.concatenate([one_hot(target == lane + 128 * k) for k in range(2 * plan.cols // 128)], 1)


def send_cotangent_kernel(plan, cotangent_ref, out_ref):
    chosen = tile_selector(plan)
    halves = []
    for parity in range(2):
        rows = []
        for low in range(2):
            pair = [cotangent_ref[2 * (2 * high + low) + parity].astype(f32) for high in range(2)]
            rows.append(jnp.concatenate(pair, 1))
        halves.append(jnp.concatenate(rows, 0))
    found = dot(chosen, jnp.concatenate(halves, 1).astype(bf16))
    for chip in range(CHIPS):
        for parity in range(2):
            for plane in range(plan.branches):
                at = (chip * plan.branches + plane) * plan.tile
                out_ref[(2 * chip + parity) * plan.branches + plane] = found[
                    at:at + plan.tile, parity * 128:(parity + 1) * 128
                ].astype(bf16)


def send_cotangent(plan, cotangent):
    return pl.pallas_call(
        functools.partial(send_cotangent_kernel, plan),
        out_shape=jax.ShapeDtypeStruct((GROUP * plan.branches, plan.tile, 128), bf16),
        in_specs=[VMEM],
        out_specs=VMEM,
        compiler_params=pltpu.CompilerParams(vmem_limit_bytes=40 << 20),
        name="send_cotangent",
    )(cotangent)


def place_output_kernel(plan, tiles_ref, out_ref):
    chosen = tile_selector(plan)
    halves = []
    for parity in range(2):
        blocks = []
        for chip in range(CHIPS):
            for plane in range(plan.branches):
                blocks.append(tiles_ref[(2 * chip + parity) * plan.branches + plane].astype(f32))
        halves.append(jnp.concatenate(blocks, 0))
    found = dot(chosen, jnp.concatenate(halves, 1).astype(bf16), ((0,), (0,))).astype(bf16)
    for parity in range(2):
        for high in range(2):
            for low in range(2):
                lane = parity * 128 + high * 64
                out_ref[2 * (2 * high + low) + parity] = found[low * plan.cols:(low + 1) * plan.cols, lane:lane + 64]


def place_output(plan, tiles):
    return pl.pallas_call(
        functools.partial(place_output_kernel, plan),
        out_shape=jax.ShapeDtypeStruct((plan.rows, plan.cols, plan.part), bf16),
        in_specs=[VMEM],
        out_specs=VMEM,
        compiler_params=pltpu.CompilerParams(vmem_limit_bytes=40 << 20),
        name="place_output",
    )(tiles)


def swap_halves(left, right):
    low = iota(left.shape, 1) < 64
    return (
        jnp.where(low, left, pltpu.roll(right, 64, 1)),
        jnp.where(low, pltpu.roll(left, 64, 1), right),
    )


def main_kernel(plan, scale, halo, mask_ref, cotangent_ref, *refs):
    count = GROUP + (2 if halo else 0)
    piece_refs, refs = refs[:GROUP], refs[count:] if not halo else refs[GROUP:]
    halo_refs, refs = (refs[:2], refs[2:]) if halo else ((), refs)
    branches, width, chans = plan.branches, plan.width, plan.chans
    depth_refs, refs = refs[:branches], refs[branches:]
    (point_ref, joining_ref), refs = refs[:2], refs[2:]
    mine_refs, refs = refs[:branches - 1], refs[branches - 1:]
    other_refs, refs = refs[:branches - 1], refs[branches - 1:]
    output_ref, keep_ref, send_ref = refs[:3]
    (pieces, halo_pieces, depth, point, joining, spread, dw_out, branch_out, slope, grad_dw, joined, sorted_rows, dgrad,
     grads, sems) = refs[3:]
    plane, strip, chip, core = whereabouts()
    slots, active_count = slots_of(mask_ref, branches)

    copies = []

    def fetch(source, target):
        copy = pltpu.make_async_copy(source, target, sems.at[len(copies)])
        copy.start()
        copies.append(copy)

    for hop in range(GROUP):
        fetch(piece_refs[hop], pieces.at[strip ^ hop])
    for place, ref in enumerate(halo_refs):
        fetch(ref, halo_pieces.at[place])
    for hop in range(branches):
        fetch(depth_refs[hop].at[0], depth.at[plane ^ hop])
    early = len(copies)
    fetch(point_ref.at[0], point.at[plane])
    fetch(joining_ref, joining.at[plane])
    half_point, half_join = chans // 2, width // 2
    for hop in range(1, branches):
        for side, ref in ((core, mine_refs[hop - 1]), (1 - core, other_refs[hop - 1])):
            at_point = pl.multiple_of(side * half_point, half_point)
            at_join = pl.multiple_of(side * half_join, half_join)
            fetch(ref.at[pl.ds(0, half_point)], point.at[plane ^ hop, pl.ds(at_point, half_point)])
            fetch(ref.at[pl.ds(half_point, half_join)], joining.at[plane ^ hop, pl.ds(at_join, half_join)])

    for group in range(plan.lanes):
        edge = jnp.zeros((plan.window, plan.pad, 128), f32)
        spread[group, 0:plan.window, 0:plan.pad] = edge
        spread[group, 0:plan.window, plan.pad + plan.sub_rows:plan.tall] = edge
        spread[group, plan.window] = jnp.zeros((plan.tall, 128), f32)
    grads[...] = jnp.zeros_like(grads)
    joined[...] = jnp.zeros_like(joined)
    for copy in copies[:early]:
        copy.wait()

    low_rows = iota((8, 128), 0) < 4

    def lay(source, place, row):
        @pl.loop(0, plan.piece // 16)
        def _(quad):
            at = pl.multiple_of(quad * 16, 16)
            for group in range(plan.lanes):
                lanes = pl.ds(group * 128, 128)
                upper = source[place, pl.ds(at, 16), lanes].astype(f32)
                lower = source[place + 1, pl.ds(at, 16), lanes].astype(f32)
                for part in range(2):
                    a, b = upper[8 * part:8 * part + 8], lower[8 * part:8 * part + 8]
                    column = quad * 4 + 2 * part
                    spread[group, column, row:row + 8] = jnp.where(low_rows, a, pltpu.roll(b, 4, 0))
                    spread[group, column + 1, row:row + 8] = jnp.where(low_rows, pltpu.roll(a, 4, 0), b)

    for pair in range(CHIPS):
        lay(pieces, 2 * pair, plan.pad + 8 * pair)
    if halo:
        for pair in range(2):
            lay(halo_pieces.at[0], 2 * pair, plan.pad - 16 + 8 * pair)
            lay(halo_pieces.at[1], 2 * pair, plan.pad + plan.sub_rows + 8 * pair)

    segments = plan.segments(plane * CHIPS + chip)

    for branch in range(branches):
        @pl.when(mask_ref[branch] > 0)
        def _():
            taps = depth[branch].astype(f32)
            for group in range(plan.lanes):
                kernel = [
                    jnp.broadcast_to(taps[tap:tap + 1, group * 128:(group + 1) * 128], (plan.sub_rows, 128))
                    for tap in range(9)
                ]

                @pl.loop(0, plan.work)
                def _(w):
                    total = None
                    for j in range(3):
                        column = plan.neighbour(segments, w, (j - 1) * (branch + 1))
                        for i in range(3):
                            row = plan.pad + (i - 1) * plan.step_rows * (branch + 1)
                            term = spread[group, column, row:row + plan.sub_rows] * kernel[3 * i + j]
                            total = term if total is None else total + term
                    at = pl.multiple_of(w * plan.sub_rows, plan.sub_rows)
                    dw_out[branch, pl.ds(at, plan.sub_rows), group * 128:(group + 1) * 128] = total.astype(bf16)

    for copy in copies[early:]:
        copy.wait()

    @pl.loop(0, branches)
    def _(branch):
        @pl.when(mask_ref[branch] > 0)
        def _():
            value, derivative = gelu_both(dot(dw_out[branch], point[branch]))
            value = value.astype(bf16)
            branch_out[branch] = value
            slope[branch] = derivative
            joined[...] += dot(value, joining[branch])

    pixel = iota((plan.pixels, 128), 0)
    column, row = pixel // plan.sub_rows, pixel % plan.sub_rows
    source = (row // 2) * plan.tile + 2 * column + row % 2
    lane = iota(source.shape, 1)
    order = jnp.concatenate([one_hot(source == lane + 128 * k) for k in range(plan.pixels // 128)], 1)
    pixel = iota((plan.pixels, plan.pixels), 1)
    column, row = pixel // plan.sub_rows, pixel % plan.sub_rows
    source = (row // 2) * plan.tile + 2 * column + row % 2
    back = one_hot(source == iota(source.shape, 0))
    for pair in range(GROUP):
        for couple in range(branches // 2):
            left = cotangent_ref[pair * branches + 2 * couple].astype(f32)
            right = cotangent_ref[pair * branches + 2 * couple + 1].astype(f32)
            first, second = swap_halves(left, right)
            lanes = pl.ds(couple * 128, 128)
            sorted_rows[pl.ds(2 * pair * plan.tile, plan.tile), lanes] = first
            sorted_rows[pl.ds((2 * pair + 1) * plan.tile, plan.tile), lanes] = second
    cotangent = dot(order, sorted_rows[...].astype(bf16))
    value, derivative = gelu_both(joined[...])
    grad_joined = (cotangent * derivative).astype(bf16)
    sorted_rows[...] = dot(back, value.astype(bf16))
    for pair in range(GROUP):
        for couple in range(branches // 2):
            lanes = pl.ds(couple * 128, 128)
            left = sorted_rows[pl.ds(2 * pair * plan.tile, plan.tile), lanes]
            right = sorted_rows[pl.ds((2 * pair + 1) * plan.tile, plan.tile), lanes]
            first, second = swap_halves(left, right)
            output_ref[pair * branches + 2 * couple] = first.astype(bf16)
            output_ref[pair * branches + 2 * couple + 1] = second.astype(bf16)

    for branch in range(branches):
        slot = slots[branch]

        @pl.when(mask_ref[branch] > 0)
        def _():
            at = pl.multiple_of(slot * plan.grad_rows, 32)
            joining_part = (dot(branch_out[branch], grad_joined, ((0,), (0,))) * scale).astype(bf16)
            for chunk in range(GROUP):
                grads[chunk, pl.ds(at, plan.join_rows)] = joining_part[chunk * plan.join_rows:(chunk + 1) * plan.join_rows]
            grad_branch = dot(grad_joined, joining[branch], ((1,), (1,)))
            grad_pre = (grad_branch * slope[branch]).astype(bf16)
            at = pl.multiple_of(slot * plan.grad_rows + plan.join_rows, 32)
            point_part = (dot(dw_out[branch], grad_pre, ((0,), (0,))) * scale).astype(bf16)
            for chunk in range(GROUP):
                grads[chunk, pl.ds(at, plan.point_rows)] = point_part[
                    chunk * plan.point_rows:(chunk + 1) * plan.point_rows
                ]
            for group in range(plan.lanes):
                grad_dw[group] = dot(grad_pre, point[branch, group * 128:(group + 1) * 128], ((1,), (1,)))
            for group in range(plan.lanes):
                def add_column(w, sums):
                    at = pl.multiple_of(w * plan.sub_rows, plan.sub_rows)
                    given = grad_dw[group, pl.ds(at, plan.sub_rows)]
                    sums = list(sums)
                    for j in range(3):
                        column = plan.neighbour(segments, w, (j - 1) * (branch + 1))
                        for i in range(3):
                            row = plan.pad + (i - 1) * plan.step_rows * (branch + 1)
                            product = spread[group, column, row:row + plan.sub_rows] * given
                            for part in range(plan.sub_rows // 8):
                                sums[3 * i + j] = sums[3 * i + j] + product[8 * part:8 * part + 8]
                    return tuple(sums)

                sums = lax.fori_loop(0, plan.work, add_column, (jnp.zeros((8, 128), f32),) * 9)
                for tap in range(9):
                    dgrad[tap:tap + 1] = jnp.sum(sums[tap], axis=0, keepdims=True) * scale
                lanes = pl.ds(pl.multiple_of((slot % 2) * 128, 128), 128)
                grads[(slot // 2) * CHIPS + group, SLOTS * plan.grad_rows:, lanes] = dgrad[...].astype(bf16)

    half = GROUP // 2
    first = pltpu.make_async_copy(grads.at[pl.ds((1 - core) * half, half)], send_ref, sems.at[0])
    second = pltpu.make_async_copy(grads.at[pl.ds(core * half, half)], keep_ref, sems.at[1])
    first.start()
    second.start()
    first.wait()
    second.wait()


def main_step(plan, scale, mask, cotangent, pieces, halos, depths, point, joining, mine, others):
    halo = len(halos) > 0
    message = SLOTS * plan.grad_rows + 16
    operands = [mask, cotangent, *pieces, *halos, *depths, point, joining, *mine, *others]
    return pl.pallas_call(
        functools.partial(main_kernel, plan, scale, halo),
        out_shape=[
            jax.ShapeDtypeStruct(cotangent.shape, bf16),
            jax.ShapeDtypeStruct((GROUP // 2, message, plan.width), bf16),
            jax.ShapeDtypeStruct((GROUP // 2, message, plan.width), bf16),
        ],
        in_specs=[SMEM, VMEM] + [ANY] * (len(operands) - 2),
        out_specs=[VMEM, ANY, ANY],
        scratch_shapes=[
            pltpu.VMEM((GROUP, plan.piece, plan.chans), bf16),
            pltpu.VMEM((2, 4, plan.piece, plan.chans) if halo else (16, 128), bf16),
            pltpu.VMEM((plan.branches, 9, plan.chans), bf16),
            pltpu.VMEM((plan.branches, plan.chans, plan.width), bf16),
            pltpu.VMEM((plan.branches, plan.width, plan.width), bf16),
            pltpu.VMEM((plan.lanes, plan.window + 1, plan.tall, 128), f32),
            pltpu.VMEM((plan.branches, plan.pixels, plan.chans), bf16),
            pltpu.VMEM((plan.branches, plan.pixels, plan.width), bf16),
            pltpu.VMEM((plan.branches, plan.pixels, plan.width), f32),
            pltpu.VMEM((plan.lanes, plan.pixels, 128), f32),
            pltpu.VMEM((plan.pixels, plan.width), f32),
            pltpu.VMEM((plan.pixels, plan.width), f32),
            pltpu.VMEM((16, 128), f32),
            pltpu.VMEM((GROUP, message, plan.width), bf16),
            pltpu.SemaphoreType.DMA((40,)),
        ],
        compiler_params=pltpu.CompilerParams(vmem_limit_bytes=48 << 20),
        name="forward_and_backward",
    )(*operands)


def chip_sum_kernel(keep_ref, other_ref, *out_refs):
    _, _, chip, _ = whereabouts()
    for hop in range(CHIPS):
        out_refs[hop][...] = (keep_ref[chip ^ hop].astype(f32) + other_ref[chip ^ hop].astype(f32)).astype(bf16)


def chip_sum(keep, other):
    return pl.pallas_call(
        chip_sum_kernel,
        out_shape=[jax.ShapeDtypeStruct(keep.shape[1:], bf16)] * CHIPS,
        in_specs=[VMEM] * 2,
        out_specs=[VMEM] * CHIPS,
        compiler_params=pltpu.CompilerParams(vmem_limit_bytes=40 << 20),
        name="chip_sum",
    )(keep, other)


def plane_sum_kernel(plan, mask_ref, *refs):
    total, out_refs = refs[-1], refs[CHIPS:-1]
    plane, _, _, _ = whereabouts()
    slots, _ = slots_of(mask_ref, plan.branches)
    added = refs[0][...].astype(f32)
    for ref in refs[1:CHIPS]:
        added = added + ref[...].astype(f32)
    total[...] = added
    rows = plan.grad_rows
    for hop in range(plan.branches):
        at = pl.multiple_of(pick(slots, plane ^ hop) * rows, 32)
        out_refs[hop][0:rows] = total[pl.ds(at, rows)].astype(bf16)
        out_refs[hop][rows:rows + 16] = total[SLOTS * rows:].astype(bf16)


def plane_sum(plan, mask, parts):
    return pl.pallas_call(
        functools.partial(plane_sum_kernel, plan),
        out_shape=[jax.ShapeDtypeStruct((plan.grad_rows + 16, plan.width), bf16)] * plan.branches,
        in_specs=[SMEM] + [VMEM] * CHIPS,
        out_specs=[VMEM] * plan.branches,
        scratch_shapes=[pltpu.VMEM(parts[0].shape, f32)],
        compiler_params=pltpu.CompilerParams(vmem_limit_bytes=40 << 20),
        name="plane_sum",
    )(mask, *parts)


def place_grads_kernel(plan, mask_ref, chunks_ref, joining_ref, point_ref, depth_ref):
    plane, _, _, _ = whereabouts()
    slots, _ = slots_of(mask_ref, plan.branches)
    slot = pick(slots, plane)
    active = pick([mask_ref[branch] for branch in range(plan.branches)], plane) > 0
    rows = plan.grad_rows
    for chip in range(CHIPS):
        for core in range(2):
            chunk = jnp.where(active, chunks_ref[2 * chip + core, 0:rows].astype(f32), 0.0)
            at = core * CHIPS + chip
            joining_ref[at * plan.join_rows:(at + 1) * plan.join_rows] = chunk[:plan.join_rows]
            point_ref[0, at * plan.point_rows:(at + 1) * plan.point_rows] = chunk[plan.join_rows:]
        lanes = pl.ds(pl.multiple_of((slot % 2) * 128, 128), 128)
        part = chunks_ref[2 * chip + slot // 2, rows:rows + 16, lanes].astype(f32)
        depth_ref[0, :, chip * 128:(chip + 1) * 128] = jnp.where(active, part, 0.0)[0:9]


def place_grads(plan, mask, chunks):
    return pl.pallas_call(
        functools.partial(place_grads_kernel, plan),
        out_shape=[
            jax.ShapeDtypeStruct((plan.width, plan.width), f32),
            jax.ShapeDtypeStruct((1, plan.chans, plan.width), f32),
            jax.ShapeDtypeStruct((1, 9, plan.chans), f32),
        ],
        in_specs=[SMEM, VMEM],
        out_specs=[VMEM] * 3,
        compiler_params=pltpu.CompilerParams(vmem_limit_bytes=40 << 20),
        name="place_grads",
    )(mask, chunks)


def per_device(features, cotangent, depth_weight, point_weight, joining_weight, branch_mask):
    row_count, col_count, chan_count = features.shape
    strips = lax.axis_size("strip")
    branches = lax.axis_size("branch")
    width = joining_weight.shape[1]
    plan = Plan(row_count, col_count, chan_count, width, branches)
    scale = 1.0 / math.sqrt(row_count * col_count * strips)
    groups = None if strips == GROUP else [list(range(g, g + GROUP)) for g in range(0, strips, GROUP)]
    core = lax.axis_index("strip") % 2

    def flip_strip(value, hop):
        return lax.ppermute(value, "strip", [(s, s ^ hop) for s in range(strips)])

    def flip_branch(value, hop):
        return lax.ppermute(value, "branch", [(b, b ^ hop) for b in range(branches)])

    def all_to_all(tiles):
        if groups is None:
            return lax.all_to_all(tiles, ("strip", "branch"), 0, 0, tiled=True)
        tiles = tiles.reshape(GROUP, branches, *tiles.shape[1:])
        tiles = lax.all_to_all(tiles, "branch", 1, 1, tiled=True)
        tiles = lax.all_to_all(tiles, "strip", 0, 0, tiled=True, axis_index_groups=groups)
        return tiles.reshape(GROUP * branches, *tiles.shape[2:])

    depths = [depth_weight] + [flip_branch(depth_weight, hop) for hop in range(1, branches)]
    half = jnp.concatenate([
        lax.dynamic_slice(point_weight[0], (core * (chan_count // 2), 0), (chan_count // 2, width)),
        lax.dynamic_slice(joining_weight, (core * (width // 2), 0), (width // 2, width)),
    ])
    mine = [flip_branch(half, hop) for hop in range(1, branches)]
    others = [flip_strip(value, 1) for value in mine]

    sent = spread_features(plan, features)
    pieces = [sent[0]] + [flip_strip(sent[hop], hop) for hop in range(1, GROUP)]
    halos = []
    if groups is not None:
        strip = lax.axis_index("strip") % GROUP
        stacked = jnp.take(jnp.stack(pieces), jnp.arange(GROUP) ^ strip, axis=0)
        down = [(s, s + GROUP) for s in range(strips - GROUP)]
        up = [(s + GROUP, s) for s in range(strips - GROUP)]
        halos = [lax.ppermute(stacked[GROUP - 4:], "strip", down), lax.ppermute(stacked[:4], "strip", up)]

    cotangent_tiles = all_to_all(send_cotangent(plan, cotangent))
    output_tiles, keep, send = main_step(
        plan, scale, branch_mask, cotangent_tiles, pieces, halos, depths, point_weight, joining_weight, mine, others
    )
    parts = chip_sum(keep, flip_strip(send, 1))
    parts = [parts[0]] + [flip_strip(parts[hop], 2 * hop) for hop in range(1, CHIPS)]
    output = place_output(plan, all_to_all(output_tiles))
    shares = plane_sum(plan, branch_mask, parts)
    shares = [shares[0]] + [flip_branch(shares[hop], hop) for hop in range(1, branches)]
    share = sum(value.astype(f32) for value in shares)
    if groups is not None:
        peers = [list(range(s, strips, GROUP)) for s in range(GROUP)]
        share = lax.psum(share, "strip", axis_index_groups=peers)
    chunks = lax.all_gather(share.astype(bf16), "strip", axis=0, axis_index_groups=groups)
    joining_total, point_total, depth_total = place_grads(plan, branch_mask, chunks)
    return (output, joining_total, point_total, depth_total)


def solution(mesh):
    placed = (
        P("strip", None, None),
        P("strip", None, "branch"),
        P("branch", None, None),
        P("branch", None, None),
        P("branch", None),
        P(),
    )
    return jax.shard_map(
        per_device,
        mesh=mesh,
        in_specs=placed,
        out_specs=(
            P("strip", None, "branch"),
            P("branch", None),
            P("branch", None, None),
            P("branch", None, None),
        ),
        check_vma=False,
    )
```

time: 283 us -> 110 us (0.39)
  waiting for transfers between devices: 169 us -> 36 us
  blocking collectives: 41.1 us -> 8.85 us
  starting transfers between devices: 15.4 us -> 39.8 us
  Pallas kernels: 0 us -> 21.4 us
  matrix products: 15.1 us -> 0 us
  between operations: 14.9 us -> 0.84 us
  local copies, waits for them, and re-layouts: 17.5 us -> 4.6 us
  other arithmetic: 8.57 us -> 0.05 us
    ppermute x6 -> x23, waiting for transfers between devices: 119 us -> 36 us  [the longest x9 20 us: flip_branch(): lax.ppermute(value, 'branch', [(b, b ^ hop) for b in range(branches)])]
    psum x1 -> x0, waiting for transfers between devices: 30.7 us -> none  [per_device(): lax.psum((joining_part, point_part, depth_part), 'strip')]
    psum x1 -> x0, blocking collectives: 22.9 us -> none  [per_device(): lax.psum((joining_part, point_part, depth_part), 'strip')]
    pallas_call x0 -> x7, Pallas kernels: none -> 21.4 us  [the longest x1 17 us: main_step(): pl.pallas_call(functools.partial(main_kernel, plan, scale, halo), out_sha...]
    reduce_scatter x1 -> x0, waiting for transfers between devices: 19.8 us -> none  [per_device(): lax.psum_scatter(partial_sum.astype(jnp.bfloat16), 'branch', scatter_dime...]
    dot_general x6 -> x0, matrix products: 15.1 us -> none  [the longest x2 9.93 us: contract_cols(): lax.dot_general(left, right, (((1,), (1,)), ((), ())), preferred_element_...]
    ppermute x6 -> x23, starting transfers between devices: 15.4 us -> 29.9 us  [the longest x9 15.3 us: flip_branch(): lax.ppermute(value, 'branch', [(b, b ^ hop) for b in range(branches)])]
    all_to_all x0 -> x2, starting transfers between devices: none -> 9.9 us  [all_to_all(): return lax.all_to_all(tiles, ('strip', 'branch'), 0, 0, tiled=True)]
  transfers between devices with their start and end apart: 8 -> 25, of which waited for: 6 -> 13; matrix products, arithmetic and copies ran while one was open for 4% -> 2% of each run, Pallas kernels for 0% -> 3%
where the time goes in v1:
time: 110 us; the launch traced here: 112 us
  starting transfers between devices  39.8 us (36%)
  waiting for transfers between devices  36 us (33%)
  Pallas kernels  21.4 us (19%)
  blocking collectives  8.85 us (8%)
  local copies, waits for them, and re-layouts  4.6 us (4%)
    ppermute x9, waiting for transfers between devices, flip_branch(): lax.ppermute(value, 'branch', [(b, b ^ hop) for b in range(branches)])  20 us
    pallas_call x1, Pallas kernels, main_step(): pl.pallas_call(functools.partial(main_kernel, plan, scale, halo), out_sha...  17 us
    ppermute x14, waiting for transfers between devices, flip_strip(): return lax.ppermute(value, 'strip', [(s, s ^ hop) for s in range(strips)])  16.1 us
    ppermute x9, starting transfers between devices, flip_branch(): lax.ppermute(value, 'branch', [(b, b ^ hop) for b in range(branches)])  15.3 us
    ppermute x14, starting transfers between devices, flip_strip(): return lax.ppermute(value, 'strip', [(s, s ^ hop) for s in range(strips)])  14.6 us
    all_to_all x2, starting transfers between devices, all_to_all(): return lax.all_to_all(tiles, ('strip', 'branch'), 0, 0, tiled=True)  9.9 us
    all_gather x1, blocking collectives, per_device(): lax.all_gather(share.astype(bf16), 'strip', axis=0, axis_index_groups=gro...  8.85 us
    unnamed x13, local copies, waits for them, and re-layouts  2.72 us
  transfers between devices with their start and end apart: 25, of which 13 were waited for; matrix products, arithmetic and copies ran while one was open for 2% of the time, Pallas kernels for 3%

profile of v1, /device:TPU:0, one launch (start us, length us, event | category | flops | bytes accessed | tf_op | source)
XLA Modules:
  0.0 111.6 jit_solution(6361677293933856902)
XLA Ops:
  2.6 5.1 %collective-permute-start.12 = (bf16[384,256]{1,0:T(8,128)(2,1)S(1)}, bf16[384,256]{1,0:T(8,128)(2,1)S(1)}, u32[]{:S(2)}, u32[]{:S(2)}) collective-permute-start(bf16[384,256]{1,0:T(8,128)(2,1)S(1)} %pad_maximum_fusion), channel_id=1, source_target_pairs={{0,3},{1,2},{2,1},{3,0},{4,7},{5,6},{6,5},{7,4},{8,11},{9,10},{10,... | collective-permute-start | bytes 589832 | tf_op jit(solution)/shard_map/ppermute | solution.py:544
  10.6 6.0 %all-to-all-start = ((bf16[32,24,128]{2,1,0:T(8,128)(2,1)}), bf16[32,24,128]{2,1,0:T(8,128)(2,1)S(1)}, u32[]{:S(2)}, u32[]{:S(2)}) async-start(bf16[32,24,128]{2,1,0:T(8,128)(2,1)} %send_cotangent.1), calls=%async_computation | async-start | bytes 393216 | tf_op jit(solution)/shard_map/all_to_all | solution.py:548
  17.6 2.6 %collective-permute-start.8 = (bf16[1,9,512]{2,1,0:T(8,128)(2,1)S(1)}, bf16[1,9,512]{2,1,0:T(8,128)(2,1)S(1)}, u32[]{:S(2)}, u32[]{:S(2)}) collective-permute-start(bf16[1,9,512]{2,1,0:T(8,128)(2,1)S(1)} %copy-done.3), channel_id=1, source_target_pairs={{0,2},{1,3},{2,0},{3,1},{4,6},{5,7},{6,4},{7,5},{8,10},{9,11},{10,... | collective-permute-start | bytes 27656 | tf_op jit(solution)/shard_map/ppermute | solution.py:544
  20.2 9.1 %collective-permute-done.8.refs_10_ = bf16[1,9,512]{2,1,0:T(8,128)(2,1)S(1)} collective-permute-done((bf16[1,9,512]{2,1,0:T(8,128)(2,1)S(1)}, bf16[1,9,512]{2,1,0:T(8,128)(2,1)S(1)}, u32[]{:S(2)}, u32[]{:S(2)}) %collective-permute-start.8) | collective-permute-done | bytes 9248 | tf_op jit(solution)/shard_map/ppermute | solution.py:544
  29.3 3.7 %collective-permute-done.7.refs_9_ = bf16[1,9,512]{2,1,0:T(8,128)(2,1)S(1)} collective-permute-done((bf16[1,9,512]{2,1,0:T(8,128)(2,1)S(1)}, bf16[1,9,512]{2,1,0:T(8,128)(2,1)S(1)}, u32[]{:S(2)}, u32[]{:S(2)}) %collective-permute-start.7) | collective-permute-done | bytes 9248 | tf_op jit(solution)/shard_map/ppermute | solution.py:544
  33.1 2.5 %collective-permute-start.9 = (bf16[1,9,512]{2,1,0:T(8,128)(2,1)S(1)}, bf16[1,9,512]{2,1,0:T(8,128)(2,1)S(1)}, u32[]{:S(2)}, u32[]{:S(2)}) collective-permute-start(bf16[1,9,512]{2,1,0:T(8,128)(2,1)S(1)} %copy-done.3), channel_id=1, source_target_pairs={{0,3},{1,2},{2,1},{3,0},{4,7},{5,6},{6,5},{7,4},{8,11},{9,10},{10,... | collective-permute-start | bytes 27656 | tf_op jit(solution)/shard_map/ppermute | solution.py:544
  35.5 3.1 %collective-permute-done.9.refs_11_ = bf16[1,9,512]{2,1,0:T(8,128)(2,1)S(1)} collective-permute-done((bf16[1,9,512]{2,1,0:T(8,128)(2,1)S(1)}, bf16[1,9,512]{2,1,0:T(8,128)(2,1)S(1)}, u32[]{:S(2)}, u32[]{:S(2)}) %collective-permute-start.9) | collective-permute-done | bytes 9248 | tf_op jit(solution)/shard_map/ppermute | solution.py:544
  38.6 1.5 %collective-permute-start.1 = (bf16[80,512]{1,0:T(8,128)(2,1)S(1)}, bf16[80,512]{1,0:T(8,128)(2,1)S(1)}, u32[]{:S(2)}, u32[]{:S(2)}) collective-permute-start(bf16[80,512]{1,0:T(8,128)(2,1)S(1)} %get-tuple-element.28), channel_id=1, source_target_pairs={{0,8},{4,12},{8,0},{12,4},{16,24},{20,28},{24,16},{28,20},{1,9},{5... | collective-permute-start | bytes 245768 | tf_op jit(solution)/shard_map/ppermute | solution.py:541
  41.3 1.8 %collective-permute-done.1.refs_2_ = bf16[80,512]{1,0:T(8,128)(2,1)S(1)} collective-permute-done((bf16[80,512]{1,0:T(8,128)(2,1)S(1)}, bf16[80,512]{1,0:T(8,128)(2,1)S(1)}, u32[]{:S(2)}, u32[]{:S(2)}) %collective-permute-start.1) | collective-permute-done | bytes 81952 | tf_op jit(solution)/shard_map/ppermute | solution.py:541
  43.1 1.5 %collective-permute-start.3 = (bf16[80,512]{1,0:T(8,128)(2,1)S(1)}, bf16[80,512]{1,0:T(8,128)(2,1)S(1)}, u32[]{:S(2)}, u32[]{:S(2)}) collective-permute-start(bf16[80,512]{1,0:T(8,128)(2,1)S(1)} %get-tuple-element.30), channel_id=1, source_target_pairs={{0,16},{4,20},{8,24},{12,28},{16,0},{20,4},{24,8},{28,12},{1,17},{... | collective-permute-start | bytes 245768 | tf_op jit(solution)/shard_map/ppermute | solution.py:541
  47.5 4.1 %collective-permute-start.5 = (bf16[80,512]{1,0:T(8,128)(2,1)S(1)}, bf16[80,512]{1,0:T(8,128)(2,1)S(1)}, u32[]{:S(2)}, u32[]{:S(2)}) collective-permute-start(bf16[80,512]{1,0:T(8,128)(2,1)S(1)} %get-tuple-element.32), channel_id=1, source_target_pairs={{0,24},{4,28},{8,16},{12,20},{16,8},{20,12},{24,0},{28,4},{1,25},{... | collective-permute-start | bytes 245768 | tf_op jit(solution)/shard_map/ppermute | solution.py:541
  54.0 2.4 %collective-permute-done.6.refs_7_ = bf16[80,512]{1,0:T(8,128)(2,1)S(1)} collective-permute-done((bf16[80,512]{1,0:T(8,128)(2,1)S(1)}, bf16[80,512]{1,0:T(8,128)(2,1)S(1)}, u32[]{:S(2)}, u32[]{:S(2)}) %collective-permute-start.6) | collective-permute-done | bytes 81952 | tf_op jit(solution)/shard_map/ppermute | solution.py:541
  56.4 17.0 %forward_and_backward.1 = (bf16[32,24,128]{2,1,0:T(8,128)(2,1)}, bf16[4,304,256]{2,1,0:T(8,128)(2,1)S(1)}, bf16[4,304,256]{2,1,0:T(8,128)(2,1)}) custom-call(s32[4]{0:T(128)S(1)} %copy-done.4, bf16[32,24,128]{2,1,0:T(8,128)(2,1)S(1)} %all-to-all-done.cotangent_ref, bf16[80,512]{1,0:T(8,128)(2,1)S(1)} %get-tuple-element.26.refs_0_, ...), custom_call_target="tpu_custom_call" | custom-call | tf_op jit(solution)/shard_map/forward_and_backward/pallas_call | solution.py:423
  73.5 3.9 %all-to-all-start.1 = ((bf16[32,24,128]{2,1,0:T(8,128)(2,1)}), bf16[32,24,128]{2,1,0:T(8,128)(2,1)S(1)}, u32[]{:S(2)}, u32[]{:S(2)}) async-start(bf16[32,24,128]{2,1,0:T(8,128)(2,1)} %get-tuple-element.34), calls=%async_computation.1 | async-start | bytes 393216 | tf_op jit(solution)/shard_map/all_to_all | solution.py:548
  77.6 1.8 %collective-permute-start.17 = (bf16[304,256]{1,0:T(8,128)(2,1)S(1)}, bf16[304,256]{1,0:T(8,128)(2,1)S(1)}, u32[]{:S(2)}, u32[]{:S(2)}) collective-permute-start(bf16[304,256]{1,0:T(8,128)(2,1)S(1)} %get-tuple-element.38), channel_id=1, source_target_pairs={{0,8},{4,12},{8,0},{12,4},{16,24},{20,28},{24,16},{28,20},{1,9},{5... | collective-permute-start | bytes 466952 | tf_op jit(solution)/shard_map/ppermute | solution.py:541
  81.2 4.9 %collective-permute-done.17.refs_1_ = bf16[304,256]{1,0:T(8,128)(2,1)S(1)} collective-permute-done((bf16[304,256]{1,0:T(8,128)(2,1)S(1)}, bf16[304,256]{1,0:T(8,128)(2,1)S(1)}, u32[]{:S(2)}, u32[]{:S(2)}) %collective-permute-start.17) | collective-permute-done | bytes 155680 | tf_op jit(solution)/shard_map/ppermute | solution.py:541
  86.1 2.6 %collective-permute-done.18.refs_2_ = bf16[304,256]{1,0:T(8,128)(2,1)S(1)} collective-permute-done((bf16[304,256]{1,0:T(8,128)(2,1)S(1)}, bf16[304,256]{1,0:T(8,128)(2,1)S(1)}, u32[]{:S(2)}, u32[]{:S(2)}) %collective-permute-start.18) | collective-permute-done | bytes 155680 | tf_op jit(solution)/shard_map/ppermute | solution.py:541
  88.6 1.5 %collective-permute-done.19.refs_3_ = bf16[304,256]{1,0:T(8,128)(2,1)S(1)} collective-permute-done((bf16[304,256]{1,0:T(8,128)(2,1)S(1)}, bf16[304,256]{1,0:T(8,128)(2,1)S(1)}, u32[]{:S(2)}, u32[]{:S(2)}) %collective-permute-start.19) | collective-permute-done | bytes 155680 | tf_op jit(solution)/shard_map/ppermute | solution.py:541
  90.8 1.5 %collective-permute-start.20 = (bf16[112,256]{1,0:T(8,128)(2,1)S(1)}, bf16[112,256]{1,0:T(8,128)(2,1)S(1)}, u32[]{:S(2)}, u32[]{:S(2)}) collective-permute-start(bf16[112,256]{1,0:T(8,128)(2,1)S(1)} %get-tuple-element.42), channel_id=1, source_target_pairs={{0,1},{1,0},{2,3},{3,2},{4,5},{5,4},{6,7},{7,6},{8,9},{9,8},{10,11... | collective-permute-start | bytes 172040 | tf_op jit(solution)/shard_map/ppermute | solution.py:544
  92.3 2.3 %collective-permute-start.21 = (bf16[112,256]{1,0:T(8,128)(2,1)S(1)}, bf16[112,256]{1,0:T(8,128)(2,1)S(1)}, u32[]{:S(2)}, u32[]{:S(2)}) collective-permute-start(bf16[112,256]{1,0:T(8,128)(2,1)S(1)} %get-tuple-element.43), channel_id=1, source_target_pairs={{0,2},{1,3},{2,0},{3,1},{4,6},{5,7},{6,4},{7,5},{8,10},{9,11},{10,... | collective-permute-start | bytes 172040 | tf_op jit(solution)/shard_map/ppermute | solution.py:544
  96.6 1.8 %collective-permute-done.21 = bf16[112,256]{1,0:T(8,128)(2,1)S(1)} collective-permute-done((bf16[112,256]{1,0:T(8,128)(2,1)S(1)}, bf16[112,256]{1,0:T(8,128)(2,1)S(1)}, u32[]{:S(2)}, u32[]{:S(2)}) %collective-permute-start.21) | collective-permute-done | bytes 57376 | tf_op jit(solution)/shard_map/ppermute | solution.py:544
  98.4 2.2 %collective-permute-done.22 = bf16[112,256]{1,0:T(8,128)(2,1)S(1)} collective-permute-done((bf16[112,256]{1,0:T(8,128)(2,1)S(1)}, bf16[112,256]{1,0:T(8,128)(2,1)S(1)}, u32[]{:S(2)}, u32[]{:S(2)}) %collective-permute-start.22) | collective-permute-done | bytes 57376 | tf_op jit(solution)/shard_map/ppermute | solution.py:544
  100.6 8.8 %all-gather = bf16[896,256]{1,0:T(8,128)(2,1)S(1)} all-gather(bf16[112,256]{1,0:T(8,128)(2,1)S(1)} %add_convert_fusion), channel_id=2, replica_groups=mesh['strip'=8,'branch'=4] {'strip'}, dimensions={0}, use_global_device_ids=true | all-gather | bytes 516096 | tf_op jit(solution)/shard_map/all_gather | solution.py:585
  109.5 1.5 %place_grads.1 = (f32[256,256]{1,0:T(8,128)}, f32[1,512,256]{2,1,0:T(8,128)}, f32[1,9,512]{2,1,0:T(8,128)S(1)}) custom-call(s32[4]{0:T(128)S(1)} %copy-done.4, bf16[8,112,256]{2,1,0:T(8,128)(2,1)S(1)} %bitcast.3), custom_call_target="tpu_custom_call" | custom-call | tf_op jit(solution)/shard_map/place_grads/pallas_call | solution.py:516
  (51 shorter events, 17.5 us)
Async XLA Ops:
  2.6 37.5 %collective-permute-start.12 = (bf16[384,256]{1,0:T(8,128)(2,1)S(1)}, bf16[384,256]{1,0:T(8,128)(2,1)S(1)}, u32[]{:S(2)}, u32[]{:S(2)}) collective-permute-start(bf16[384,256]{1,0:T(8,128)(2,1)S(1)} %pad_maximum_fusion), channel_id=1, source_target_pairs={{0,3},{1,2},{2,1},{3,0},{4,7},{5,6},{6,5},{7,4},{8,11},{9,10},{10,... | collective-permute-start | bytes 589832 | tf_op jit(solution)/shard_map/ppermute | solution.py:544
  7.7 33.0 %collective-permute-start.11 = (bf16[384,256]{1,0:T(8,128)(2,1)S(1)}, bf16[384,256]{1,0:T(8,128)(2,1)S(1)}, u32[]{:S(2)}, u32[]{:S(2)}) collective-permute-start(bf16[384,256]{1,0:T(8,128)(2,1)S(1)} %pad_maximum_fusion), channel_id=1, source_target_pairs={{0,2},{1,3},{2,0},{3,1},{4,6},{5,7},{6,4},{7,5},{8,10},{9,11},{10,... | collective-permute-start | bytes 589832 | tf_op jit(solution)/shard_map/ppermute | solution.py:544
  7.7 33.1 %collective-permute-start.10 = (bf16[384,256]{1,0:T(8,128)(2,1)S(1)}, bf16[384,256]{1,0:T(8,128)(2,1)S(1)}, u32[]{:S(2)}, u32[]{:S(2)}) collective-permute-start(bf16[384,256]{1,0:T(8,128)(2,1)S(1)} %pad_maximum_fusion), channel_id=1, source_target_pairs={{0,1},{1,0},{2,3},{3,2},{4,5},{5,4},{6,7},{7,6},{8,9},{9,8},{10,11... | collective-permute-start | bytes 589832 | tf_op jit(solution)/shard_map/ppermute | solution.py:544
  10.6 45.8 %all-to-all-start = ((bf16[32,24,128]{2,1,0:T(8,128)(2,1)}), bf16[32,24,128]{2,1,0:T(8,128)(2,1)S(1)}, u32[]{:S(2)}, u32[]{:S(2)}) async-start(bf16[32,24,128]{2,1,0:T(8,128)(2,1)} %send_cotangent.1), calls=%async_computation | async-start | bytes 393216 | tf_op jit(solution)/shard_map/all_to_all | solution.py:548
  17.3 22.8 %collective-permute-start = (bf16[80,512]{1,0:T(8,128)(2,1)S(1)}, bf16[80,512]{1,0:T(8,128)(2,1)S(1)}, u32[]{:S(2)}, u32[]{:S(2)}) collective-permute-start(bf16[80,512]{1,0:T(8,128)(2,1)S(1)} %get-tuple-element.27), channel_id=1, source_target_pairs={{0,4},{4,0},{8,12},{12,8},{16,20},{20,16},{24,28},{28,24},{1,5},{5... | collective-permute-start | bytes 245768 | tf_op jit(solution)/shard_map/ppermute | solution.py:541
  17.6 11.7 %collective-permute-start.8 = (bf16[1,9,512]{2,1,0:T(8,128)(2,1)S(1)}, bf16[1,9,512]{2,1,0:T(8,128)(2,1)S(1)}, u32[]{:S(2)}, u32[]{:S(2)}) collective-permute-start(bf16[1,9,512]{2,1,0:T(8,128)(2,1)S(1)} %copy-done.3), channel_id=1, source_target_pairs={{0,2},{1,3},{2,0},{3,1},{4,6},{5,7},{6,4},{7,5},{8,10},{9,11},{10,... | collective-permute-start | bytes 27656 | tf_op jit(solution)/shard_map/ppermute | solution.py:544
  33.1 5.5 %collective-permute-start.9 = (bf16[1,9,512]{2,1,0:T(8,128)(2,1)S(1)}, bf16[1,9,512]{2,1,0:T(8,128)(2,1)S(1)}, u32[]{:S(2)}, u32[]{:S(2)}) collective-permute-start(bf16[1,9,512]{2,1,0:T(8,128)(2,1)S(1)} %copy-done.3), channel_id=1, source_target_pairs={{0,3},{1,2},{2,1},{3,0},{4,7},{5,6},{6,5},{7,4},{8,11},{9,10},{10,... | collective-permute-start | bytes 27656 | tf_op jit(solution)/shard_map/ppermute | solution.py:544
  38.6 4.4 %collective-permute-start.1 = (bf16[80,512]{1,0:T(8,128)(2,1)S(1)}, bf16[80,512]{1,0:T(8,128)(2,1)S(1)}, u32[]{:S(2)}, u32[]{:S(2)}) collective-permute-start(bf16[80,512]{1,0:T(8,128)(2,1)S(1)} %get-tuple-element.28), channel_id=1, source_target_pairs={{0,8},{4,12},{8,0},{12,4},{16,24},{20,28},{24,16},{28,20},{1,9},{5... | collective-permute-start | bytes 245768 | tf_op jit(solution)/shard_map/ppermute | solution.py:541
  40.1 4.7 %collective-permute-start.2 = (bf16[80,512]{1,0:T(8,128)(2,1)S(1)}, bf16[80,512]{1,0:T(8,128)(2,1)S(1)}, u32[]{:S(2)}, u32[]{:S(2)}) collective-permute-start(bf16[80,512]{1,0:T(8,128)(2,1)S(1)} %get-tuple-element.29), channel_id=1, source_target_pairs={{0,12},{4,8},{8,4},{12,0},{16,28},{20,24},{24,20},{28,16},{1,13},{... | collective-permute-start | bytes 245768 | tf_op jit(solution)/shard_map/ppermute | solution.py:541
  40.1 16.3 %collective-permute-start.15 = (bf16[384,256]{1,0:T(8,128)(2,1)S(1)}, bf16[384,256]{1,0:T(8,128)(2,1)S(1)}, u32[]{:S(2)}, u32[]{:S(2)}) collective-permute-start(bf16[384,256]{1,0:T(8,128)(2,1)S(1)} %collective-permute-done.12.refs_16_), channel_id=1, source_target_pairs={{0,4},{4,0},{8,12},{12,8},{16,20},{20,16},{24,28},{28,24},{1,5},{5... | collective-permute-start | bytes 589832 | tf_op jit(solution)/shard_map/ppermute | solution.py:541
  40.8 15.6 %collective-permute-start.14 = (bf16[384,256]{1,0:T(8,128)(2,1)S(1)}, bf16[384,256]{1,0:T(8,128)(2,1)S(1)}, u32[]{:S(2)}, u32[]{:S(2)}) collective-permute-start(bf16[384,256]{1,0:T(8,128)(2,1)S(1)} %collective-permute-done.11.refs_15_), channel_id=1, source_target_pairs={{0,4},{4,0},{8,12},{12,8},{16,20},{20,16},{24,28},{28,24},{1,5},{5... | collective-permute-start | bytes 589832 | tf_op jit(solution)/shard_map/ppermute | solution.py:541
  40.8 15.5 %collective-permute-start.13 = (bf16[384,256]{1,0:T(8,128)(2,1)S(1)}, bf16[384,256]{1,0:T(8,128)(2,1)S(1)}, u32[]{:S(2)}, u32[]{:S(2)}) collective-permute-start(bf16[384,256]{1,0:T(8,128)(2,1)S(1)} %collective-permute-done.10.refs_14_), channel_id=1, source_target_pairs={{0,4},{4,0},{8,12},{12,8},{16,20},{20,16},{24,28},{28,24},{1,5},{5... | collective-permute-start | bytes 589832 | tf_op jit(solution)/shard_map/ppermute | solution.py:541
  43.1 4.4 %collective-permute-start.3 = (bf16[80,512]{1,0:T(8,128)(2,1)S(1)}, bf16[80,512]{1,0:T(8,128)(2,1)S(1)}, u32[]{:S(2)}, u32[]{:S(2)}) collective-permute-start(bf16[80,512]{1,0:T(8,128)(2,1)S(1)} %get-tuple-element.30), channel_id=1, source_target_pairs={{0,16},{4,20},{8,24},{12,28},{16,0},{20,4},{24,8},{28,12},{1,17},{... | collective-permute-start | bytes 245768 | tf_op jit(solution)/shard_map/ppermute | solution.py:541
  44.8 6.8 %collective-permute-start.4 = (bf16[80,512]{1,0:T(8,128)(2,1)S(1)}, bf16[80,512]{1,0:T(8,128)(2,1)S(1)}, u32[]{:S(2)}, u32[]{:S(2)}) collective-permute-start(bf16[80,512]{1,0:T(8,128)(2,1)S(1)} %get-tuple-element.31), channel_id=1, source_target_pairs={{0,20},{4,16},{8,28},{12,24},{16,4},{20,0},{24,12},{28,8},{1,21},{... | collective-permute-start | bytes 245768 | tf_op jit(solution)/shard_map/ppermute | solution.py:541
  47.5 6.5 %collective-permute-start.5 = (bf16[80,512]{1,0:T(8,128)(2,1)S(1)}, bf16[80,512]{1,0:T(8,128)(2,1)S(1)}, u32[]{:S(2)}, u32[]{:S(2)}) collective-permute-start(bf16[80,512]{1,0:T(8,128)(2,1)S(1)} %get-tuple-element.32), channel_id=1, source_target_pairs={{0,24},{4,28},{8,16},{12,20},{16,8},{20,12},{24,0},{28,4},{1,25},{... | collective-permute-start | bytes 245768 | tf_op jit(solution)/shard_map/ppermute | solution.py:541
  51.6 4.8 %collective-permute-start.6 = (bf16[80,512]{1,0:T(8,128)(2,1)S(1)}, bf16[80,512]{1,0:T(8,128)(2,1)S(1)}, u32[]{:S(2)}, u32[]{:S(2)}) collective-permute-start(bf16[80,512]{1,0:T(8,128)(2,1)S(1)} %get-tuple-element.33), channel_id=1, source_target_pairs={{0,28},{4,24},{8,20},{12,16},{16,12},{20,8},{24,4},{28,0},{1,29},{... | collective-permute-start | bytes 245768 | tf_op jit(solution)/shard_map/ppermute | solution.py:541
  73.4 4.0 %collective-permute-start.16 = (bf16[4,304,256]{2,1,0:T(8,128)(2,1)}, bf16[4,304,256]{2,1,0:T(8,128)(2,1)S(1)}, u32[]{:S(2)}, u32[]{:S(2)}) collective-permute-start(bf16[4,304,256]{2,1,0:T(8,128)(2,1)} %get-tuple-element.36), channel_id=1, source_target_pairs={{0,4},{4,0},{8,12},{12,8},{16,20},{20,16},{24,28},{28,24},{1,5},{5... | collective-permute-start | bytes 1867784 | tf_op jit(solution)/shard_map/ppermute | solution.py:541
  73.5 21.8 %all-to-all-start.1 = ((bf16[32,24,128]{2,1,0:T(8,128)(2,1)}), bf16[32,24,128]{2,1,0:T(8,128)(2,1)S(1)}, u32[]{:S(2)}, u32[]{:S(2)}) async-start(bf16[32,24,128]{2,1,0:T(8,128)(2,1)} %get-tuple-element.34), calls=%async_computation.1 | async-start | bytes 393216 | tf_op jit(solution)/shard_map/all_to_all | solution.py:548
  77.6 8.5 %collective-permute-start.17 = (bf16[304,256]{1,0:T(8,128)(2,1)S(1)}, bf16[304,256]{1,0:T(8,128)(2,1)S(1)}, u32[]{:S(2)}, u32[]{:S(2)}) collective-permute-start(bf16[304,256]{1,0:T(8,128)(2,1)S(1)} %get-tuple-element.38), channel_id=1, source_target_pairs={{0,8},{4,12},{8,0},{12,4},{16,24},{20,28},{24,16},{28,20},{1,9},{5... | collective-permute-start | bytes 466952 | tf_op jit(solution)/shard_map/ppermute | solution.py:541
  79.4 9.2 %collective-permute-start.18 = (bf16[304,256]{1,0:T(8,128)(2,1)S(1)}, bf16[304,256]{1,0:T(8,128)(2,1)S(1)}, u32[]{:S(2)}, u32[]{:S(2)}) collective-permute-start(bf16[304,256]{1,0:T(8,128)(2,1)S(1)} %get-tuple-element.39), channel_id=1, source_target_pairs={{0,16},{4,20},{8,24},{12,28},{16,0},{20,4},{24,8},{28,12},{1,17},{... | collective-permute-start | bytes 466952 | tf_op jit(solution)/shard_map/ppermute | solution.py:541
  80.9 9.2 %collective-permute-start.19 = (bf16[304,256]{1,0:T(8,128)(2,1)S(1)}, bf16[304,256]{1,0:T(8,128)(2,1)S(1)}, u32[]{:S(2)}, u32[]{:S(2)}) collective-permute-start(bf16[304,256]{1,0:T(8,128)(2,1)S(1)} %get-tuple-element.40), channel_id=1, source_target_pairs={{0,24},{4,28},{8,16},{12,20},{16,8},{20,12},{24,0},{28,4},{1,25},{... | collective-permute-start | bytes 466952 | tf_op jit(solution)/shard_map/ppermute | solution.py:541
  90.8 5.8 %collective-permute-start.20 = (bf16[112,256]{1,0:T(8,128)(2,1)S(1)}, bf16[112,256]{1,0:T(8,128)(2,1)S(1)}, u32[]{:S(2)}, u32[]{:S(2)}) collective-permute-start(bf16[112,256]{1,0:T(8,128)(2,1)S(1)} %get-tuple-element.42), channel_id=1, source_target_pairs={{0,1},{1,0},{2,3},{3,2},{4,5},{5,4},{6,7},{7,6},{8,9},{9,8},{10,11... | collective-permute-start | bytes 172040 | tf_op jit(solution)/shard_map/ppermute | solution.py:544
  92.3 6.0 %collective-permute-start.21 = (bf16[112,256]{1,0:T(8,128)(2,1)S(1)}, bf16[112,256]{1,0:T(8,128)(2,1)S(1)}, u32[]{:S(2)}, u32[]{:S(2)}) collective-permute-start(bf16[112,256]{1,0:T(8,128)(2,1)S(1)} %get-tuple-element.43), channel_id=1, source_target_pairs={{0,2},{1,3},{2,0},{3,1},{4,6},{5,7},{6,4},{7,5},{8,10},{9,11},{10,... | collective-permute-start | bytes 172040 | tf_op jit(solution)/shard_map/ppermute | solution.py:544
  94.6 6.0 %collective-permute-start.22 = (bf16[112,256]{1,0:T(8,128)(2,1)S(1)}, bf16[112,256]{1,0:T(8,128)(2,1)S(1)}, u32[]{:S(2)}, u32[]{:S(2)}) collective-permute-start(bf16[112,256]{1,0:T(8,128)(2,1)S(1)} %get-tuple-element.44), channel_id=1, source_target_pairs={{0,3},{1,2},{2,1},{3,0},{4,7},{5,6},{6,5},{7,4},{8,11},{9,10},{10,... | collective-permute-start | bytes 172040 | tf_op jit(solution)/shard_map/ppermute | solution.py:544
  (6 other events, 196.2 us)

commit v2 on v1

v2 whole, which is shorter than its diff:
```python
import functools
import math

import jax
import jax.numpy as jnp
from jax import lax
from jax.experimental import pallas as pl
from jax.experimental.pallas import tpu as pltpu
from jax.sharding import PartitionSpec as P

DILATION_STEP = 6
GROUP = 8
CHIPS = 4
SLOTS = 3

tanh_coef = 0.7978845608
cubic_coef = 0.044715
slope_coef = 0.134145

f32, bf16, i32 = jnp.float32, jnp.bfloat16, jnp.int32
VMEM = pl.BlockSpec(memory_space=pltpu.VMEM)
SMEM = pl.BlockSpec(memory_space=pltpu.SMEM)
ANY = pl.BlockSpec(memory_space=pl.ANY)
HBM = pl.BlockSpec(memory_space=pltpu.HBM)


def gelu_both(values):
    square = values * values
    inner = jnp.tanh(tanh_coef * (values + cubic_coef * values * square))
    half = 0.5 * (1.0 + inner)
    slope = half + 0.5 * values * (1.0 - inner * inner) * tanh_coef * (1.0 + slope_coef * square)
    return values * half, slope


def dot(left, right, dims=((1,), (0,))):
    return lax.dot_general(left, right, (dims, ((), ())), preferred_element_type=f32)


def iota(shape, dim):
    return lax.broadcasted_iota(i32, shape, dim)


def one_hot(mask):
    return jnp.where(mask, 1.0, 0.0).astype(bf16)


class Plan:
    def __init__(self, row_count, col_count, chan_count, width, branches):
        self.rows, self.cols, self.chans, self.width, self.branches = row_count, col_count, chan_count, width, branches
        self.classes = DILATION_STEP
        self.run = col_count // DILATION_STEP
        self.work = col_count // (branches * CHIPS)
        self.taps_t = row_count // 2
        self.sub_rows = GROUP * self.taps_t
        self.pixels = self.sub_rows * self.work
        self.lanes = chan_count // 128
        self.window = max(self.segments(m)[5] for m in range(branches * CHIPS))
        self.piece = self.window * self.taps_t
        self.part = width // branches
        self.step_rows = DILATION_STEP // 2
        self.pad = -(-self.step_rows * branches // 16) * 16
        self.tall = self.pad + self.sub_rows + self.pad
        self.grad_rows = (width + chan_count) // GROUP
        self.join_rows = width // GROUP
        self.point_rows = chan_count // GROUP
        self.tile = 2 * self.work
        self.depth_rows = -(-9 * self.lanes // GROUP // 8) * 8
        self.wide = -(-self.cols // 128) * 128

    def segments(self, m):
        smaller, larger = (min, max) if isinstance(m, int) else (jnp.minimum, jnp.maximum)
        first = m * self.work
        klass = first // self.run
        start = first - klass * self.run
        length = smaller(self.work, self.run - start)
        low = larger(0, start - self.branches)
        size = smaller(self.run, start + length + self.branches) - low
        rest = self.work - length
        if isinstance(m, int):
            total = size + (min(self.run, rest + self.branches) if rest else 0)
        else:
            total = size + jnp.where(rest > 0, jnp.minimum(self.run, rest + self.branches), 0)
        return klass, start, length, low, size, total

    def column(self, m, w):
        klass, start, length, _, _, _ = self.segments(m)
        return jnp.where(w < length, self.classes * (start + w) + klass, self.classes * (w - length) + klass + 1)

    def window_column(self, m, j):
        klass, _, _, low, size, total = self.segments(m)
        inside = jnp.where(j < size, self.classes * (low + j) + klass, self.classes * (j - size) + klass + 1)
        return jnp.where(j < total, inside, -(1 << 20))

    def neighbour(self, segments, w, shift):
        _, start, length, low, size, _ = segments
        first = w < length
        place = jnp.where(first, start + w, w - length) + shift
        found = jnp.where(first, place - low, size + place)
        return jnp.where(jnp.logical_and(place >= 0, place < self.run), found, self.window)


def whereabouts():
    strip = lax.axis_index("strip") % GROUP
    return lax.axis_index("branch"), strip, strip // 2, strip % 2


def slots_of(mask_ref, branches):
    slots, count = [], 0
    for branch in range(branches):
        slots.append(jnp.minimum(count, SLOTS - 1) + 0 * mask_ref[branch])
        count = count + mask_ref[branch]
    return slots, count


def pick(values, index):
    result = values[0]
    for place in range(1, len(values)):
        result = jnp.where(index == place, values[place], result)
    return result


def tile_selector(plan):
    blocks = []
    for chip in range(CHIPS):
        for plane in range(plan.branches):
            row = iota((plan.tile, 128), 0)
            column = plan.column(plane * CHIPS + chip, row // 2)
            blocks.append(column + (row % 2) * plan.wide)
    target = jnp.concatenate(blocks, 0)
    lane = iota(target.shape, 1)
    return jnp.concatenate([one_hot(target == lane + 128 * k) for k in range(2 * plan.wide // 128)], 1)


def halve_kernel(plan, point_ref, joining_ref, half_ref, sems):
    _, _, _, core = whereabouts()
    half_point, half_join = plan.chans // 2, plan.width // 2
    copies = [
        pltpu.make_async_copy(
            point_ref.at[0, pl.ds(pl.multiple_of(core * half_point, half_point), half_point)],
            half_ref.at[pl.ds(0, half_point)],
            sems.at[0],
        ),
        pltpu.make_async_copy(
            joining_ref.at[pl.ds(pl.multiple_of(core * half_join, half_join), half_join)],
            half_ref.at[pl.ds(half_point, half_join)],
            sems.at[1],
        ),
    ]
    for copy in copies:
        copy.start()
    for copy in copies:
        copy.wait()


def halve_weights(plan, point, joining):
    return pl.pallas_call(
        functools.partial(halve_kernel, plan),
        out_shape=jax.ShapeDtypeStruct(((plan.chans + plan.width) // 2, plan.width), bf16),
        in_specs=[HBM] * 2,
        out_specs=VMEM,
        scratch_shapes=[pltpu.SemaphoreType.DMA((2,))],
        compiler_params=pltpu.CompilerParams(vmem_limit_bytes=8 << 20),
        name="halve_weights",
    )(point, joining)


def spread_kernel(plan, features_ref, keep_ref, send_ref):
    plane, _, _, core = whereabouts()
    depth = plan.taps_t * plan.cols
    targets = []
    for chip in range(CHIPS):
        row = iota((plan.piece, 128), 0)
        column = plan.window_column(plane * CHIPS + chip, row // plan.taps_t)
        targets.append(column + (row % plan.taps_t) * plan.cols)
    target = jnp.concatenate(targets, 0)
    lane = iota(target.shape, 1)
    chosen = jnp.concatenate([one_hot(target == lane + 128 * k) for k in range(depth // 128)], 1)
    for flip, out_ref in enumerate((keep_ref, send_ref)):
        rows = jnp.concatenate([features_ref[2 * t + (core ^ flip)] for t in range(plan.taps_t)], 0)
        found = dot(chosen, rows).astype(bf16)
        for chip in range(CHIPS):
            out_ref[chip] = found[chip * plan.piece:(chip + 1) * plan.piece]


def spread_features(plan, features):
    half = jax.ShapeDtypeStruct((CHIPS, plan.piece, plan.chans), bf16)
    return pl.pallas_call(
        functools.partial(spread_kernel, plan),
        out_shape=[half, half],
        in_specs=[VMEM],
        out_specs=[VMEM] * 2,
        compiler_params=pltpu.CompilerParams(vmem_limit_bytes=16 << 20),
        name="spread_features",
    )(features)


def join_kernel(plan, keep_ref, other_ref, *out_refs):
    _, _, chip, _ = whereabouts()
    for hop in range(CHIPS):
        out_refs[hop][0:plan.piece] = keep_ref[chip ^ hop]
        out_refs[hop][plan.piece:] = other_ref[chip ^ hop]


def join_features(plan, keep, other):
    return pl.pallas_call(
        functools.partial(join_kernel, plan),
        out_shape=[jax.ShapeDtypeStruct((2 * plan.piece, plan.chans), bf16)] * CHIPS,
        in_specs=[VMEM] * 2,
        out_specs=[VMEM] * CHIPS,
        compiler_params=pltpu.CompilerParams(vmem_limit_bytes=8 << 20),
        name="join_features",
    )(keep, other)


def send_cotangent_kernel(plan, cotangent_ref, depth_ref, tiles_ref, cotangent, depth, taps, sems):
    _, strip, _, _ = whereabouts()
    copies = [
        pltpu.make_async_copy(cotangent_ref, cotangent, sems.at[0]),
        pltpu.make_async_copy(depth_ref, depth, sems.at[1]),
    ]
    for copy in copies:
        copy.start()
    chosen = tile_selector(plan)
    for copy in copies:
        copy.wait()

    taps[...] = jnp.zeros_like(taps)
    values = depth[0].astype(f32)
    for tap in range(9):
        for group in range(plan.lanes):
            row = tap * plan.lanes + group
            taps[row:row + 1] = values[tap:tap + 1, group * 128:(group + 1) * 128]
    share = taps[pl.ds(pl.multiple_of(strip * plan.depth_rows, 8), plan.depth_rows)]
    fill = jnp.zeros((plan.part, plan.wide - plan.cols), f32)
    blocks = []
    for parity in range(2):
        for high in range(2):
            rows = []
            for low in range(2):
                rows += [cotangent[2 * (2 * high + low) + parity].astype(f32), fill]
            blocks.append(jnp.concatenate(rows, 1))
    found = dot(chosen, jnp.concatenate(blocks, 0).astype(bf16), ((1,), (1,)))
    for chip in range(CHIPS):
        for parity in range(2):
            for plane in range(plan.branches):
                at = (chip * plan.branches + plane) * plan.tile
                tile = found[at:at + plan.tile, parity * 128:(parity + 1) * 128]
                tiles_ref[(2 * chip + parity) * plan.branches + plane] = jnp.concatenate([tile, share], 0).astype(bf16)


def send_cotangent(plan, cotangent, depth):
    return pl.pallas_call(
        functools.partial(send_cotangent_kernel, plan),
        out_shape=jax.ShapeDtypeStruct((GROUP * plan.branches, plan.tile + plan.depth_rows, 128), bf16),
        in_specs=[HBM] * 2,
        out_specs=VMEM,
        scratch_shapes=[
            pltpu.VMEM(cotangent.shape, bf16),
            pltpu.VMEM(depth.shape, bf16),
            pltpu.VMEM((GROUP * plan.depth_rows, 128), f32),
            pltpu.SemaphoreType.DMA((2,)),
        ],
        compiler_params=pltpu.CompilerParams(vmem_limit_bytes=16 << 20),
        cost_estimate=pl.CostEstimate(flops=1, bytes_accessed=1, transcendentals=0),
        name="send_cotangent",
    )(cotangent, depth)


def place_output_kernel(plan, tiles_ref, out_ref):
    chosen = tile_selector(plan)
    halves = []
    for parity in range(2):
        blocks = []
        for chip in range(CHIPS):
            for plane in range(plan.branches):
                blocks.append(tiles_ref[(2 * chip + parity) * plan.branches + plane].astype(f32))
        halves.append(jnp.concatenate(blocks, 0))
    found = dot(jnp.concatenate(halves, 1).astype(bf16), chosen, ((0,), (0,))).astype(bf16)
    for parity in range(2):
        for high in range(2):
            for low in range(2):
                at = parity * 128 + high * plan.part
                out_ref[2 * (2 * high + low) + parity] = found[
                    at:at + plan.part, low * plan.wide:low * plan.wide + plan.cols
                ]


def place_output(plan, tiles):
    return pl.pallas_call(
        functools.partial(place_output_kernel, plan),
        out_shape=jax.ShapeDtypeStruct((plan.rows, plan.part, plan.cols), bf16),
        in_specs=[VMEM],
        out_specs=VMEM,
        compiler_params=pltpu.CompilerParams(vmem_limit_bytes=16 << 20),
        name="place_output",
    )(tiles)


def swap_halves(left, right):
    low = iota(left.shape, 1) < 64
    return (
        jnp.where(low, left, pltpu.roll(right, 64, 1)),
        jnp.where(low, pltpu.roll(left, 64, 1), right),
    )


def main_kernel(plan, scale, halo, mask_ref, cotangent_ref, *refs):
    branches, width, chans = plan.branches, plan.width, plan.chans
    piece_refs, refs = refs[:CHIPS], refs[CHIPS:]
    halo_refs, refs = (refs[:2], refs[2:]) if halo else ((), refs)
    (point_ref, joining_ref), refs = refs[:2], refs[2:]
    mine_refs, refs = refs[:branches - 1], refs[branches - 1:]
    other_refs, refs = refs[:branches - 1], refs[branches - 1:]
    output_ref, keep_ref, send_ref, grad_pre_ref, point, spread = refs[:6]
    pieces, halo_pieces, dw_out, joining, branch_out, slope, joined, sorted_rows, grads, sems = refs[6:]
    plane, strip, chip, core = whereabouts()
    slots, _ = slots_of(mask_ref, branches)

    copies = []

    def fetch(source, target):
        copy = pltpu.make_async_copy(source, target, sems.at[len(copies)])
        copy.start()
        copies.append(copy)

    for hop in range(CHIPS):
        for flip in range(2):
            fetch(
                piece_refs[hop].at[pl.ds(flip * plan.piece, plan.piece)], pieces.at[2 * (chip ^ hop) + (core ^ flip)]
            )
    for place, ref in enumerate(halo_refs):
        fetch(ref, halo_pieces.at[place])
    early = len(copies)
    fetch(point_ref.at[0], point.at[plane])
    fetch(joining_ref, joining.at[plane])
    half_point, half_join = chans // 2, width // 2
    for hop in range(1, branches):
        for side, ref in ((core, mine_refs[hop - 1]), (1 - core, other_refs[hop - 1])):
            at_point = pl.multiple_of(side * half_point, half_point)
            at_join = pl.multiple_of(side * half_join, half_join)
            fetch(ref.at[pl.ds(0, half_point)], point.at[plane ^ hop, pl.ds(at_point, half_point)])
            fetch(ref.at[pl.ds(half_point, half_join)], joining.at[plane ^ hop, pl.ds(at_join, half_join)])

    for group in range(plan.lanes):
        edge = jnp.zeros((plan.window, plan.pad, 128), f32)
        spread[group, 0:plan.window, 0:plan.pad] = edge
        spread[group, 0:plan.window, plan.pad + plan.sub_rows:plan.tall] = edge
        spread[group, plan.window] = jnp.zeros((plan.tall, 128), f32)

    low_rows = iota((8, 128), 0) < 4

    def lay(source, place, row):
        @pl.loop(0, plan.piece // 16)
        def _(quad):
            at = pl.multiple_of(quad * 16, 16)
            for group in range(plan.lanes):
                lanes = pl.ds(group * 128, 128)
                upper = source[place, pl.ds(at, 16), lanes].astype(f32)
                lower = source[place + 1, pl.ds(at, 16), lanes].astype(f32)
                for part in range(2):
                    a, b = upper[8 * part:8 * part + 8], lower[8 * part:8 * part + 8]
                    column = quad * 4 + 2 * part
                    spread[group, column, row:row + 8] = jnp.where(low_rows, a, pltpu.roll(b, 4, 0))
                    spread[group, column + 1, row:row + 8] = jnp.where(low_rows, pltpu.roll(a, 4, 0), b)

    for copy in copies[:early]:
        copy.wait()
    for pair in range(CHIPS):
        lay(pieces, 2 * pair, plan.pad + 8 * pair)
    if halo:
        for pair in range(2):
            lay(halo_pieces.at[0], 2 * pair, plan.pad - 16 + 8 * pair)
            lay(halo_pieces.at[1], 2 * pair, plan.pad + plan.sub_rows + 8 * pair)

    segments = plan.segments(plane * CHIPS + chip)
    for branch in range(plan.branches):
        @pl.when(mask_ref[branch] > 0)
        def _():
            shares = [
                cotangent_ref[strip * plan.branches + branch].astype(f32)
                for strip in range(-(-9 * plan.lanes // plan.depth_rows))
            ]
            for group in range(plan.lanes):
                kernel = []
                for tap in range(9):
                    row = tap * plan.lanes + group
                    at = plan.tile + row % plan.depth_rows
                    kernel.append(jnp.broadcast_to(shares[row // plan.depth_rows][at:at + 1], (plan.sub_rows, 128)))

                @pl.loop(0, plan.work)
                def _(w):
                    total = None
                    for j in range(3):
                        column = plan.neighbour(segments, w, (j - 1) * (branch + 1))
                        for i in range(3):
                            row = plan.pad + (i - 1) * plan.step_rows * (branch + 1)
                            term = spread[group, column, row:row + plan.sub_rows] * kernel[3 * i + j]
                            total = term if total is None else total + term
                    at = pl.multiple_of(w * plan.sub_rows, plan.sub_rows)
                    dw_out[branch, pl.ds(at, plan.sub_rows), group * 128:(group + 1) * 128] = total.astype(bf16)

    pixel = iota((plan.pixels, 128), 0)
    column, row = pixel // plan.sub_rows, pixel % plan.sub_rows
    source = (row // 2) * plan.tile + 2 * column + row % 2
    lane = iota(source.shape, 1)
    order = jnp.concatenate([one_hot(source == lane + 128 * k) for k in range(plan.pixels // 128)], 1)
    for pair in range(GROUP):
        for couple in range(branches // 2):
            left = cotangent_ref[pair * branches + 2 * couple].astype(f32)[:plan.tile]
            right = cotangent_ref[pair * branches + 2 * couple + 1].astype(f32)[:plan.tile]
            first, second = swap_halves(left, right)
            lanes = pl.ds(couple * 128, 128)
            sorted_rows[pl.ds(2 * pair * plan.tile, plan.tile), lanes] = first
            sorted_rows[pl.ds((2 * pair + 1) * plan.tile, plan.tile), lanes] = second
    cotangent = dot(order, sorted_rows[...].astype(bf16))
    joined[...] = jnp.zeros_like(joined)
    grads[...] = jnp.zeros_like(grads)
    for copy in copies[early:]:
        copy.wait()

    @pl.loop(0, branches)
    def _(branch):
        @pl.when(mask_ref[branch] > 0)
        def _():
            value, derivative = gelu_both(dot(dw_out[branch], point[branch]))
            value = value.astype(bf16)
            branch_out[branch] = value
            slope[branch] = derivative
            joined[...] += dot(value, joining[branch])

    value, derivative = gelu_both(joined[...])
    grad_joined = (cotangent * derivative).astype(bf16)
    pixel = iota((plan.pixels, plan.pixels), 1)
    column, row = pixel // plan.sub_rows, pixel % plan.sub_rows
    source = (row // 2) * plan.tile + 2 * column + row % 2
    back = one_hot(source == iota(source.shape, 0))
    sorted_rows[...] = dot(back, value.astype(bf16))
    for pair in range(GROUP):
        for couple in range(branches // 2):
            lanes = pl.ds(couple * 128, 128)
            left = sorted_rows[pl.ds(2 * pair * plan.tile, plan.tile), lanes]
            right = sorted_rows[pl.ds((2 * pair + 1) * plan.tile, plan.tile), lanes]
            first, second = swap_halves(left, right)
            output_ref[pair * branches + 2 * couple] = first.astype(bf16)
            output_ref[pair * branches + 2 * couple + 1] = second.astype(bf16)

    for branch in range(branches):
        slot = slots[branch]

        @pl.when(mask_ref[branch] > 0)
        def _():
            at = pl.multiple_of(slot * plan.grad_rows, 32)
            joining_part = (dot(branch_out[branch], grad_joined, ((0,), (0,))) * scale).astype(bf16)
            for chunk in range(GROUP):
                grads[chunk, pl.ds(at, plan.join_rows)] = joining_part[chunk * plan.join_rows:(chunk + 1) * plan.join_rows]
            grad_branch = dot(grad_joined, joining[branch], ((1,), (1,)))
            grad_pre = (grad_branch * slope[branch]).astype(bf16)
            grad_pre_ref[branch] = grad_pre
            at = pl.multiple_of(slot * plan.grad_rows + plan.join_rows, 32)
            point_part = (dot(dw_out[branch], grad_pre, ((0,), (0,))) * scale).astype(bf16)
            for chunk in range(GROUP):
                grads[chunk, pl.ds(at, plan.point_rows)] = point_part[
                    chunk * plan.point_rows:(chunk + 1) * plan.point_rows
                ]

    half = GROUP // 2
    first = pltpu.make_async_copy(grads.at[pl.ds((1 - core) * half, half)], send_ref, sems.at[0])
    second = pltpu.make_async_copy(grads.at[pl.ds(core * half, half)], keep_ref, sems.at[1])
    first.start()
    second.start()
    first.wait()
    second.wait()


def main_step(plan, scale, mask, tiles, pieces, halos, point, joining, mine, others):
    operands = [mask, tiles, *pieces, *halos, point, joining, *mine, *others]
    half = jax.ShapeDtypeStruct((GROUP // 2, SLOTS * plan.grad_rows, plan.width), bf16)
    return pl.pallas_call(
        functools.partial(main_kernel, plan, scale, len(halos) > 0),
        out_shape=[
            jax.ShapeDtypeStruct((GROUP * plan.branches, plan.tile, 128), bf16),
            half,
            half,
            jax.ShapeDtypeStruct((plan.branches, plan.pixels, plan.width), bf16),
            jax.ShapeDtypeStruct((plan.branches, plan.chans, plan.width), bf16),
            jax.ShapeDtypeStruct((plan.lanes, plan.window + 1, plan.tall, 128), f32),
        ],
        in_specs=[SMEM, VMEM] + [ANY] * (len(operands) - 2),
        out_specs=[VMEM, ANY, ANY, VMEM, VMEM, VMEM],
        scratch_shapes=[
            pltpu.VMEM((GROUP, plan.piece, plan.chans), bf16),
            pltpu.VMEM((2, 4, plan.piece, plan.chans) if halos else (16, 128), bf16),
            pltpu.VMEM((plan.branches, plan.pixels, plan.chans), bf16),
            pltpu.VMEM((plan.branches, plan.width, plan.width), bf16),
            pltpu.VMEM((plan.branches, plan.pixels, plan.width), bf16),
            pltpu.VMEM((plan.branches, plan.pixels, plan.width), f32),
            pltpu.VMEM((plan.pixels, plan.width), f32),
            pltpu.VMEM((plan.pixels, plan.width), f32),
            pltpu.VMEM((GROUP, SLOTS * plan.grad_rows, plan.width), bf16),
            pltpu.SemaphoreType.DMA((GROUP + 2 + 4 * plan.branches,)),
        ],
        compiler_params=pltpu.CompilerParams(vmem_limit_bytes=32 << 20),
        cost_estimate=pl.CostEstimate(flops=1 << 31, bytes_accessed=1 << 24, transcendentals=0),
        name="forward_and_backward",
    )(*operands)


def depth_grad_kernel(plan, scale, mask_ref, grad_pre_ref, point, spread, out_ref, grad_dw, rows):
    plane, _, chip, _ = whereabouts()
    slots, _ = slots_of(mask_ref, plan.branches)
    segments = plan.segments(plane * CHIPS + chip)
    out_ref[...] = jnp.zeros_like(out_ref)
    rows[...] = jnp.zeros_like(rows)
    for branch in range(plan.branches):
        @pl.when(mask_ref[branch] > 0)
        def _():
            grad_pre = grad_pre_ref[branch]
            for group in range(plan.lanes):
                grad_dw[group] = dot(grad_pre, point[branch, group * 128:(group + 1) * 128], ((1,), (1,)))
            for group in range(plan.lanes):
                def add_column(w, sums):
                    at = pl.multiple_of(w * plan.sub_rows, plan.sub_rows)
                    given = grad_dw[group, pl.ds(at, plan.sub_rows)]
                    sums = list(sums)
                    for j in range(3):
                        column = plan.neighbour(segments, w, (j - 1) * (branch + 1))
                        for i in range(3):
                            row = plan.pad + (i - 1) * plan.step_rows * (branch + 1)
                            product = spread[group, column, row:row + plan.sub_rows] * given
                            for part in range(plan.sub_rows // 8):
                                sums[3 * i + j] = sums[3 * i + j] + product[8 * part:8 * part + 8]
                    return tuple(sums)

                sums = lax.fori_loop(0, plan.work, add_column, (jnp.zeros((8, 128), f32),) * 9)
                lanes = slice((group % 2) * 128, (group % 2) * 128 + 128)
                for tap in range(9):
                    row = 2 * tap + group // 2
                    rows[row:row + 1, lanes] = jnp.sum(sums[tap], axis=0, keepdims=True) * scale
            out_ref[slots[branch]] = rows[...].astype(bf16)


def depth_grad(plan, scale, mask, grad_pre, point, spread):
    return pl.pallas_call(
        functools.partial(depth_grad_kernel, plan, scale),
        out_shape=jax.ShapeDtypeStruct((SLOTS, 32, plan.width), bf16),
        in_specs=[SMEM] + [VMEM] * 3,
        out_specs=VMEM,
        scratch_shapes=[
            pltpu.VMEM((plan.lanes, plan.pixels, 128), f32),
            pltpu.VMEM((32, plan.width), f32),
        ],
        compiler_params=pltpu.CompilerParams(vmem_limit_bytes=24 << 20),
        cost_estimate=pl.CostEstimate(flops=1 << 26, bytes_accessed=1 << 24, transcendentals=0),
        name="depth_grad",
    )(mask, grad_pre, point, spread)


def chip_sum_kernel(keep_ref, other_ref, *out_refs):
    _, _, chip, _ = whereabouts()
    for hop in range(CHIPS):
        out_refs[hop][...] = (keep_ref[chip ^ hop].astype(f32) + other_ref[chip ^ hop].astype(f32)).astype(bf16)


def chip_sum(keep, other):
    return pl.pallas_call(
        chip_sum_kernel,
        out_shape=[jax.ShapeDtypeStruct(keep.shape[1:], bf16)] * CHIPS,
        in_specs=[VMEM] * 2,
        out_specs=[VMEM] * CHIPS,
        compiler_params=pltpu.CompilerParams(vmem_limit_bytes=16 << 20),
        name="chip_sum",
    )(keep, other)


def plane_sum_kernel(plan, mask_ref, depth_ref, *refs):
    total, out_refs = refs[-1], refs[CHIPS:-1]
    plane, _, _, _ = whereabouts()
    slots, _ = slots_of(mask_ref, plan.branches)
    added = refs[0][...].astype(f32)
    for ref in refs[1:CHIPS]:
        added = added + ref[...].astype(f32)
    total[...] = added
    rows = plan.grad_rows
    for hop in range(plan.branches):
        slot = pick(slots, plane ^ hop)
        out_refs[hop][0:rows] = total[pl.ds(pl.multiple_of(slot * rows, 32), rows)].astype(bf16)
        out_refs[hop][rows:] = depth_ref[slot]


def plane_sum(plan, mask, depth, parts):
    return pl.pallas_call(
        functools.partial(plane_sum_kernel, plan),
        out_shape=[jax.ShapeDtypeStruct((plan.grad_rows + depth.shape[1], plan.width), bf16)] * plan.branches,
        in_specs=[SMEM] + [VMEM] * (1 + CHIPS),
        out_specs=[VMEM] * plan.branches,
        scratch_shapes=[pltpu.VMEM(parts[0].shape, f32)],
        compiler_params=pltpu.CompilerParams(vmem_limit_bytes=16 << 20),
        name="plane_sum",
    )(mask, depth, *parts)


def place_grads_kernel(plan, mask_ref, chunks_ref, joining_ref, point_ref, depth_ref):
    plane, _, _, _ = whereabouts()
    active = pick([mask_ref[branch] for branch in range(plan.branches)], plane) > 0
    rows = plan.grad_rows
    taps = None
    for chip in range(CHIPS):
        for core in range(2):
            chunk = jnp.where(active, chunks_ref[2 * chip + core].astype(f32), 0.0)
            at = core * CHIPS + chip
            joining_ref[at * plan.join_rows:(at + 1) * plan.join_rows] = chunk[:plan.join_rows]
            point_ref[0, at * plan.point_rows:(at + 1) * plan.point_rows] = chunk[plan.join_rows:rows]
            taps = chunk[rows:] if taps is None else taps + chunk[rows:]
    for tap in range(9):
        for group in range(plan.lanes):
            row, lane = 2 * tap + group // 2, (group % 2) * 128
            depth_ref[0, tap:tap + 1, group * 128:(group + 1) * 128] = taps[row:row + 1, lane:lane + 128]


def place_grads(plan, mask, chunks):
    return pl.pallas_call(
        functools.partial(place_grads_kernel, plan),
        out_shape=[
            jax.ShapeDtypeStruct((plan.width, plan.width), f32),
            jax.ShapeDtypeStruct((1, plan.chans, plan.width), f32),
            jax.ShapeDtypeStruct((1, 9, plan.chans), f32),
        ],
        in_specs=[SMEM, VMEM],
        out_specs=[VMEM] * 3,
        compiler_params=pltpu.CompilerParams(vmem_limit_bytes=16 << 20),
        name="place_grads",
    )(mask, chunks)


def per_device(features, cotangent, depth_weight, point_weight, joining_weight, branch_mask):
    row_count, col_count, chan_count = features.shape
    strips = lax.axis_size("strip")
    branches = lax.axis_size("branch")
    width = joining_weight.shape[1]
    plan = Plan(row_count, col_count, chan_count, width, branches)
    scale = 1.0 / math.sqrt(row_count * col_count * strips)
    groups = None if strips == GROUP else [list(range(g, g + GROUP)) for g in range(0, strips, GROUP)]

    def flip_strip(value, hop):
        return lax.ppermute(value, "strip", [(s, s ^ hop) for s in range(strips)])

    def flip_branch(value, hop):
        return lax.ppermute(value, "branch", [(b, b ^ hop) for b in range(branches)])

    def all_to_all(tiles):
        if groups is None:
            return lax.all_to_all(tiles, ("strip", "branch"), 0, 0, tiled=True)
        tiles = tiles.reshape(GROUP, branches, *tiles.shape[1:])
        tiles = lax.all_to_all(tiles, "branch", 1, 1, tiled=True)
        tiles = lax.all_to_all(tiles, "strip", 0, 0, tiled=True, axis_index_groups=groups)
        return tiles.reshape(GROUP * branches, *tiles.shape[2:])

    half = halve_weights(plan, point_weight, joining_weight)
    mine = [flip_branch(half, hop) for hop in range(1, branches)]

    keep, send = spread_features(plan, features)
    joint = join_features(plan, keep, flip_strip(send, 1))
    pieces = [joint[0]] + [flip_strip(joint[hop], 2 * hop) for hop in range(1, CHIPS)]
    mine, pieces = lax.optimization_barrier((mine, pieces))
    others = [flip_strip(value, 1) for value in mine]
    halos = []
    if groups is not None:
        strip = lax.axis_index("strip") % GROUP
        near = jnp.stack(pieces).reshape(CHIPS, 2, plan.piece, plan.chans)
        at = jnp.arange(GROUP)
        near = near[(at // 2) ^ (strip // 2), (at % 2) ^ (strip % 2)]
        down = [(s, s + GROUP) for s in range(strips - GROUP)]
        up = [(s + GROUP, s) for s in range(strips - GROUP)]
        halos = [lax.ppermute(near[GROUP - 4:], "strip", down), lax.ppermute(near[:4], "strip", up)]
    tiles = all_to_all(send_cotangent(plan, jnp.swapaxes(cotangent, 1, 2), depth_weight))

    output_tiles, keep, send, grad_pre, points, spread = main_step(
        plan, scale, branch_mask, tiles, pieces, halos, point_weight, joining_weight, mine, others
    )
    parts = chip_sum(keep, flip_strip(send, 1))
    parts, output_tiles, grad_pre = lax.optimization_barrier((parts, output_tiles, grad_pre))
    parts = [parts[0]] + [flip_strip(parts[hop], 2 * hop) for hop in range(1, CHIPS)]
    taps = depth_grad(plan, scale, branch_mask, grad_pre, points, spread)
    output = place_output(plan, all_to_all(output_tiles))
    shares = plane_sum(plan, branch_mask, taps, parts)
    shares = [shares[0]] + [flip_branch(shares[hop], hop) for hop in range(1, branches)]
    share = sum(value.astype(f32) for value in shares)
    if groups is not None:
        peers = [list(range(s, strips, GROUP)) for s in range(GROUP)]
        share = lax.psum(share, "strip", axis_index_groups=peers)
    chunks = lax.all_gather(share.astype(bf16), "strip", axis=0, axis_index_groups=groups)
    joining_total, point_total, depth_total = place_grads(plan, branch_mask, chunks)
    return (jnp.swapaxes(output, 1, 2), joining_total, point_total, depth_total)


def solution(mesh):
    placed = (
        P("strip", None, None),
        P("strip", None, "branch"),
        P("branch", None, None),
        P("branch", None, None),
        P("branch", None),
        P(),
    )
    return jax.shard_map(
        per_device,
        mesh=mesh,
        in_specs=placed,
        out_specs=(
            P("strip", None, "branch"),
            P("branch", None),
            P("branch", None, None),
            P("branch", None, None),
        ),
        check_vma=False,
    )
```

time: 110 us -> 82.7 us (0.75)
  waiting for transfers between devices: 36 us -> 16 us
  starting transfers between devices: 39.8 us -> 28.1 us
  Pallas kernels: 21.4 us -> 22.8 us
  blocking collectives: 8.85 us -> 10.1 us
    ppermute x14 -> x11, waiting for transfers between devices: 16.1 us -> 5.15 us  [flip_strip(): return lax.ppermute(value, 'strip', [(s, s ^ hop) for s in range(strips)])]
    ppermute x9 -> x6, waiting for transfers between devices: 20 us -> 10.9 us  [flip_branch(): lax.ppermute(value, 'branch', [(b, b ^ hop) for b in range(branches)])]
    ppermute x14 -> x11, starting transfers between devices: 14.6 us -> 8.56 us  [flip_strip(): return lax.ppermute(value, 'strip', [(s, s ^ hop) for s in range(strips)])]
    all_to_all x2, starting transfers between devices: 9.9 us -> 6.13 us  [all_to_all(): return lax.all_to_all(tiles, ('strip', 'branch'), 0, 0, tiled=True)]
    unnamed x13 -> x17, local copies, waits for them, and re-layouts: 2.72 us -> 5.56 us
    ppermute x9 -> x6, starting transfers between devices: 15.3 us -> 13.4 us  [flip_branch(): lax.ppermute(value, 'branch', [(b, b ^ hop) for b in range(branches)])]
    dynamic_slice x2 -> x0, local copies, waits for them, and re-layouts: 1.87 us -> none  [the longest x1 0.96 us: per_device(): lax.dynamic_slice(joining_weight, (core * (width // 2), 0), (width // 2,...]
    all_gather x1, blocking collectives: 8.85 us -> 10.1 us  [per_device(): lax.all_gather(share.astype(bf16), 'strip', axis=0, axis_index_groups=gro...]
  transfers between devices with their start and end apart: 25 -> 19, of which waited for: 13 -> 7; matrix products, arithmetic and copies ran while one was open for 2% -> 1% of each run, Pallas kernels for 3% -> 9%
where the time goes in v2:
time: 82.7 us; the launch traced here: 83.4 us
  starting transfers between devices  28.1 us (34%)
  Pallas kernels  22.8 us (28%)
  waiting for transfers between devices  16 us (19%)
  blocking collectives  10.1 us (12%)
  local copies, waits for them, and re-layouts  5.56 us (7%)
    ppermute x6, starting transfers between devices, flip_branch(): lax.ppermute(value, 'branch', [(b, b ^ hop) for b in range(branches)])  13.4 us
    pallas_call x1, Pallas kernels, main_step(): pl.pallas_call(functools.partial(main_kernel, plan, scale, len(halos) > 0...  12.5 us
    ppermute x6, waiting for transfers between devices, flip_branch(): lax.ppermute(value, 'branch', [(b, b ^ hop) for b in range(branches)])  10.9 us
    all_gather x1, blocking collectives, per_device(): lax.all_gather(share.astype(bf16), 'strip', axis=0, axis_index_groups=gro...  10.1 us
    ppermute x11, starting transfers between devices, flip_strip(): return lax.ppermute(value, 'strip', [(s, s ^ hop) for s in range(strips)])  8.56 us
    all_to_all x2, starting transfers between devices, all_to_all(): return lax.all_to_all(tiles, ('strip', 'branch'), 0, 0, tiled=True)  6.13 us
    unnamed x17, local copies, waits for them, and re-layouts  5.56 us
    ppermute x11, waiting for transfers between devices, flip_strip(): return lax.ppermute(value, 'strip', [(s, s ^ hop) for s in range(strips)])  5.15 us
  transfers between devices with their start and end apart: 19, of which 7 were waited for; matrix products, arithmetic and copies ran while one was open for 1% of the time, Pallas kernels for 9%

profile of v2, /device:TPU:0, one launch (start us, length us, event | category | flops | bytes accessed | tf_op | source)
XLA Modules:
  0.0 83.4 jit_solution(706258233412511239)
XLA Ops:
  0.6 1.4 %copy-done = bf16[8,192,512]{2,1,0:T(8,128)(2,1)S(1)} copy-done((bf16[8,192,512]{2,1,0:T(8,128)(2,1)S(1)}, bf16[8,192,512]{2,1,0:T(8,128)(2,1)}, u32[]{:S(2)}) %copy-start) | copy-done | bytes 1572888
  3.3 0.9 %copy-done.2 = bf16[1,512,256]{2,1,0:T(8,128)(2,1)S(1)} copy-done((bf16[1,512,256]{2,1,0:T(8,128)(2,1)S(1)}, bf16[1,512,256]{2,1,0:T(8,128)(2,1)}, u32[]{:S(2)}) %copy-start.2) | copy-done | bytes 262168
  4.2 0.9 %copy-done.4 = bf16[256,256]{1,0:T(8,128)(2,1)S(1)} copy-done((bf16[256,256]{1,0:T(8,128)(2,1)S(1)}, bf16[256,256]{1,0:T(8,128)(2,1)}, u32[]{:S(2)}) %copy-start.4) | copy-done | bytes 131096
  5.4 4.7 %collective-permute-start.2 = (bf16[384,256]{1,0:T(8,128)(2,1)S(1)}, bf16[384,256]{1,0:T(8,128)(2,1)S(1)}, u32[]{:S(2)}, u32[]{:S(2)}) collective-permute-start(bf16[384,256]{1,0:T(8,128)(2,1)S(1)} %halve_weights.1), channel_id=1, source_target_pairs={{0,3},{1,2},{2,1},{3,0},{4,7},{5,6},{6,5},{7,4},{8,11},{9,10},{10,... | collective-permute-start | bytes 589832 | tf_op jit(solution)/shard_map/ppermute | solution.py:648
  10.0 0.9 %copy-done.1 = bf16[8,192,64]{1,2,0:T(8,128)(2,1)S(1)} copy-done((bf16[8,192,64]{1,2,0:T(8,128)(2,1)S(1)}, bf16[8,192,64]{1,2,0:T(8,128)(2,1)}, u32[]{:S(2)}) %copy-start.1) | copy-done | bytes 196632
  11.7 1.2 %send_cotangent.1 = bf16[32,32,128]{2,1,0:T(8,128)(2,1)} custom-call(bf16[8,64,192]{2,1,0:T(8,128)(2,1)S(1)} %bitcast.4, bf16[1,9,512]{2,1,0:T(8,128)(2,1)S(1)} %copy-done.6), custom_call_target="tpu_custom_call" | custom-call | flops 1 | bytes 1 | tf_op jit(solution)/shard_map/send_cotangent/pallas_call | solution.py:252
  12.9 2.8 %all-to-all-start = ((bf16[32,32,128]{2,1,0:T(8,128)(2,1)}), bf16[32,32,128]{2,1,0:T(8,128)(2,1)S(1)}, u32[]{:S(2)}, u32[]{:S(2)}) async-start(bf16[32,32,128]{2,1,0:T(8,128)(2,1)} %send_cotangent.1), calls=%async_computation | async-start | bytes 524288 | tf_op jit(solution)/shard_map/all_to_all | solution.py:652
  15.7 2.7 %collective-permute-start.1 = (bf16[384,256]{1,0:T(8,128)(2,1)S(1)}, bf16[384,256]{1,0:T(8,128)(2,1)S(1)}, u32[]{:S(2)}, u32[]{:S(2)}) collective-permute-start(bf16[384,256]{1,0:T(8,128)(2,1)S(1)} %halve_weights.1), channel_id=1, source_target_pairs={{0,2},{1,3},{2,0},{3,1},{4,6},{5,7},{6,4},{7,5},{8,10},{9,11},{10,... | collective-permute-start | bytes 589832 | tf_op jit(solution)/shard_map/ppermute | solution.py:648
  18.5 1.5 %collective-permute-start = (bf16[384,256]{1,0:T(8,128)(2,1)S(1)}, bf16[384,256]{1,0:T(8,128)(2,1)S(1)}, u32[]{:S(2)}, u32[]{:S(2)}) collective-permute-start(bf16[384,256]{1,0:T(8,128)(2,1)S(1)} %halve_weights.1), channel_id=1, source_target_pairs={{0,1},{1,0},{2,3},{3,2},{4,5},{5,4},{6,7},{7,6},{8,9},{9,8},{10,11... | collective-permute-start | bytes 589832 | tf_op jit(solution)/shard_map/ppermute | solution.py:648
  20.0 1.5 %collective-permute-start.4 = (bf16[160,512]{1,0:T(8,128)(2,1)S(1)}, bf16[160,512]{1,0:T(8,128)(2,1)S(1)}, u32[]{:S(2)}, u32[]{:S(2)}) collective-permute-start(bf16[160,512]{1,0:T(8,128)(2,1)S(1)} %get-tuple-element.43), channel_id=1, source_target_pairs={{0,8},{4,12},{8,0},{12,4},{16,24},{20,28},{24,16},{28,20},{1,9},{5... | collective-permute-start | bytes 491528 | tf_op jit(solution)/shard_map/ppermute | solution.py:645
  21.6 1.5 %collective-permute-start.5 = (bf16[160,512]{1,0:T(8,128)(2,1)S(1)}, bf16[160,512]{1,0:T(8,128)(2,1)S(1)}, u32[]{:S(2)}, u32[]{:S(2)}) collective-permute-start(bf16[160,512]{1,0:T(8,128)(2,1)S(1)} %get-tuple-element.44), channel_id=1, source_target_pairs={{0,16},{4,20},{8,24},{12,28},{16,0},{20,4},{24,8},{28,12},{1,17},{... | collective-permute-start | bytes 491528 | tf_op jit(solution)/shard_map/ppermute | solution.py:645
  23.6 10.0 %collective-permute-done.1.refs_7_ = bf16[384,256]{1,0:T(8,128)(2,1)S(1)} collective-permute-done((bf16[384,256]{1,0:T(8,128)(2,1)S(1)}, bf16[384,256]{1,0:T(8,128)(2,1)S(1)}, u32[]{:S(2)}, u32[]{:S(2)}) %collective-permute-start.1) | collective-permute-done | bytes 196640 | tf_op jit(solution)/shard_map/ppermute | solution.py:648
  35.6 12.5 %forward_and_backward.1 = (bf16[32,24,128]{2,1,0:T(8,128)(2,1)}, bf16[4,288,256]{2,1,0:T(8,128)(2,1)S(1)}, bf16[4,288,256]{2,1,0:T(8,128)(2,1)S(1)}, bf16[4,384,...) custom-call(s32[4]{0:T(128)S(1)} %copy-done.7, ...), custom_call_target="tpu_custom_call" | custom-call | flops 2147483648 | bytes 16777216 | tf_op jit(solution)/shard_map/forward_and_backward/pallas_call | solution.py:478
  48.4 1.8 %collective-permute-done.10.other_ref = bf16[4,288,256]{2,1,0:T(8,128)(2,1)S(1)} collective-permute-done((bf16[4,288,256]{2,1,0:T(8,128)(2,1)S(1)}, bf16[4,288,256]{2,1,0:T(8,128)(2,1)S(1)}, u32[]{:S(2)}, u32[]{:S(2)}) %collective-permute-start.10) | collective-permute-done | bytes 589856 | tf_op jit(solution)/shard_map/ppermute | solution.py:645
  50.3 1.5 %collective-permute-start.11 = (bf16[288,256]{1,0:T(8,128)(2,1)S(1)}, bf16[288,256]{1,0:T(8,128)(2,1)S(1)}, u32[]{:S(2)}, u32[]{:S(2)}) collective-permute-start(bf16[288,256]{1,0:T(8,128)(2,1)S(1)} %get-tuple-element.66), channel_id=1, source_target_pairs={{0,8},{4,12},{8,0},{12,4},{16,24},{20,28},{24,16},{28,20},{1,9},{5... | collective-permute-start | bytes 442376 | tf_op jit(solution)/shard_map/ppermute | solution.py:645
  51.9 1.5 %collective-permute-start.12 = (bf16[288,256]{1,0:T(8,128)(2,1)S(1)}, bf16[288,256]{1,0:T(8,128)(2,1)S(1)}, u32[]{:S(2)}, u32[]{:S(2)}) collective-permute-start(bf16[288,256]{1,0:T(8,128)(2,1)S(1)} %get-tuple-element.67), channel_id=1, source_target_pairs={{0,16},{4,20},{8,24},{12,28},{16,0},{20,4},{24,8},{28,12},{1,17},{... | collective-permute-start | bytes 442376 | tf_op jit(solution)/shard_map/ppermute | solution.py:645
  53.9 4.9 %depth_grad.1.depth_ref = bf16[3,32,256]{2,1,0:T(8,128)(2,1)S(1)} custom-call(s32[4]{0:T(128)S(1)} %copy-done.7, bf16[4,384,256]{2,1,0:T(8,128)(2,1)S(1)} %get-tuple-element.62.grad_pre_ref, bf16[4,512,256]{2,1,0:T(8,128)(2,1)S(1)} %get-tuple-element.63.point, f32[4,21,64,128]{3,2,1,0:T(8,128)S(1)} %get-tuple-element.64.spread), custom_call_target="tpu_custom_call" | custom-call | flops 67108864 | bytes 16777216 | tf_op jit(solution)/shard_map/depth_grad/pallas_call | solution.py:543
  58.8 1.9 %collective-permute-done.12.refs_2_ = bf16[288,256]{1,0:T(8,128)(2,1)S(1)} collective-permute-done((bf16[288,256]{1,0:T(8,128)(2,1)S(1)}, bf16[288,256]{1,0:T(8,128)(2,1)S(1)}, u32[]{:S(2)}, u32[]{:S(2)}) %collective-permute-start.12) | collective-permute-done | bytes 147488 | tf_op jit(solution)/shard_map/ppermute | solution.py:645
  61.5 2.5 %collective-permute-start.15 = (bf16[128,256]{1,0:T(8,128)(2,1)S(1)}, bf16[128,256]{1,0:T(8,128)(2,1)S(1)}, u32[]{:S(2)}, u32[]{:S(2)}) collective-permute-start(bf16[128,256]{1,0:T(8,128)(2,1)S(1)} %get-tuple-element.71), channel_id=1, source_target_pairs={{0,2},{1,3},{2,0},{3,1},{4,6},{5,7},{6,4},{7,5},{8,10},{9,11},{10,... | collective-permute-start | bytes 196616 | tf_op jit(solution)/shard_map/ppermute | solution.py:648
  64.0 1.8 %collective-permute-start.16 = (bf16[128,256]{1,0:T(8,128)(2,1)S(1)}, bf16[128,256]{1,0:T(8,128)(2,1)S(1)}, u32[]{:S(2)}, u32[]{:S(2)}) collective-permute-start(bf16[128,256]{1,0:T(8,128)(2,1)S(1)} %get-tuple-element.72), channel_id=1, source_target_pairs={{0,3},{1,2},{2,1},{3,0},{4,7},{5,6},{6,5},{7,4},{8,11},{9,10},{10,... | collective-permute-start | bytes 196616 | tf_op jit(solution)/shard_map/ppermute | solution.py:648
  65.9 3.3 %all-to-all-start.1 = ((bf16[32,24,128]{2,1,0:T(8,128)(2,1)}), bf16[32,24,128]{2,1,0:T(8,128)(2,1)S(1)}, u32[]{:S(2)}, u32[]{:S(2)}) async-start(bf16[32,24,128]{2,1,0:T(8,128)(2,1)} %get-tuple-element.61), calls=%async_computation.1 | async-start | bytes 393216 | tf_op jit(solution)/shard_map/all_to_all | solution.py:652
  70.1 10.1 %all-gather = bf16[1024,256]{1,0:T(8,128)(2,1)S(1)} all-gather(bf16[128,256]{1,0:T(8,128)(2,1)S(1)} %add_convert_fusion), channel_id=2, replica_groups=mesh['strip'=8,'branch'=4] {'strip'}, dimensions={0}, use_global_device_ids=true | all-gather | bytes 589824 | tf_op jit(solution)/shard_map/all_gather | solution.py:691
  80.2 1.5 %place_grads.1 = (f32[256,256]{1,0:T(8,128)}, f32[1,512,256]{2,1,0:T(8,128)}, f32[1,9,512]{2,1,0:T(8,128)S(1)}) custom-call(s32[4]{0:T(128)S(1)} %copy-done.7, bf16[8,128,256]{2,1,0:T(8,128)(2,1)S(1)} %bitcast.3), custom_call_target="tpu_custom_call" | custom-call | tf_op jit(solution)/shard_map/place_grads/pallas_call | solution.py:621
  82.3 1.0 %place_output.1 = bf16[8,64,192]{2,1,0:T(8,128)(2,1)} custom-call(bf16[32,24,128]{2,1,0:T(8,128)(2,1)S(1)} %all-to-all-done.1.tiles_ref), custom_call_target="tpu_custom_call" | custom-call | tf_op jit(solution)/shard_map/place_output/pallas_call | solution.py:289
  (43 shorter events, 8.1 us)
Async XLA Ops:
  0.6 1.4 %copy-start = (bf16[8,192,512]{2,1,0:T(8,128)(2,1)S(1)}, bf16[8,192,512]{2,1,0:T(8,128)(2,1)}, u32[]{:S(2)}) copy-start(bf16[8,192,512]{2,1,0:T(8,128)(2,1)} %features_ref.1) | copy-start | bytes 4718596
  2.0 33.6 %copy-start.3 = (bf16[1,512,256]{2,1,0:T(8,128)(2,1)S(1)}, bf16[1,512,256]{2,1,0:T(8,128)(2,1)}, u32[]{:S(2)}) copy-start(bf16[1,512,256]{2,1,0:T(8,128)(2,1)} %refs_4_.1) | copy-start | bytes 786436
  2.0 33.6 %copy-start.5 = (bf16[256,256]{1,0:T(8,128)(2,1)S(1)}, bf16[256,256]{1,0:T(8,128)(2,1)}, u32[]{:S(2)}) copy-start(bf16[256,256]{1,0:T(8,128)(2,1)} %refs_5_.1) | copy-start | bytes 393220
  2.0 33.6 %copy-start.7 = (s32[4]{0:T(128)S(1)}, s32[4]{0:T(128)}, u32[]{:S(2)}) copy-start(s32[4]{0:T(128)} %mask_ref.7) | copy-start | bytes 52
  2.7 17.2 %collective-permute-start.3 = (bf16[4,80,512]{2,1,0:T(8,128)(2,1)S(1)}, bf16[4,80,512]{2,1,0:T(8,128)(2,1)S(1)}, u32[]{:S(2)}, u32[]{:S(2)}) collective-permute-start(bf16[4,80,512]{2,1,0:T(8,128)(2,1)S(1)} %get-tuple-element.41), channel_id=1, source_target_pairs={{0,4},{4,0},{8,12},{12,8},{16,20},{20,16},{24,28},{28,24},{1,5},{5... | collective-permute-start | bytes 983048 | tf_op jit(solution)/shard_map/ppermute | solution.py:645
  3.3 0.9 %copy-start.2 = (bf16[1,512,256]{2,1,0:T(8,128)(2,1)S(1)}, bf16[1,512,256]{2,1,0:T(8,128)(2,1)}, u32[]{:S(2)}) copy-start(bf16[1,512,256]{2,1,0:T(8,128)(2,1)} %refs_4_.1) | copy-start | bytes 786436
  5.4 17.7 %collective-permute-start.2 = (bf16[384,256]{1,0:T(8,128)(2,1)S(1)}, bf16[384,256]{1,0:T(8,128)(2,1)S(1)}, u32[]{:S(2)}, u32[]{:S(2)}) collective-permute-start(bf16[384,256]{1,0:T(8,128)(2,1)S(1)} %halve_weights.1), channel_id=1, source_target_pairs={{0,3},{1,2},{2,1},{3,0},{4,7},{5,6},{6,5},{7,4},{8,11},{9,10},{10,... | collective-permute-start | bytes 589832 | tf_op jit(solution)/shard_map/ppermute | solution.py:648
  12.9 21.3 %all-to-all-start = ((bf16[32,32,128]{2,1,0:T(8,128)(2,1)}), bf16[32,32,128]{2,1,0:T(8,128)(2,1)S(1)}, u32[]{:S(2)}, u32[]{:S(2)}) async-start(bf16[32,32,128]{2,1,0:T(8,128)(2,1)} %send_cotangent.1), calls=%async_computation | async-start | bytes 524288 | tf_op jit(solution)/shard_map/all_to_all | solution.py:652
  15.7 17.8 %collective-permute-start.1 = (bf16[384,256]{1,0:T(8,128)(2,1)S(1)}, bf16[384,256]{1,0:T(8,128)(2,1)S(1)}, u32[]{:S(2)}, u32[]{:S(2)}) collective-permute-start(bf16[384,256]{1,0:T(8,128)(2,1)S(1)} %halve_weights.1), channel_id=1, source_target_pairs={{0,2},{1,3},{2,0},{3,1},{4,6},{5,7},{6,4},{7,5},{8,10},{9,11},{10,... | collective-permute-start | bytes 589832 | tf_op jit(solution)/shard_map/ppermute | solution.py:648
  18.5 15.1 %collective-permute-start = (bf16[384,256]{1,0:T(8,128)(2,1)S(1)}, bf16[384,256]{1,0:T(8,128)(2,1)S(1)}, u32[]{:S(2)}, u32[]{:S(2)}) collective-permute-start(bf16[384,256]{1,0:T(8,128)(2,1)S(1)} %halve_weights.1), channel_id=1, source_target_pairs={{0,1},{1,0},{2,3},{3,2},{4,5},{5,4},{6,7},{7,6},{8,9},{9,8},{10,11... | collective-permute-start | bytes 589832 | tf_op jit(solution)/shard_map/ppermute | solution.py:648
  20.0 13.5 %collective-permute-start.4 = (bf16[160,512]{1,0:T(8,128)(2,1)S(1)}, bf16[160,512]{1,0:T(8,128)(2,1)S(1)}, u32[]{:S(2)}, u32[]{:S(2)}) collective-permute-start(bf16[160,512]{1,0:T(8,128)(2,1)S(1)} %get-tuple-element.43), channel_id=1, source_target_pairs={{0,8},{4,12},{8,0},{12,4},{16,24},{20,28},{24,16},{28,20},{1,9},{5... | collective-permute-start | bytes 491528 | tf_op jit(solution)/shard_map/ppermute | solution.py:645
  21.6 12.0 %collective-permute-start.5 = (bf16[160,512]{1,0:T(8,128)(2,1)S(1)}, bf16[160,512]{1,0:T(8,128)(2,1)S(1)}, u32[]{:S(2)}, u32[]{:S(2)}) collective-permute-start(bf16[160,512]{1,0:T(8,128)(2,1)S(1)} %get-tuple-element.44), channel_id=1, source_target_pairs={{0,16},{4,20},{8,24},{12,28},{16,0},{20,4},{24,8},{28,12},{1,17},{... | collective-permute-start | bytes 491528 | tf_op jit(solution)/shard_map/ppermute | solution.py:645
  23.1 10.5 %collective-permute-start.6 = (bf16[160,512]{1,0:T(8,128)(2,1)S(1)}, bf16[160,512]{1,0:T(8,128)(2,1)S(1)}, u32[]{:S(2)}, u32[]{:S(2)}) collective-permute-start(bf16[160,512]{1,0:T(8,128)(2,1)S(1)} %get-tuple-element.45), channel_id=1, source_target_pairs={{0,24},{4,28},{8,16},{12,20},{16,8},{20,12},{24,0},{28,4},{1,25},{... | collective-permute-start | bytes 491528 | tf_op jit(solution)/shard_map/ppermute | solution.py:645
  33.6 1.5 %collective-permute-start.7 = (bf16[384,256]{1,0:T(8,128)(2,1)S(1)}, bf16[384,256]{1,0:T(8,128)(2,1)S(1)}, u32[]{:S(2)}, u32[]{:S(2)}) collective-permute-start(bf16[384,256]{1,0:T(8,128)(2,1)S(1)} %collective-permute-done.refs_6_), channel_id=1, source_target_pairs={{0,4},{4,0},{8,12},{12,8},{16,20},{20,16},{24,28},{28,24},{1,5},{5... | collective-permute-start | bytes 589832 | tf_op jit(solution)/shard_map/ppermute | solution.py:645
  33.6 1.7 %collective-permute-start.8 = (bf16[384,256]{1,0:T(8,128)(2,1)S(1)}, bf16[384,256]{1,0:T(8,128)(2,1)S(1)}, u32[]{:S(2)}, u32[]{:S(2)}) collective-permute-start(bf16[384,256]{1,0:T(8,128)(2,1)S(1)} %collective-permute-done.1.refs_7_), channel_id=1, source_target_pairs={{0,4},{4,0},{8,12},{12,8},{16,20},{20,16},{24,28},{28,24},{1,5},{5... | collective-permute-start | bytes 589832 | tf_op jit(solution)/shard_map/ppermute | solution.py:645
  34.1 1.5 %collective-permute-start.9 = (bf16[384,256]{1,0:T(8,128)(2,1)S(1)}, bf16[384,256]{1,0:T(8,128)(2,1)S(1)}, u32[]{:S(2)}, u32[]{:S(2)}) collective-permute-start(bf16[384,256]{1,0:T(8,128)(2,1)S(1)} %collective-permute-done.2.refs_8_), channel_id=1, source_target_pairs={{0,4},{4,0},{8,12},{12,8},{16,20},{20,16},{24,28},{28,24},{1,5},{5... | collective-permute-start | bytes 589832 | tf_op jit(solution)/shard_map/ppermute | solution.py:645
  48.1 2.1 %collective-permute-start.10 = (bf16[4,288,256]{2,1,0:T(8,128)(2,1)S(1)}, bf16[4,288,256]{2,1,0:T(8,128)(2,1)S(1)}, u32[]{:S(2)}, u32[]{:S(2)}) collective-permute-start(bf16[4,288,256]{2,1,0:T(8,128)(2,1)S(1)} %get-tuple-element.54), channel_id=1, source_target_pairs={{0,4},{4,0},{8,12},{12,8},{16,20},{20,16},{24,28},{28,24},{1,5},{5... | collective-permute-start | bytes 1769480 | tf_op jit(solution)/shard_map/ppermute | solution.py:645
  50.3 8.4 %collective-permute-start.11 = (bf16[288,256]{1,0:T(8,128)(2,1)S(1)}, bf16[288,256]{1,0:T(8,128)(2,1)S(1)}, u32[]{:S(2)}, u32[]{:S(2)}) collective-permute-start(bf16[288,256]{1,0:T(8,128)(2,1)S(1)} %get-tuple-element.66), channel_id=1, source_target_pairs={{0,8},{4,12},{8,0},{12,4},{16,24},{20,28},{24,16},{28,20},{1,9},{5... | collective-permute-start | bytes 442376 | tf_op jit(solution)/shard_map/ppermute | solution.py:645
  51.9 8.9 %collective-permute-start.12 = (bf16[288,256]{1,0:T(8,128)(2,1)S(1)}, bf16[288,256]{1,0:T(8,128)(2,1)S(1)}, u32[]{:S(2)}, u32[]{:S(2)}) collective-permute-start(bf16[288,256]{1,0:T(8,128)(2,1)S(1)} %get-tuple-element.67), channel_id=1, source_target_pairs={{0,16},{4,20},{8,24},{12,28},{16,0},{20,4},{24,8},{28,12},{1,17},{... | collective-permute-start | bytes 442376 | tf_op jit(solution)/shard_map/ppermute | solution.py:645
  53.3 7.4 %collective-permute-start.13 = (bf16[288,256]{1,0:T(8,128)(2,1)S(1)}, bf16[288,256]{1,0:T(8,128)(2,1)S(1)}, u32[]{:S(2)}, u32[]{:S(2)}) collective-permute-start(bf16[288,256]{1,0:T(8,128)(2,1)S(1)} %get-tuple-element.68), channel_id=1, source_target_pairs={{0,24},{4,28},{8,16},{12,20},{16,8},{20,12},{24,0},{28,4},{1,25},{... | collective-permute-start | bytes 442376 | tf_op jit(solution)/shard_map/ppermute | solution.py:645
  61.4 7.8 %collective-permute-start.14 = (bf16[128,256]{1,0:T(8,128)(2,1)S(1)}, bf16[128,256]{1,0:T(8,128)(2,1)S(1)}, u32[]{:S(2)}, u32[]{:S(2)}) collective-permute-start(bf16[128,256]{1,0:T(8,128)(2,1)S(1)} %get-tuple-element.70), channel_id=1, source_target_pairs={{0,1},{1,0},{2,3},{3,2},{4,5},{5,4},{6,7},{7,6},{8,9},{9,8},{10,11... | collective-permute-start | bytes 196616 | tf_op jit(solution)/shard_map/ppermute | solution.py:648
  61.5 7.7 %collective-permute-start.15 = (bf16[128,256]{1,0:T(8,128)(2,1)S(1)}, bf16[128,256]{1,0:T(8,128)(2,1)S(1)}, u32[]{:S(2)}, u32[]{:S(2)}) collective-permute-start(bf16[128,256]{1,0:T(8,128)(2,1)S(1)} %get-tuple-element.71), channel_id=1, source_target_pairs={{0,2},{1,3},{2,0},{3,1},{4,6},{5,7},{6,4},{7,5},{8,10},{9,11},{10,... | collective-permute-start | bytes 196616 | tf_op jit(solution)/shard_map/ppermute | solution.py:648
  64.0 6.1 %collective-permute-start.16 = (bf16[128,256]{1,0:T(8,128)(2,1)S(1)}, bf16[128,256]{1,0:T(8,128)(2,1)S(1)}, u32[]{:S(2)}, u32[]{:S(2)}) collective-permute-start(bf16[128,256]{1,0:T(8,128)(2,1)S(1)} %get-tuple-element.72), channel_id=1, source_target_pairs={{0,3},{1,2},{2,1},{3,0},{4,7},{5,6},{6,5},{7,4},{8,11},{9,10},{10,... | collective-permute-start | bytes 196616 | tf_op jit(solution)/shard_map/ppermute | solution.py:648
  65.9 16.5 %all-to-all-start.1 = ((bf16[32,24,128]{2,1,0:T(8,128)(2,1)}), bf16[32,24,128]{2,1,0:T(8,128)(2,1)S(1)}, u32[]{:S(2)}, u32[]{:S(2)}) async-start(bf16[32,24,128]{2,1,0:T(8,128)(2,1)} %get-tuple-element.61), calls=%async_computation.1 | async-start | bytes 393216 | tf_op jit(solution)/shard_map/all_to_all | solution.py:652
  (3 other events, 2.6 us)

commit v3 on v2

--- a/solution.py
+++ b/solution.py
@@ -11,6 +11,8 @@
 DILATION_STEP = 6
 GROUP = 8
 CHIPS = 4
+JOIN_COST = 1 << 30
+DEPTHWISE_COST = 1 << 31
 SLOTS = 3
 
 tanh_coef = 0.7978845608
@@ -266,7 +268,8 @@
     )(cotangent, depth)
 
 
-def place_output_kernel(plan, tiles_ref, out_ref):
+def place_output_kernel(plan, tiles_ref, out_ref, token_ref):
+    token_ref[...] = jnp.zeros_like(token_ref)
     chosen = tile_selector(plan)
     halves = []
     for parity in range(2):
@@ -288,9 +291,12 @@
 def place_output(plan, tiles):
     return pl.pallas_call(
         functools.partial(place_output_kernel, plan),
-        out_shape=jax.ShapeDtypeStruct((plan.rows, plan.part, plan.cols), bf16),
+        out_shape=[
+            jax.ShapeDtypeStruct((plan.rows, plan.part, plan.cols), bf16),
+            jax.ShapeDtypeStruct((8, 128), f32),
+        ],
         in_specs=[VMEM],
-        out_specs=VMEM,
+        out_specs=[VMEM] * 2,
         compiler_params=pltpu.CompilerParams(vmem_limit_bytes=16 << 20),
         name="place_output",
     )(tiles)
@@ -304,42 +310,35 @@
     )
 
 
-def main_kernel(plan, scale, halo, mask_ref, cotangent_ref, *refs):
-    branches, width, chans = plan.branches, plan.width, plan.chans
+class Copies:
+    def __init__(self, sems):
+        self.sems, self.all = sems, []
+
+    def start(self, source, target):
+        copy = pltpu.make_async_copy(source, target, self.sems.at[len(self.all)])
+        copy.start()
+        self.all.append(copy)
+
+    def wait(self):
+        for copy in self.all:
+            copy.wait()
+        self.all = []
+
+
+def depthwise_kernel(plan, halo, mask_ref, tiles_ref, *refs):
     piece_refs, refs = refs[:CHIPS], refs[CHIPS:]
     halo_refs, refs = (refs[:2], refs[2:]) if halo else ((), refs)
-    (point_ref, joining_ref), refs = refs[:2], refs[2:]
-    mine_refs, refs = refs[:branches - 1], refs[branches - 1:]
-    other_refs, refs = refs[:branches - 1], refs[branches - 1:]
-    output_ref, keep_ref, send_ref, grad_pre_ref, point, spread = refs[:6]
-    pieces, halo_pieces, dw_out, joining, branch_out, slope, joined, sorted_rows, grads, sems = refs[6:]
-    plane, strip, chip, core = whereabouts()
-    slots, _ = slots_of(mask_ref, branches)
-
-    copies = []
-
-    def fetch(source, target):
-        copy = pltpu.make_async_copy(source, target, sems.at[len(copies)])
-        copy.start()
-        copies.append(copy)
-
+    dw_out, spread, cotangent_ref, order_ref, token, pieces, halo_pieces, sorted_rows, sems = refs
+    token[...] = jnp.zeros_like(token)
+    plane, _, chip, core = whereabouts()
+    copies = Copies(sems)
     for hop in range(CHIPS):
         for flip in range(2):
-            fetch(
+            copies.start(
                 piece_refs[hop].at[pl.ds(flip * plan.piece, plan.piece)], pieces.at[2 * (chip ^ hop) + (core ^ flip)]
             )
     for place, ref in enumerate(halo_refs):
-        fetch(ref, halo_pieces.at[place])
-    early = len(copies)
-    fetch(point_ref.at[0], point.at[plane])
-    fetch(joining_ref, joining.at[plane])
-    half_point, half_join = chans // 2, width // 2
-    for hop in range(1, branches):
-        for side, ref in ((core, mine_refs[hop - 1]), (1 - core, other_refs[hop - 1])):
-            at_point = pl.multiple_of(side * half_point, half_point)
-            at_join = pl.multiple_of(side * half_join, half_join)
-            fetch(ref.at[pl.ds(0, half_point)], point.at[plane ^ hop, pl.ds(at_point, half_point)])
-            fetch(ref.at[pl.ds(half_point, half_join)], joining.at[plane ^ hop, pl.ds(at_join, half_join)])
+        copies.start(ref, halo_pieces.at[place])
 
     for group in range(plan.lanes):
         edge = jnp.zeros((plan.window, plan.pad, 128), f32)
@@ -363,8 +362,7 @@
                     spread[group, column, row:row + 8] = jnp.where(low_rows, a, pltpu.roll(b, 4, 0))
                     spread[group, column + 1, row:row + 8] = jnp.where(low_rows, pltpu.roll(a, 4, 0), b)
 
-    for copy in copies[:early]:
-        copy.wait()
+    copies.wait()
     for pair in range(CHIPS):
         lay(pieces, 2 * pair, plan.pad + 8 * pair)
     if halo:
@@ -377,7 +375,7 @@
         @pl.when(mask_ref[branch] > 0)
         def _():
             shares = [
-                cotangent_ref[strip * plan.branches + branch].astype(f32)
+                tiles_ref[strip * plan.branches + branch].astype(f32)
                 for strip in range(-(-9 * plan.lanes // plan.depth_rows))
             ]
             for group in range(plan.lanes):
@@ -400,23 +398,87 @@
                     dw_out[branch, pl.ds(at, plan.sub_rows), group * 128:(group + 1) * 128] = total.astype(bf16)
 
     pixel = iota((plan.pixels, 128), 0)
-    column, row = pixel // plan.sub_rows, pixel % plan.sub_rows
+    column = pixel // plan.sub_rows
+    row = pixel - column * plan.sub_rows
     source = (row // 2) * plan.tile + 2 * column + row % 2
     lane = iota(source.shape, 1)
     order = jnp.concatenate([one_hot(source == lane + 128 * k) for k in range(plan.pixels // 128)], 1)
     for pair in range(GROUP):
-        for couple in range(branches // 2):
-            left = cotangent_ref[pair * branches + 2 * couple].astype(f32)[:plan.tile]
-            right = cotangent_ref[pair * branches + 2 * couple + 1].astype(f32)[:plan.tile]
+        for couple in range(plan.branches // 2):
+            left = tiles_ref[pair * plan.branches + 2 * couple].astype(f32)[:plan.tile]
+            right = tiles_ref[pair * plan.branches + 2 * couple + 1].astype(f32)[:plan.tile]
             first, second = swap_halves(left, right)
             lanes = pl.ds(couple * 128, 128)
             sorted_rows[pl.ds(2 * pair * plan.tile, plan.tile), lanes] = first
             sorted_rows[pl.ds((2 * pair + 1) * plan.tile, plan.tile), lanes] = second
-    cotangent = dot(order, sorted_rows[...].astype(bf16))
+    cotangent_ref[...] = dot(order, sorted_rows[...].astype(bf16))
+    order_ref[...] = order
+
+
+def depthwise(plan, mask, tiles, pieces, halos):
+    operands = [mask, tiles, *pieces, *halos]
+    return pl.pallas_call(
+        functools.partial(depthwise_kernel, plan, len(halos) > 0),
+        out_shape=[
+            jax.ShapeDtypeStruct((plan.branches, plan.pixels, plan.chans), bf16),
+            jax.ShapeDtypeStruct((plan.lanes, plan.window + 1, plan.tall, 128), f32),
+            jax.ShapeDtypeStruct((plan.pixels, plan.width), f32),
+            jax.ShapeDtypeStruct((plan.pixels, plan.pixels), bf16),
+            jax.ShapeDtypeStruct((8, 128), f32),
+        ],
+        in_specs=[SMEM, VMEM] + [ANY] * (len(operands) - 2),
+        out_specs=[VMEM] * 5,
+        scratch_shapes=[
+            pltpu.VMEM((GROUP, plan.piece, plan.chans), bf16),
+            pltpu.VMEM((2, 4, plan.piece, plan.chans) if halos else (16, 128), bf16),
+            pltpu.VMEM((plan.pixels, plan.width), f32),
+            pltpu.SemaphoreType.DMA((GROUP + 2,)),
+        ],
+        compiler_params=pltpu.CompilerParams(vmem_limit_bytes=20 << 20),
+        cost_estimate=pl.CostEstimate(flops=DEPTHWISE_COST, bytes_accessed=1 << 10, transcendentals=0),
+        name="depthwise",
+    )(*operands)
+
+
+def join_weights_kernel(plan, point_ref, joining_ref, *refs):
+    mine_refs, other_refs = refs[:plan.branches - 1], refs[plan.branches - 1:2 * plan.branches - 2]
+    point, joining, sems = refs[-3:]
+    plane, _, _, core = whereabouts()
+    copies = Copies(sems)
+    copies.start(point_ref.at[0], point.at[plane])
+    copies.start(joining_ref, joining.at[plane])
+    half_point, half_join = plan.chans // 2, plan.width // 2
+    for hop in range(1, plan.branches):
+        for side, ref in ((core, mine_refs[hop - 1]), (1 - core, other_refs[hop - 1])):
+            at_point = pl.multiple_of(side * half_point, half_point)
+            at_join = pl.multiple_of(side * half_join, half_join)
+            copies.start(ref.at[pl.ds(0, half_point)], point.at[plane ^ hop, pl.ds(at_point, half_point)])
+            copies.start(ref.at[pl.ds(half_point, half_join)], joining.at[plane ^ hop, pl.ds(at_join, half_join)])
+    copies.wait()
+
+
+def join_weights(plan, point, joining, mine, others, token):
+    return pl.pallas_call(
+        functools.partial(join_weights_kernel, plan),
+        out_shape=[
+            jax.ShapeDtypeStruct((plan.branches, plan.chans, plan.width), bf16),
+            jax.ShapeDtypeStruct((plan.branches, plan.width, plan.width), bf16),
+        ],
+        in_specs=[ANY] * (3 + len(mine) + len(others)),
+        out_specs=[VMEM] * 2,
+        scratch_shapes=[pltpu.SemaphoreType.DMA((4 * plan.branches,))],
+        compiler_params=pltpu.CompilerParams(vmem_limit_bytes=8 << 20),
+        cost_estimate=pl.CostEstimate(flops=JOIN_COST, bytes_accessed=1 << 20, transcendentals=0),
+        name="join_weights",
+    )(point, joining, *mine, *others, token)
+
+
+def main_kernel(plan, scale, mask_ref, dw_out, cotangent_ref, order_ref, point, joining,
+                output_ref, keep_ref, send_ref, grad_pre_ref, branch_out, slope, joined, sorted_rows):
+    branches, width, chans = plan.branches, plan.width, plan.chans
+    _, _, _, core = whereabouts()
+    slots, active_count = slots_of(mask_ref, branches)
     joined[...] = jnp.zeros_like(joined)
-    grads[...] = jnp.zeros_like(grads)
-    for copy in copies[early:]:
-        copy.wait()
 
     @pl.loop(0, branches)
     def _(branch):
@@ -429,12 +491,41 @@
             joined[...] += dot(value, joining[branch])
 
     value, derivative = gelu_both(joined[...])
-    grad_joined = (cotangent * derivative).astype(bf16)
-    pixel = iota((plan.pixels, plan.pixels), 1)
-    column, row = pixel // plan.sub_rows, pixel % plan.sub_rows
-    source = (row // 2) * plan.tile + 2 * column + row % 2
-    back = one_hot(source == iota(source.shape, 0))
-    sorted_rows[...] = dot(back, value.astype(bf16))
+    grad_joined = (cotangent_ref[...] * derivative).astype(bf16)
+
+    def store_grads(slot, part, first, rows):
+        at = pl.multiple_of(slot * plan.grad_rows + first, 32)
+        for half in range(2):
+            for kept, ref in ((True, keep_ref), (False, send_ref)):
+                @pl.when((core == half) == kept)
+                def _():
+                    for chip in range(CHIPS):
+                        chunk = half * CHIPS + chip
+                        ref[chip, pl.ds(at, rows)] = part[chunk * rows:(chunk + 1) * rows]
+
+    @pl.loop(0, branches)
+    def _(branch):
+        @pl.when(mask_ref[branch] > 0)
+        def _():
+            slot = pick(slots, branch)
+            joining_part = (dot(branch_out[branch], grad_joined, ((0,), (0,))) * scale).astype(bf16)
+            store_grads(slot, joining_part, 0, plan.join_rows)
+            grad_branch = dot(grad_joined, joining[branch], ((1,), (1,)))
+            grad_pre = (grad_branch * slope[branch]).astype(bf16)
+            grad_pre_ref[branch] = grad_pre
+            point_part = (dot(dw_out[branch], grad_pre, ((0,), (0,))) * scale).astype(bf16)
+            store_grads(slot, point_part, plan.join_rows, plan.point_rows)
+
+    for slot in range(1, SLOTS):
+        @pl.when(slot >= active_count)
+        def _():
+            rows = pl.ds(slot * plan.grad_rows, plan.grad_rows)
+            empty = jnp.zeros((plan.grad_rows, width), bf16)
+            for chip in range(CHIPS):
+                keep_ref[chip, rows] = empty
+                send_ref[chip, rows] = empty
+
+    sorted_rows[...] = dot(order_ref[...], value.astype(bf16), ((0,), (0,)))
     for pair in range(GROUP):
         for couple in range(branches // 2):
             lanes = pl.ds(couple * 128, 128)
@@ -444,65 +535,29 @@
             output_ref[pair * branches + 2 * couple] = first.astype(bf16)
             output_ref[pair * branches + 2 * couple + 1] = second.astype(bf16)
 
-    for branch in range(branches):
-        slot = slots[branch]
-
-        @pl.when(mask_ref[branch] > 0)
-        def _():
-            at = pl.multiple_of(slot * plan.grad_rows, 32)
-            joining_part = (dot(branch_out[branch], grad_joined, ((0,), (0,))) * scale).astype(bf16)
-            for chunk in range(GROUP):
-                grads[chunk, pl.ds(at, plan.join_rows)] = joining_part[chunk * plan.join_rows:(chunk + 1) * plan.join_rows]
-            grad_branch = dot(grad_joined, joining[branch], ((1,), (1,)))
-            grad_pre = (grad_branch * slope[branch]).astype(bf16)
-            grad_pre_ref[branch] = grad_pre
-            at = pl.multiple_of(slot * plan.grad_rows + plan.join_rows, 32)
-            point_part = (dot(dw_out[branch], grad_pre, ((0,), (0,))) * scale).astype(bf16)
-            for chunk in range(GROUP):
-                grads[chunk, pl.ds(at, plan.point_rows)] = point_part[
-                    chunk * plan.point_rows:(chunk + 1) * plan.point_rows
-                ]
-
-    half = GROUP // 2
-    first = pltpu.make_async_copy(grads.at[pl.ds((1 - core) * half, half)], send_ref, sems.at[0])
-    second = pltpu.make_async_copy(grads.at[pl.ds(core * half, half)], keep_ref, sems.at[1])
-    first.start()
-    second.start()
-    first.wait()
-    second.wait()
-
-
-def main_step(plan, scale, mask, tiles, pieces, halos, point, joining, mine, others):
-    operands = [mask, tiles, *pieces, *halos, point, joining, *mine, *others]
+
+def main_step(plan, scale, mask, dw_out, cotangent, order, point, joining):
     half = jax.ShapeDtypeStruct((GROUP // 2, SLOTS * plan.grad_rows, plan.width), bf16)
     return pl.pallas_call(
-        functools.partial(main_kernel, plan, scale, len(halos) > 0),
+        functools.partial(main_kernel, plan, scale),
         out_shape=[
             jax.ShapeDtypeStruct((GROUP * plan.branches, plan.tile, 128), bf16),
             half,
             half,
             jax.ShapeDtypeStruct((plan.branches, plan.pixels, plan.width), bf16),
-            jax.ShapeDtypeStruct((plan.branches, plan.chans, plan.width), bf16),
-            jax.ShapeDtypeStruct((plan.lanes, plan.window + 1, plan.tall, 128), f32),
-        ],
-        in_specs=[SMEM, VMEM] + [ANY] * (len(operands) - 2),
-        out_specs=[VMEM, ANY, ANY, VMEM, VMEM, VMEM],
+        ],
+        in_specs=[SMEM] + [VMEM] * 5,
+        out_specs=[VMEM] * 4,
         scratch_shapes=[
-            pltpu.VMEM((GROUP, plan.piece, plan.chans), bf16),
-            pltpu.VMEM((2, 4, plan.piece, plan.chans) if halos else (16, 128), bf16),
-            pltpu.VMEM((plan.branches, plan.pixels, plan.chans), bf16),
-            pltpu.VMEM((plan.branches, plan.width, plan.width), bf16),
             pltpu.VMEM((plan.branches, plan.pixels, plan.width), bf16),
             pltpu.VMEM((plan.branches, plan.pixels, plan.width), f32),
             pltpu.VMEM((plan.pixels, plan.width), f32),
             pltpu.VMEM((plan.pixels, plan.width), f32),
-            pltpu.VMEM((GROUP, SLOTS * plan.grad_rows, plan.width), bf16),
-            pltpu.SemaphoreType.DMA((GROUP + 2 + 4 * plan.branches,)),
-        ],
-        compiler_params=pltpu.CompilerParams(vmem_limit_bytes=32 << 20),
+        ],
+        compiler_params=pltpu.CompilerParams(vmem_limit_bytes=24 << 20),
         cost_estimate=pl.CostEstimate(flops=1 << 31, bytes_accessed=1 << 24, transcendentals=0),
         name="forward_and_backward",
-    )(*operands)
+    )(mask, dw_out, cotangent, order, point, joining)
 
 
 def depth_grad_kernel(plan, scale, mask_ref, grad_pre_ref, point, spread, out_ref, grad_dw, rows):
@@ -599,17 +654,19 @@
     )(mask, depth, *parts)
 
 
-def place_grads_kernel(plan, mask_ref, chunks_ref, joining_ref, point_ref, depth_ref):
-    plane, _, _, _ = whereabouts()
+def place_grads_kernel(plan, mask_ref, *refs):
+    chunk_refs, (joining_ref, point_ref, depth_ref) = refs[:GROUP], refs[GROUP + 1:]
+    plane, _, chip, core = whereabouts()
     active = pick([mask_ref[branch] for branch in range(plan.branches)], plane) > 0
     rows = plan.grad_rows
     taps = None
-    for chip in range(CHIPS):
-        for core in range(2):
-            chunk = jnp.where(active, chunks_ref[2 * chip + core].astype(f32), 0.0)
-            at = core * CHIPS + chip
-            joining_ref[at * plan.join_rows:(at + 1) * plan.join_rows] = chunk[:plan.join_rows]
-            point_ref[0, at * plan.point_rows:(at + 1) * plan.point_rows] = chunk[plan.join_rows:rows]
+    for flip in range(2):
+        for hop in range(CHIPS):
+            chunk = jnp.where(active, chunk_refs[flip * CHIPS + hop][...].astype(f32), 0.0)
+            at = (core ^ flip) * CHIPS + (chip ^ hop)
+            joining_ref[pl.ds(pl.multiple_of(at * plan.join_rows, plan.join_rows), plan.join_rows)] = chunk[:plan.join_rows]
+            place = pl.multiple_of(at * plan.point_rows, plan.point_rows)
+            point_ref[0, pl.ds(place, plan.point_rows)] = chunk[plan.join_rows:rows]
             taps = chunk[rows:] if taps is None else taps + chunk[rows:]
     for tap in range(9):
         for group in range(plan.lanes):
@@ -617,7 +674,7 @@
             depth_ref[0, tap:tap + 1, group * 128:(group + 1) * 128] = taps[row:row + 1, lane:lane + 128]
 
 
-def place_grads(plan, mask, chunks):
+def place_grads(plan, mask, chunks, token):
     return pl.pallas_call(
         functools.partial(place_grads_kernel, plan),
         out_shape=[
@@ -625,11 +682,11 @@
             jax.ShapeDtypeStruct((1, plan.chans, plan.width), f32),
             jax.ShapeDtypeStruct((1, 9, plan.chans), f32),
         ],
-        in_specs=[SMEM, VMEM],
+        in_specs=[SMEM] + [VMEM] * GROUP + [ANY],
         out_specs=[VMEM] * 3,
         compiler_params=pltpu.CompilerParams(vmem_limit_bytes=16 << 20),
         name="place_grads",
-    )(mask, chunks)
+    )(mask, *chunks, token)
 
 
 def per_device(features, cotangent, depth_weight, point_weight, joining_weight, branch_mask):
@@ -656,13 +713,12 @@
         return tiles.reshape(GROUP * branches, *tiles.shape[2:])
 
     half = halve_weights(plan, point_weight, joining_weight)
-    mine = [flip_branch(half, hop) for hop in range(1, branches)]
+    mine = [flip_branch(half, 1), flip_branch(half, 2)]
+    mine.append(flip_branch(mine[1], 1))
 
     keep, send = spread_features(plan, features)
     joint = join_features(plan, keep, flip_strip(send, 1))
     pieces = [joint[0]] + [flip_strip(joint[hop], 2 * hop) for hop in range(1, CHIPS)]
-    mine, pieces = lax.optimization_barrier((mine, pieces))
-    others = [flip_strip(value, 1) for value in mine]
     halos = []
     if groups is not None:
         strip = lax.axis_index("strip") % GROUP
@@ -673,23 +729,29 @@
         up = [(s + GROUP, s) for s in range(strips - GROUP)]
         halos = [lax.ppermute(near[GROUP - 4:], "strip", down), lax.ppermute(near[:4], "strip", up)]
     tiles = all_to_all(send_cotangent(plan, jnp.swapaxes(cotangent, 1, 2), depth_weight))
-
-    output_tiles, keep, send, grad_pre, points, spread = main_step(
-        plan, scale, branch_mask, tiles, pieces, halos, point_weight, joining_weight, mine, others
+    dw_out, spread, pixel_cotangent, order, token = depthwise(plan, branch_mask, tiles, pieces, halos)
+
+    mine, token = lax.optimization_barrier((mine, token))
+    others = [flip_strip(value, 1) for value in mine]
+    points, joinings = join_weights(plan, point_weight, joining_weight, mine, others, token)
+    output_tiles, keep, send, grad_pre = main_step(
+        plan, scale, branch_mask, dw_out, pixel_cotangent, order, points, joinings
     )
     parts = chip_sum(keep, flip_strip(send, 1))
     parts, output_tiles, grad_pre = lax.optimization_barrier((parts, output_tiles, grad_pre))
     parts = [parts[0]] + [flip_strip(parts[hop], 2 * hop) for hop in range(1, CHIPS)]
     taps = depth_grad(plan, scale, branch_mask, grad_pre, points, spread)
-    output = place_output(plan, all_to_all(output_tiles))
+    output, token = place_output(plan, all_to_all(output_tiles))
     shares = plane_sum(plan, branch_mask, taps, parts)
     shares = [shares[0]] + [flip_branch(shares[hop], hop) for hop in range(1, branches)]
     share = sum(value.astype(f32) for value in shares)
     if groups is not None:
         peers = [list(range(s, strips, GROUP)) for s in range(GROUP)]
         share = lax.psum(share, "strip", axis_index_groups=peers)
-    chunks = lax.all_gather(share.astype(bf16), "strip", axis=0, axis_index_groups=groups)
-    joining_total, point_total, depth_total = place_grads(plan, branch_mask, chunks)
+    share = share.astype(bf16)
+    chunks = [share] + [flip_strip(share, 2 * hop) for hop in range(1, CHIPS)]
+    chunks = chunks + [flip_strip(chunk, 1) for chunk in chunks]
+    joining_total, point_total, depth_total = place_grads(plan, branch_mask, chunks, token)
     return (jnp.swapaxes(output, 1, 2), joining_total, point_total, depth_total)
 
 

time: 82.7 us -> 77 us (0.931)
  blocking collectives: 10.1 us -> 0 us
  waiting for transfers between devices: 16 us -> 21.4 us
  starting transfers between devices: 28.1 us -> 30.9 us
  Pallas kernels: 22.8 us -> 20.5 us
  local copies, waits for them, and re-layouts: 5.56 us -> 3.7 us
    all_gather x1 -> x0, blocking collectives: 10.1 us -> none  [per_device(): lax.all_gather(share.astype(bf16), 'strip', axis=0, axis_index_groups=gro...]
    ppermute x11 -> x18, waiting for transfers between devices: 5.15 us -> 10.4 us  [flip_strip(): return lax.ppermute(value, 'strip', [(s, s ^ hop) for s in range(strips)])]
    ppermute x6, starting transfers between devices: 13.4 us -> 8.62 us  [flip_branch(): lax.ppermute(value, 'branch', [(b, b ^ hop) for b in range(branches)])]
    all_to_all x2, starting transfers between devices: 6.13 us -> 10.3 us  [all_to_all(): return lax.all_to_all(tiles, ('strip', 'branch'), 0, 0, tiled=True)]
    ppermute x11 -> x18, starting transfers between devices: 8.56 us -> 12 us  [flip_strip(): return lax.ppermute(value, 'strip', [(s, s ^ hop) for s in range(strips)])]
    unnamed x17 -> x13, local copies, waits for them, and re-layouts: 5.56 us -> 3.7 us
    pallas_call x1, Pallas kernels: 4.88 us -> 3.47 us  [depth_grad(): pl.pallas_call(functools.partial(depth_grad_kernel, plan, scale), out_sha...]
    pallas_call x2 -> x4, Pallas kernels: 13.5 us -> 12.6 us  [the longest x1 5.18 us: main_step(): pl.pallas_call(functools.partial(main_kernel, plan, scale), out_shape=[ja...]
  transfers between devices with their start and end apart: 19 -> 26, of which waited for: 7 -> 12; matrix products, arithmetic and copies ran while one was open for 1% -> 0% of each run, Pallas kernels for 9% -> 13%
where the time goes in v3:
time: 77 us; the launch traced here: 77.3 us
  starting transfers between devices  30.9 us (40%)
  waiting for transfers between devices  21.4 us (28%)
  Pallas kernels  20.5 us (27%)
  local copies, waits for them, and re-layouts  3.7 us (5%)
  between operations  0.82 us (1%)
    ppermute x18, starting transfers between devices, flip_strip(): return lax.ppermute(value, 'strip', [(s, s ^ hop) for s in range(strips)])  12 us
    ppermute x18, waiting for transfers between devices, flip_strip(): return lax.ppermute(value, 'strip', [(s, s ^ hop) for s in range(strips)])  10.4 us
    ppermute x6, waiting for transfers between devices, flip_branch(): lax.ppermute(value, 'branch', [(b, b ^ hop) for b in range(branches)])  10.3 us
    all_to_all x2, starting transfers between devices, all_to_all(): return lax.all_to_all(tiles, ('strip', 'branch'), 0, 0, tiled=True)  10.3 us
    ppermute x6, starting transfers between devices, flip_branch(): lax.ppermute(value, 'branch', [(b, b ^ hop) for b in range(branches)])  8.62 us
    pallas_call x1, Pallas kernels, main_step(): pl.pallas_call(functools.partial(main_kernel, plan, scale), out_shape=[ja...  5.18 us
    pallas_call x1, Pallas kernels, depthwise(): pl.pallas_call(functools.partial(depthwise_kernel, plan, len(halos) > 0),...  4.47 us
    unnamed x13, local copies, waits for them, and re-layouts  3.7 us
  transfers between devices with their start and end apart: 26, of which 12 were waited for; matrix products, arithmetic and copies ran while one was open for 0% of the time, Pallas kernels for 13%

profile of v3, /device:TPU:0, one launch (start us, length us, event | category | flops | bytes accessed | tf_op | source)
XLA Modules:
  0.0 77.3 jit_solution(13860748046322829334)
XLA Ops:
  2.3 1.2 %send_cotangent.1 = bf16[32,32,128]{2,1,0:T(8,128)(2,1)} custom-call(bf16[8,64,192]{2,1,0:T(8,128)(2,1)S(1)} %bitcast.2, bf16[1,9,512]{2,1,0:T(8,128)(2,1)S(1)} %copy-done.4), custom_call_target="tpu_custom_call" | custom-call | flops 1 | bytes 1 | tf_op jit(solution)/shard_map/send_cotangent/pallas_call | solution.py:254
  3.5 7.3 %all-to-all-start = ((bf16[32,32,128]{2,1,0:T(8,128)(2,1)}), bf16[32,32,128]{2,1,0:T(8,128)(2,1)S(1)}, u32[]{:S(2)}, u32[]{:S(2)}) async-start(bf16[32,32,128]{2,1,0:T(8,128)(2,1)} %send_cotangent.1), calls=%async_computation | async-start | bytes 524288 | tf_op jit(solution)/shard_map/all_to_all | solution.py:709
  10.8 1.4 %copy-done = bf16[8,192,512]{2,1,0:T(8,128)(2,1)S(1)} copy-done((bf16[8,192,512]{2,1,0:T(8,128)(2,1)S(1)}, bf16[8,192,512]{2,1,0:T(8,128)(2,1)}, u32[]{:S(2)}) %copy-start) | copy-done | bytes 1572888
  13.5 2.7 %collective-permute-start.5 = (bf16[384,256]{1,0:T(8,128)(2,1)S(1)}, bf16[384,256]{1,0:T(8,128)(2,1)S(1)}, u32[]{:S(2)}, u32[]{:S(2)}) collective-permute-start(bf16[384,256]{1,0:T(8,128)(2,1)S(1)} %halve_weights.1), channel_id=1, source_target_pairs={{0,2},{1,3},{2,0},{3,1},{4,6},{5,7},{6,4},{7,5},{8,10},{9,11},{10,... | collective-permute-start | bytes 589832 | tf_op jit(solution)/shard_map/ppermute | solution.py:705
  16.2 1.5 %collective-permute-start.1 = (bf16[160,512]{1,0:T(8,128)(2,1)S(1)}, bf16[160,512]{1,0:T(8,128)(2,1)S(1)}, u32[]{:S(2)}, u32[]{:S(2)}) collective-permute-start(bf16[160,512]{1,0:T(8,128)(2,1)S(1)} %get-tuple-element.47), channel_id=1, source_target_pairs={{0,8},{4,12},{8,0},{12,4},{16,24},{20,28},{24,16},{28,20},{1,9},{5... | collective-permute-start | bytes 491528 | tf_op jit(solution)/shard_map/ppermute | solution.py:702
  17.7 1.5 %collective-permute-start.2 = (bf16[160,512]{1,0:T(8,128)(2,1)S(1)}, bf16[160,512]{1,0:T(8,128)(2,1)S(1)}, u32[]{:S(2)}, u32[]{:S(2)}) collective-permute-start(bf16[160,512]{1,0:T(8,128)(2,1)S(1)} %get-tuple-element.48), channel_id=1, source_target_pairs={{0,16},{4,20},{8,24},{12,28},{16,0},{20,4},{24,8},{28,12},{1,17},{... | collective-permute-start | bytes 491528 | tf_op jit(solution)/shard_map/ppermute | solution.py:702
  19.8 1.5 %collective-permute-start.4 = (bf16[384,256]{1,0:T(8,128)(2,1)S(1)}, bf16[384,256]{1,0:T(8,128)(2,1)S(1)}, u32[]{:S(2)}, u32[]{:S(2)}) collective-permute-start(bf16[384,256]{1,0:T(8,128)(2,1)S(1)} %halve_weights.1), channel_id=1, source_target_pairs={{0,1},{1,0},{2,3},{3,2},{4,5},{5,4},{6,7},{7,6},{8,9},{9,8},{10,11... | collective-permute-start | bytes 589832 | tf_op jit(solution)/shard_map/ppermute | solution.py:705
  21.3 7.4 %collective-permute-done.5.refs_1_ = bf16[384,256]{1,0:T(8,128)(2,1)S(1)} collective-permute-done((bf16[384,256]{1,0:T(8,128)(2,1)S(1)}, bf16[384,256]{1,0:T(8,128)(2,1)S(1)}, u32[]{:S(2)}, u32[]{:S(2)}) %collective-permute-start.5) | collective-permute-done | bytes 196640 | tf_op jit(solution)/shard_map/ppermute | solution.py:705
  28.7 4.5 %depthwise.1 = (bf16[4,384,512]{2,1,0:T(8,128)(2,1)S(1)}, f32[4,21,64,128]{3,2,1,0:T(8,128)S(1)}, f32[384,256]{1,0:T(8,128)S(1)}, bf16[384,384]{1,0:T(8,128)(2,1)S(1)}, f32[8,128]{1,0:T(8,128)S(1)}) custom-call(s32[4]{0:T(128)S(1)} %copy-done.5, bf16[32,32,128]{2,1,0:T(8,128)(2,1)S(1)} %all-to-all-done.tiles_ref, ...), custom_call_target="tpu_custom_call" | custom-call | flops 2147483648 | bytes 1024 | tf_op jit(solution)/shard_map/depthwise/pallas_call | solution.py:420
  33.2 1.8 %collective-permute-done.6.refs_2_ = bf16[384,256]{1,0:T(8,128)(2,1)S(1)} collective-permute-done((bf16[384,256]{1,0:T(8,128)(2,1)S(1)}, bf16[384,256]{1,0:T(8,128)(2,1)S(1)}, u32[]{:S(2)}, u32[]{:S(2)}) %collective-permute-start.6) | collective-permute-done | bytes 196640 | tf_op jit(solution)/shard_map/ppermute | solution.py:705
  37.1 1.9 %join_weights.1 = (bf16[4,512,256]{2,1,0:T(8,128)(2,1)S(1)}, bf16[4,256,256]{2,1,0:T(8,128)(2,1)S(1)}) custom-call(bf16[1,512,256]{2,1,0:T(8,128)(2,1)S(1)} %copy-done.2, bf16[256,256]{1,0:T(8,128)(2,1)S(1)} %copy-done.3, bf16[384,256]{1,0:T(8,128)(2,1)S(1)} %collective-permute-done.4.refs_0_, bf16[384,256]{1,0:T(8,128)(2,1)S(1)} %collective-permute-done.5.refs_1_, ...), custom_call_target="tpu_custom_call" | custom-call | flops 1073741824 | bytes 1048576 | tf_op jit(solution)/shard_map/join_weights/pallas_call | solution.py:461
  39.0 5.2 %forward_and_backward.1 = (bf16[32,24,128]{2,1,0:T(8,128)(2,1)}, bf16[4,288,256]{2,1,0:T(8,128)(2,1)S(1)}, bf16[4,288,256]{2,1,0:T(8,128)(2,1)S(1)}, bf16[4,384,256]{2,1,0:T(8,128)(2,1)S(1)}) custom-call(s32[4]{0:T(128)S(1)} %copy-done.5, bf16[4,384,512]{2,1,0:T(8,128)(2,1)S(1)} %get-tuple-element.50.dw_out, f32[384,256]{1,0:T(8,128)S(1)} %get-tuple-element.51.cotangent_ref, ...), custom_call_target="tpu_custom_call" | custom-call | flops 2147483648 | bytes 16777216 | tf_op jit(solution)/shard_map/forward_and_backward/pallas_call | solution.py:541
  44.4 1.8 %collective-permute-done.10.other_ref = bf16[4,288,256]{2,1,0:T(8,128)(2,1)S(1)} collective-permute-done((bf16[4,288,256]{2,1,0:T(8,128)(2,1)S(1)}, bf16[4,288,256]{2,1,0:T(8,128)(2,1)S(1)}, u32[]{:S(2)}, u32[]{:S(2)}) %collective-permute-start.10) | collective-permute-done | bytes 589856 | tf_op jit(solution)/shard_map/ppermute | solution.py:702
  46.3 1.5 %collective-permute-start.11 = (bf16[288,256]{1,0:T(8,128)(2,1)S(1)}, bf16[288,256]{1,0:T(8,128)(2,1)S(1)}, u32[]{:S(2)}, u32[]{:S(2)}) collective-permute-start(bf16[288,256]{1,0:T(8,128)(2,1)S(1)} %get-tuple-element.73), channel_id=1, source_target_pairs={{0,8},{4,12},{8,0},{12,4},{16,24},{20,28},{24,16},{28,20},{1,9},{5... | collective-permute-start | bytes 442376 | tf_op jit(solution)/shard_map/ppermute | solution.py:702
  47.8 1.5 %collective-permute-start.12 = (bf16[288,256]{1,0:T(8,128)(2,1)S(1)}, bf16[288,256]{1,0:T(8,128)(2,1)S(1)}, u32[]{:S(2)}, u32[]{:S(2)}) collective-permute-start(bf16[288,256]{1,0:T(8,128)(2,1)S(1)} %get-tuple-element.74), channel_id=1, source_target_pairs={{0,16},{4,20},{8,24},{12,28},{16,0},{20,4},{24,8},{28,12},{1,17},{... | collective-permute-start | bytes 442376 | tf_op jit(solution)/shard_map/ppermute | solution.py:702
  49.8 3.5 %depth_grad.1.depth_ref = bf16[3,32,256]{2,1,0:T(8,128)(2,1)S(1)} custom-call(s32[4]{0:T(128)S(1)} %copy-done.5, bf16[4,384,256]{2,1,0:T(8,128)(2,1)S(1)} %get-tuple-element.70.grad_pre_ref, bf16[4,512,256]{2,1,0:T(8,128)(2,1)S(1)} %get-tuple-element.58.point, f32[4,21,64,128]{3,2,1,0:T(8,128)S(1)} %get-tuple-element.71.spread), custom_call_target="tpu_custom_call" | custom-call | flops 67108864 | bytes 16777216 | tf_op jit(solution)/shard_map/depth_grad/pallas_call | solution.py:598
  53.3 3.4 %collective-permute-done.12.refs_2_ = bf16[288,256]{1,0:T(8,128)(2,1)S(1)} collective-permute-done((bf16[288,256]{1,0:T(8,128)(2,1)S(1)}, bf16[288,256]{1,0:T(8,128)(2,1)S(1)}, u32[]{:S(2)}, u32[]{:S(2)}) %collective-permute-start.12) | collective-permute-done | bytes 147488 | tf_op jit(solution)/shard_map/ppermute | solution.py:702
  57.7 2.0 %collective-permute-start.15 = (bf16[128,256]{1,0:T(8,128)(2,1)S(1)}, bf16[128,256]{1,0:T(8,128)(2,1)S(1)}, u32[]{:S(2)}, u32[]{:S(2)}) collective-permute-start(bf16[128,256]{1,0:T(8,128)(2,1)S(1)} %get-tuple-element.78), channel_id=1, source_target_pairs={{0,2},{1,3},{2,0},{3,1},{4,6},{5,7},{6,4},{7,5},{8,10},{9,11},{10,... | collective-permute-start | bytes 196616 | tf_op jit(solution)/shard_map/ppermute | solution.py:705
  59.7 2.1 %collective-permute-start.16 = (bf16[128,256]{1,0:T(8,128)(2,1)S(1)}, bf16[128,256]{1,0:T(8,128)(2,1)S(1)}, u32[]{:S(2)}, u32[]{:S(2)}) collective-permute-start(bf16[128,256]{1,0:T(8,128)(2,1)S(1)} %get-tuple-element.79), channel_id=1, source_target_pairs={{0,3},{1,2},{2,1},{3,0},{4,7},{5,6},{6,5},{7,4},{8,11},{9,10},{10,... | collective-permute-start | bytes 196616 | tf_op jit(solution)/shard_map/ppermute | solution.py:705
  61.8 3.0 %all-to-all-start.1 = ((bf16[32,24,128]{2,1,0:T(8,128)(2,1)}), bf16[32,24,128]{2,1,0:T(8,128)(2,1)S(1)}, u32[]{:S(2)}, u32[]{:S(2)}) async-start(bf16[32,24,128]{2,1,0:T(8,128)(2,1)} %get-tuple-element.68), calls=%async_computation.1 | async-start | bytes 393216 | tf_op jit(solution)/shard_map/all_to_all | solution.py:709
  65.9 1.7 %collective-permute-start.19 = (bf16[128,256]{1,0:T(8,128)(2,1)S(1)}, bf16[128,256]{1,0:T(8,128)(2,1)S(1)}, u32[]{:S(2)}, u32[]{:S(2)}) collective-permute-start(bf16[128,256]{1,0:T(8,128)(2,1)S(1)} %add_convert_fusion.refs_0_), channel_id=1, source_target_pairs={{0,24},{4,28},{8,16},{12,20},{16,8},{20,12},{24,0},{28,4},{1,25},{... | collective-permute-start | bytes 196616 | tf_op jit(solution)/shard_map/ppermute | solution.py:702
  69.5 2.1 %collective-permute-done.19.refs_3_ = bf16[128,256]{1,0:T(8,128)(2,1)S(1)} collective-permute-done((bf16[128,256]{1,0:T(8,128)(2,1)S(1)}, bf16[128,256]{1,0:T(8,128)(2,1)S(1)}, u32[]{:S(2)}, u32[]{:S(2)}) %collective-permute-start.19) | collective-permute-done | bytes 65568 | tf_op jit(solution)/shard_map/ppermute | solution.py:702
  71.6 1.4 %collective-permute-done.18.refs_2_ = bf16[128,256]{1,0:T(8,128)(2,1)S(1)} collective-permute-done((bf16[128,256]{1,0:T(8,128)(2,1)S(1)}, bf16[128,256]{1,0:T(8,128)(2,1)S(1)}, u32[]{:S(2)}, u32[]{:S(2)}) %collective-permute-start.18) | collective-permute-done | bytes 65568 | tf_op jit(solution)/shard_map/ppermute | solution.py:702
  75.2 1.5 %place_grads.1 = (f32[256,256]{1,0:T(8,128)}, f32[1,512,256]{2,1,0:T(8,128)}, f32[1,9,512]{2,1,0:T(8,128)S(1)}) custom-call(s32[4]{0:T(128)S(1)} %copy-done.5, bf16[128,256]{1,0:T(8,128)(2,1)S(1)} %add_convert_fusion.refs_0_, bf16[128,256]{1,0:T(8,128)(2,1)S(1)} %collective-permute-done.17.refs_1_, bf16[128,256]{1,0:T(8,128)(2,1)S(1)} %collective-permute-done.18.refs_2_, ...), custom_call_target="tpu_custom_call" | custom-call | tf_op jit(solution)/shard_map/place_grads/pallas_call | solution.py:678
  (54 shorter events, 13.2 us)
Async XLA Ops:
  3.5 25.2 %all-to-all-start = ((bf16[32,32,128]{2,1,0:T(8,128)(2,1)}), bf16[32,32,128]{2,1,0:T(8,128)(2,1)S(1)}, u32[]{:S(2)}, u32[]{:S(2)}) async-start(bf16[32,32,128]{2,1,0:T(8,128)(2,1)} %send_cotangent.1), calls=%async_computation | async-start | bytes 524288 | tf_op jit(solution)/shard_map/all_to_all | solution.py:709
  12.9 3.2 %collective-permute-start = (bf16[4,80,512]{2,1,0:T(8,128)(2,1)S(1)}, bf16[4,80,512]{2,1,0:T(8,128)(2,1)S(1)}, u32[]{:S(2)}, u32[]{:S(2)}) collective-permute-start(bf16[4,80,512]{2,1,0:T(8,128)(2,1)S(1)} %get-tuple-element.45), channel_id=1, source_target_pairs={{0,4},{4,0},{8,12},{12,8},{16,20},{20,16},{24,28},{28,24},{1,5},{5... | collective-permute-start | bytes 983048 | tf_op jit(solution)/shard_map/ppermute | solution.py:702
  13.5 15.2 %collective-permute-start.5 = (bf16[384,256]{1,0:T(8,128)(2,1)S(1)}, bf16[384,256]{1,0:T(8,128)(2,1)S(1)}, u32[]{:S(2)}, u32[]{:S(2)}) collective-permute-start(bf16[384,256]{1,0:T(8,128)(2,1)S(1)} %halve_weights.1), channel_id=1, source_target_pairs={{0,2},{1,3},{2,0},{3,1},{4,6},{5,7},{6,4},{7,5},{8,10},{9,11},{10,... | collective-permute-start | bytes 589832 | tf_op jit(solution)/shard_map/ppermute | solution.py:705
  16.2 12.5 %collective-permute-start.1 = (bf16[160,512]{1,0:T(8,128)(2,1)S(1)}, bf16[160,512]{1,0:T(8,128)(2,1)S(1)}, u32[]{:S(2)}, u32[]{:S(2)}) collective-permute-start(bf16[160,512]{1,0:T(8,128)(2,1)S(1)} %get-tuple-element.47), channel_id=1, source_target_pairs={{0,8},{4,12},{8,0},{12,4},{16,24},{20,28},{24,16},{28,20},{1,9},{5... | collective-permute-start | bytes 491528 | tf_op jit(solution)/shard_map/ppermute | solution.py:702
  17.7 11.0 %collective-permute-start.2 = (bf16[160,512]{1,0:T(8,128)(2,1)S(1)}, bf16[160,512]{1,0:T(8,128)(2,1)S(1)}, u32[]{:S(2)}, u32[]{:S(2)}) collective-permute-start(bf16[160,512]{1,0:T(8,128)(2,1)S(1)} %get-tuple-element.48), channel_id=1, source_target_pairs={{0,16},{4,20},{8,24},{12,28},{16,0},{20,4},{24,8},{28,12},{1,17},{... | collective-permute-start | bytes 491528 | tf_op jit(solution)/shard_map/ppermute | solution.py:702
  19.2 9.5 %collective-permute-start.3 = (bf16[160,512]{1,0:T(8,128)(2,1)S(1)}, bf16[160,512]{1,0:T(8,128)(2,1)S(1)}, u32[]{:S(2)}, u32[]{:S(2)}) collective-permute-start(bf16[160,512]{1,0:T(8,128)(2,1)S(1)} %get-tuple-element.49), channel_id=1, source_target_pairs={{0,24},{4,28},{8,16},{12,20},{16,8},{20,12},{24,0},{28,4},{1,25},{... | collective-permute-start | bytes 491528 | tf_op jit(solution)/shard_map/ppermute | solution.py:702
  19.8 13.4 %collective-permute-start.4 = (bf16[384,256]{1,0:T(8,128)(2,1)S(1)}, bf16[384,256]{1,0:T(8,128)(2,1)S(1)}, u32[]{:S(2)}, u32[]{:S(2)}) collective-permute-start(bf16[384,256]{1,0:T(8,128)(2,1)S(1)} %halve_weights.1), channel_id=1, source_target_pairs={{0,1},{1,0},{2,3},{3,2},{4,5},{5,4},{6,7},{7,6},{8,9},{9,8},{10,11... | collective-permute-start | bytes 589832 | tf_op jit(solution)/shard_map/ppermute | solution.py:705
  28.7 6.4 %collective-permute-start.6 = (bf16[384,256]{1,0:T(8,128)(2,1)S(1)}, bf16[384,256]{1,0:T(8,128)(2,1)S(1)}, u32[]{:S(2)}, u32[]{:S(2)}) collective-permute-start(bf16[384,256]{1,0:T(8,128)(2,1)S(1)} %collective-permute-done.5.refs_1_), channel_id=1, source_target_pairs={{0,1},{1,0},{2,3},{3,2},{4,5},{5,4},{6,7},{7,6},{8,9},{9,8},{10,11... | collective-permute-start | bytes 589832 | tf_op jit(solution)/shard_map/ppermute | solution.py:705
  35.1 1.7 %collective-permute-start.8 = (bf16[384,256]{1,0:T(8,128)(2,1)S(1)}, bf16[384,256]{1,0:T(8,128)(2,1)S(1)}, u32[]{:S(2)}, u32[]{:S(2)}) collective-permute-start(bf16[384,256]{1,0:T(8,128)(2,1)S(1)} %collective-permute-done.5.refs_1_), channel_id=1, source_target_pairs={{0,4},{4,0},{8,12},{12,8},{16,20},{20,16},{24,28},{28,24},{1,5},{5... | collective-permute-start | bytes 589832 | tf_op jit(solution)/shard_map/ppermute | solution.py:702
  44.1 2.0 %collective-permute-start.10 = (bf16[4,288,256]{2,1,0:T(8,128)(2,1)S(1)}, bf16[4,288,256]{2,1,0:T(8,128)(2,1)S(1)}, u32[]{:S(2)}, u32[]{:S(2)}) collective-permute-start(bf16[4,288,256]{2,1,0:T(8,128)(2,1)S(1)} %get-tuple-element.61), channel_id=1, source_target_pairs={{0,4},{4,0},{8,12},{12,8},{16,20},{20,16},{24,28},{28,24},{1,5},{5... | collective-permute-start | bytes 1769480 | tf_op jit(solution)/shard_map/ppermute | solution.py:702
  46.3 7.0 %collective-permute-start.11 = (bf16[288,256]{1,0:T(8,128)(2,1)S(1)}, bf16[288,256]{1,0:T(8,128)(2,1)S(1)}, u32[]{:S(2)}, u32[]{:S(2)}) collective-permute-start(bf16[288,256]{1,0:T(8,128)(2,1)S(1)} %get-tuple-element.73), channel_id=1, source_target_pairs={{0,8},{4,12},{8,0},{12,4},{16,24},{20,28},{24,16},{28,20},{1,9},{5... | collective-permute-start | bytes 442376 | tf_op jit(solution)/shard_map/ppermute | solution.py:702
  47.8 8.9 %collective-permute-start.12 = (bf16[288,256]{1,0:T(8,128)(2,1)S(1)}, bf16[288,256]{1,0:T(8,128)(2,1)S(1)}, u32[]{:S(2)}, u32[]{:S(2)}) collective-permute-start(bf16[288,256]{1,0:T(8,128)(2,1)S(1)} %get-tuple-element.74), channel_id=1, source_target_pairs={{0,16},{4,20},{8,24},{12,28},{16,0},{20,4},{24,8},{28,12},{1,17},{... | collective-permute-start | bytes 442376 | tf_op jit(solution)/shard_map/ppermute | solution.py:702
  49.3 7.4 %collective-permute-start.13 = (bf16[288,256]{1,0:T(8,128)(2,1)S(1)}, bf16[288,256]{1,0:T(8,128)(2,1)S(1)}, u32[]{:S(2)}, u32[]{:S(2)}) collective-permute-start(bf16[288,256]{1,0:T(8,128)(2,1)S(1)} %get-tuple-element.75), channel_id=1, source_target_pairs={{0,24},{4,28},{8,16},{12,20},{16,8},{20,12},{24,0},{28,4},{1,25},{... | collective-permute-start | bytes 442376 | tf_op jit(solution)/shard_map/ppermute | solution.py:702
  57.3 7.5 %collective-permute-start.14 = (bf16[128,256]{1,0:T(8,128)(2,1)S(1)}, bf16[128,256]{1,0:T(8,128)(2,1)S(1)}, u32[]{:S(2)}, u32[]{:S(2)}) collective-permute-start(bf16[128,256]{1,0:T(8,128)(2,1)S(1)} %get-tuple-element.77), channel_id=1, source_target_pairs={{0,1},{1,0},{2,3},{3,2},{4,5},{5,4},{6,7},{7,6},{8,9},{9,8},{10,11... | collective-permute-start | bytes 196616 | tf_op jit(solution)/shard_map/ppermute | solution.py:705
  57.7 7.1 %collective-permute-start.15 = (bf16[128,256]{1,0:T(8,128)(2,1)S(1)}, bf16[128,256]{1,0:T(8,128)(2,1)S(1)}, u32[]{:S(2)}, u32[]{:S(2)}) collective-permute-start(bf16[128,256]{1,0:T(8,128)(2,1)S(1)} %get-tuple-element.78), channel_id=1, source_target_pairs={{0,2},{1,3},{2,0},{3,1},{4,6},{5,7},{6,4},{7,5},{8,10},{9,11},{10,... | collective-permute-start | bytes 196616 | tf_op jit(solution)/shard_map/ppermute | solution.py:705
  59.7 6.2 %collective-permute-start.16 = (bf16[128,256]{1,0:T(8,128)(2,1)S(1)}, bf16[128,256]{1,0:T(8,128)(2,1)S(1)}, u32[]{:S(2)}, u32[]{:S(2)}) collective-permute-start(bf16[128,256]{1,0:T(8,128)(2,1)S(1)} %get-tuple-element.79), channel_id=1, source_target_pairs={{0,3},{1,2},{2,1},{3,0},{4,7},{5,6},{6,5},{7,4},{8,11},{9,10},{10,... | collective-permute-start | bytes 196616 | tf_op jit(solution)/shard_map/ppermute | solution.py:705
  61.8 12.3 %all-to-all-start.1 = ((bf16[32,24,128]{2,1,0:T(8,128)(2,1)}), bf16[32,24,128]{2,1,0:T(8,128)(2,1)S(1)}, u32[]{:S(2)}, u32[]{:S(2)}) async-start(bf16[32,24,128]{2,1,0:T(8,128)(2,1)} %get-tuple-element.68), calls=%async_computation.1 | async-start | bytes 393216 | tf_op jit(solution)/shard_map/all_to_all | solution.py:709
  65.9 5.7 %collective-permute-start.19 = (bf16[128,256]{1,0:T(8,128)(2,1)S(1)}, bf16[128,256]{1,0:T(8,128)(2,1)S(1)}, u32[]{:S(2)}, u32[]{:S(2)}) collective-permute-start(bf16[128,256]{1,0:T(8,128)(2,1)S(1)} %add_convert_fusion.refs_0_), channel_id=1, source_target_pairs={{0,24},{4,28},{8,16},{12,20},{16,8},{20,12},{24,0},{28,4},{1,25},{... | collective-permute-start | bytes 196616 | tf_op jit(solution)/shard_map/ppermute | solution.py:702
  67.6 5.3 %collective-permute-start.18 = (bf16[128,256]{1,0:T(8,128)(2,1)S(1)}, bf16[128,256]{1,0:T(8,128)(2,1)S(1)}, u32[]{:S(2)}, u32[]{:S(2)}) collective-permute-start(bf16[128,256]{1,0:T(8,128)(2,1)S(1)} %add_convert_fusion.refs_0_), channel_id=1, source_target_pairs={{0,16},{4,20},{8,24},{12,28},{16,0},{20,4},{24,8},{28,12},{1,17},{... | collective-permute-start | bytes 196616 | tf_op jit(solution)/shard_map/ppermute | solution.py:702
  68.6 4.6 %collective-permute-start.17 = (bf16[128,256]{1,0:T(8,128)(2,1)S(1)}, bf16[128,256]{1,0:T(8,128)(2,1)S(1)}, u32[]{:S(2)}, u32[]{:S(2)}) collective-permute-start(bf16[128,256]{1,0:T(8,128)(2,1)S(1)} %add_convert_fusion.refs_0_), channel_id=1, source_target_pairs={{0,8},{4,12},{8,0},{12,4},{16,24},{20,28},{24,16},{28,20},{1,9},{5... | collective-permute-start | bytes 196616 | tf_op jit(solution)/shard_map/ppermute | solution.py:702
  69.5 5.7 %collective-permute-start.20 = (bf16[128,256]{1,0:T(8,128)(2,1)S(1)}, bf16[128,256]{1,0:T(8,128)(2,1)S(1)}, u32[]{:S(2)}, u32[]{:S(2)}) collective-permute-start(bf16[128,256]{1,0:T(8,128)(2,1)S(1)} %add_convert_fusion.refs_0_), channel_id=1, source_target_pairs={{0,4},{4,0},{8,12},{12,8},{16,20},{20,16},{24,28},{28,24},{1,5},{5... | collective-permute-start | bytes 196616 | tf_op jit(solution)/shard_map/ppermute | solution.py:702
  71.6 3.6 %collective-permute-start.23 = (bf16[128,256]{1,0:T(8,128)(2,1)S(1)}, bf16[128,256]{1,0:T(8,128)(2,1)S(1)}, u32[]{:S(2)}, u32[]{:S(2)}) collective-permute-start(bf16[128,256]{1,0:T(8,128)(2,1)S(1)} %collective-permute-done.19.refs_3_), channel_id=1, source_target_pairs={{0,4},{4,0},{8,12},{12,8},{16,20},{20,16},{24,28},{28,24},{1,5},{5... | collective-permute-start | bytes 196616 | tf_op jit(solution)/shard_map/ppermute | solution.py:702
  73.0 2.2 %collective-permute-start.22 = (bf16[128,256]{1,0:T(8,128)(2,1)S(1)}, bf16[128,256]{1,0:T(8,128)(2,1)S(1)}, u32[]{:S(2)}, u32[]{:S(2)}) collective-permute-start(bf16[128,256]{1,0:T(8,128)(2,1)S(1)} %collective-permute-done.18.refs_2_), channel_id=1, source_target_pairs={{0,4},{4,0},{8,12},{12,8},{16,20},{20,16},{24,28},{28,24},{1,5},{5... | collective-permute-start | bytes 196616 | tf_op jit(solution)/shard_map/ppermute | solution.py:702
  73.2 2.0 %collective-permute-start.21 = (bf16[128,256]{1,0:T(8,128)(2,1)S(1)}, bf16[128,256]{1,0:T(8,128)(2,1)S(1)}, u32[]{:S(2)}, u32[]{:S(2)}) collective-permute-start(bf16[128,256]{1,0:T(8,128)(2,1)S(1)} %collective-permute-done.17.refs_1_), channel_id=1, source_target_pairs={{0,4},{4,0},{8,12},{12,8},{16,20},{20,16},{24,28},{28,24},{1,5},{5... | collective-permute-start | bytes 196616 | tf_op jit(solution)/shard_map/ppermute | solution.py:702
  (8 other events, 53.1 us)

commit v4 on v3

--- a/solution.py
+++ b/solution.py
@@ -11,7 +11,6 @@
 DILATION_STEP = 6
 GROUP = 8
 CHIPS = 4
-JOIN_COST = 1 << 30
 DEPTHWISE_COST = 1 << 31
 SLOTS = 3
 
@@ -262,7 +261,7 @@
             pltpu.VMEM((GROUP * plan.depth_rows, 128), f32),
             pltpu.SemaphoreType.DMA((2,)),
         ],
-        compiler_params=pltpu.CompilerParams(vmem_limit_bytes=16 << 20),
+        compiler_params=pltpu.CompilerParams(vmem_limit_bytes=60 << 20),
         cost_estimate=pl.CostEstimate(flops=1, bytes_accessed=1, transcendentals=0),
         name="send_cotangent",
     )(cotangent, depth)
@@ -440,50 +439,42 @@
     )(*operands)
 
 
-def join_weights_kernel(plan, point_ref, joining_ref, *refs):
-    mine_refs, other_refs = refs[:plan.branches - 1], refs[plan.branches - 1:2 * plan.branches - 2]
-    point, joining, sems = refs[-3:]
+def main_kernel(plan, scale, mask_ref, dw_out, cotangent_ref, order_ref, *refs):
+    branches, width, chans = plan.branches, plan.width, plan.chans
+    (point_ref, joining_ref), refs = refs[:2], refs[2:]
+    mine_refs, refs = refs[:branches - 1], refs[branches - 1:]
+    other_refs, refs = refs[:branches - 1], refs[branches:]
+    output_ref, keep_ref, send_ref, grad_pre_ref, point, joining, branch_out, slope, joined, sorted_rows, sems = refs
     plane, _, _, core = whereabouts()
-    copies = Copies(sems)
-    copies.start(point_ref.at[0], point.at[plane])
-    copies.start(joining_ref, joining.at[plane])
-    half_point, half_join = plan.chans // 2, plan.width // 2
-    for hop in range(1, plan.branches):
-        for side, ref in ((core, mine_refs[hop - 1]), (1 - core, other_refs[hop - 1])):
-            at_point = pl.multiple_of(side * half_point, half_point)
-            at_join = pl.multiple_of(side * half_join, half_join)
-            copies.start(ref.at[pl.ds(0, half_point)], point.at[plane ^ hop, pl.ds(at_point, half_point)])
-            copies.start(ref.at[pl.ds(half_point, half_join)], joining.at[plane ^ hop, pl.ds(at_join, half_join)])
-    copies.wait()
-
-
-def join_weights(plan, point, joining, mine, others, token):
-    return pl.pallas_call(
-        functools.partial(join_weights_kernel, plan),
-        out_shape=[
-            jax.ShapeDtypeStruct((plan.branches, plan.chans, plan.width), bf16),
-            jax.ShapeDtypeStruct((plan.branches, plan.width, plan.width), bf16),
-        ],
-        in_specs=[ANY] * (3 + len(mine) + len(others)),
-        out_specs=[VMEM] * 2,
-        scratch_shapes=[pltpu.SemaphoreType.DMA((4 * plan.branches,))],
-        compiler_params=pltpu.CompilerParams(vmem_limit_bytes=8 << 20),
-        cost_estimate=pl.CostEstimate(flops=JOIN_COST, bytes_accessed=1 << 20, transcendentals=0),
-        name="join_weights",
-    )(point, joining, *mine, *others, token)
-
-
-def main_kernel(plan, scale, mask_ref, dw_out, cotangent_ref, order_ref, point, joining,
-                output_ref, keep_ref, send_ref, grad_pre_ref, branch_out, slope, joined, sorted_rows):
-    branches, width, chans = plan.branches, plan.width, plan.chans
-    _, _, _, core = whereabouts()
     slots, active_count = slots_of(mask_ref, branches)
+    half_point, half_join = chans // 2, width // 2
+
+    def fetches(hop):
+        ends = []
+        if hop == 0:
+            ends = [(point_ref.at[0], point.at[plane]), (joining_ref, joining.at[plane])]
+        else:
+            for side, ref in ((core, mine_refs[hop - 1]), (1 - core, other_refs[hop - 1])):
+                at_point = pl.ds(pl.multiple_of(side * half_point, half_point), half_point)
+                at_join = pl.ds(pl.multiple_of(side * half_join, half_join), half_join)
+                ends.append((ref.at[pl.ds(0, half_point)], point.at[plane ^ hop, at_point]))
+                ends.append((ref.at[pl.ds(half_point, half_join)], joining.at[plane ^ hop, at_join]))
+        return [pltpu.make_async_copy(*pair, sems.at[hop, place]) for place, pair in enumerate(ends)]
+
+    for hop in range(branches):
+        @pl.when(mask_ref[plane ^ hop] > 0)
+        def _():
+            for copy in fetches(hop):
+                copy.start()
+
     joined[...] = jnp.zeros_like(joined)
-
-    @pl.loop(0, branches)
-    def _(branch):
+    for hop in range(branches):
+        branch = plane ^ hop
+
         @pl.when(mask_ref[branch] > 0)
         def _():
+            for copy in fetches(hop):
+                copy.wait()
             value, derivative = gelu_both(dot(dw_out[branch], point[branch]))
             value = value.astype(bf16)
             branch_out[branch] = value
@@ -536,7 +527,8 @@
             output_ref[pair * branches + 2 * couple + 1] = second.astype(bf16)
 
 
-def main_step(plan, scale, mask, dw_out, cotangent, order, point, joining):
+def main_step(plan, scale, mask, dw_out, cotangent, order, point, joining, mine, others, token):
+    operands = [mask, dw_out, cotangent, order, point, joining, *mine, *others, token]
     half = jax.ShapeDtypeStruct((GROUP // 2, SLOTS * plan.grad_rows, plan.width), bf16)
     return pl.pallas_call(
         functools.partial(main_kernel, plan, scale),
@@ -545,19 +537,22 @@
             half,
             half,
             jax.ShapeDtypeStruct((plan.branches, plan.pixels, plan.width), bf16),
+            jax.ShapeDtypeStruct((plan.branches, plan.chans, plan.width), bf16),
         ],
-        in_specs=[SMEM] + [VMEM] * 5,
-        out_specs=[VMEM] * 4,
+        in_specs=[SMEM] + [VMEM] * 3 + [ANY] * (len(operands) - 4),
+        out_specs=[VMEM] * 5,
         scratch_shapes=[
+            pltpu.VMEM((plan.branches, plan.width, plan.width), bf16),
             pltpu.VMEM((plan.branches, plan.pixels, plan.width), bf16),
             pltpu.VMEM((plan.branches, plan.pixels, plan.width), f32),
             pltpu.VMEM((plan.pixels, plan.width), f32),
             pltpu.VMEM((plan.pixels, plan.width), f32),
+            pltpu.SemaphoreType.DMA((plan.branches, 4)),
         ],
         compiler_params=pltpu.CompilerParams(vmem_limit_bytes=24 << 20),
         cost_estimate=pl.CostEstimate(flops=1 << 31, bytes_accessed=1 << 24, transcendentals=0),
         name="forward_and_backward",
-    )(mask, dw_out, cotangent, order, point, joining)
+    )(*operands)
 
 
 def depth_grad_kernel(plan, scale, mask_ref, grad_pre_ref, point, spread, out_ref, grad_dw, rows):
@@ -733,9 +728,8 @@
 
     mine, token = lax.optimization_barrier((mine, token))
     others = [flip_strip(value, 1) for value in mine]
-    points, joinings = join_weights(plan, point_weight, joining_weight, mine, others, token)
-    output_tiles, keep, send, grad_pre = main_step(
-        plan, scale, branch_mask, dw_out, pixel_cotangent, order, points, joinings
+    output_tiles, keep, send, grad_pre, points = main_step(
+        plan, scale, branch_mask, dw_out, pixel_cotangent, order, point_weight, joining_weight, mine, others, token
     )
     parts = chip_sum(keep, flip_strip(send, 1))
     parts, output_tiles, grad_pre = lax.optimization_barrier((parts, output_tiles, grad_pre))

time: 77 us -> 77.3 us (level); the launches traced: 77.3 us -> 75.9 us
  local copies, waits for them, and re-layouts: 3.7 us -> 2.04 us
    pallas_call x1 -> x0, Pallas kernels: 1.88 us -> none  [join_weights(): pl.pallas_call(functools.partial(join_weights_kernel, plan), out_shape=[j...]
    unnamed x13 -> x9, local copies, waits for them, and re-layouts: 3.7 us -> 2.04 us
    pallas_call x1, Pallas kernels: 5.18 us -> 6.07 us  [main_step(): pl.pallas_call(functools.partial(main_kernel, plan, scale), out_shape=[ja...]
    pallas_call x1, Pallas kernels: 1.17 us -> 2.03 us  [send_cotangent(): pl.pallas_call(functools.partial(send_cotangent_kernel, plan), out_shape=...]
where the time goes in v4:
time: 77.3 us; the launch traced here: 75.9 us
  starting transfers between devices  31.3 us (40%)
  waiting for transfers between devices  21.4 us (28%)
  Pallas kernels  20.3 us (26%)
  local copies, waits for them, and re-layouts  2.04 us (3%)
  between operations  0.83 us (1%)
    ppermute x18, starting transfers between devices, flip_strip(): return lax.ppermute(value, 'strip', [(s, s ^ hop) for s in range(strips)])  12.1 us
    all_to_all x2, starting transfers between devices, all_to_all(): return lax.all_to_all(tiles, ('strip', 'branch'), 0, 0, tiled=True)  10.6 us
    ppermute x18, waiting for transfers between devices, flip_strip(): return lax.ppermute(value, 'strip', [(s, s ^ hop) for s in range(strips)])  10.5 us
    ppermute x6, waiting for transfers between devices, flip_branch(): lax.ppermute(value, 'branch', [(b, b ^ hop) for b in range(branches)])  10.2 us
    ppermute x6, starting transfers between devices, flip_branch(): lax.ppermute(value, 'branch', [(b, b ^ hop) for b in range(branches)])  8.62 us
    pallas_call x1, Pallas kernels, main_step(): pl.pallas_call(functools.partial(main_kernel, plan, scale), out_shape=[ja...  6.07 us
    pallas_call x1, Pallas kernels, depthwise(): pl.pallas_call(functools.partial(depthwise_kernel, plan, len(halos) > 0),...  4.48 us
    pallas_call x1, Pallas kernels, depth_grad(): pl.pallas_call(functools.partial(depth_grad_kernel, plan, scale), out_sha...  3.45 us
  transfers between devices with their start and end apart: 26, of which 12 were waited for; matrix products, arithmetic and copies ran while one was open for 0% of the time, Pallas kernels for 13%

profile of v4, /device:TPU:0, one launch (start us, length us, event | category | flops | bytes accessed | tf_op | source)
XLA Modules:
  0.0 75.9 jit_solution(6304453444990110441)
XLA Ops:
  0.7 2.0 %send_cotangent.1 = bf16[32,32,128]{2,1,0:T(8,128)(2,1)} custom-call(bf16[8,64,192]{2,1,0:T(8,128)(2,1)} %bitcast.2, bf16[1,9,512]{2,1,0:T(8,128)(2,1)} %depth_ref.1), custom_call_target="tpu_custom_call" | custom-call | flops 1 | bytes 1 | tf_op jit(solution)/shard_map/send_cotangent/pallas_call | solution.py:253
  2.7 7.3 %all-to-all-start = ((bf16[32,32,128]{2,1,0:T(8,128)(2,1)}), bf16[32,32,128]{2,1,0:T(8,128)(2,1)S(1)}, u32[]{:S(2)}, u32[]{:S(2)}) async-start(bf16[32,32,128]{2,1,0:T(8,128)(2,1)} %send_cotangent.1), calls=%async_computation | async-start | bytes 524288 | tf_op jit(solution)/shard_map/all_to_all | solution.py:704
  10.0 1.4 %copy-done = bf16[8,192,512]{2,1,0:T(8,128)(2,1)S(1)} copy-done((bf16[8,192,512]{2,1,0:T(8,128)(2,1)S(1)}, bf16[8,192,512]{2,1,0:T(8,128)(2,1)}, u32[]{:S(2)}) %copy-start) | copy-done | bytes 1572888
  12.7 2.7 %collective-permute-start.5 = (bf16[384,256]{1,0:T(8,128)(2,1)S(1)}, bf16[384,256]{1,0:T(8,128)(2,1)S(1)}, u32[]{:S(2)}, u32[]{:S(2)}) collective-permute-start(bf16[384,256]{1,0:T(8,128)(2,1)S(1)} %halve_weights.1), channel_id=1, source_target_pairs={{0,2},{1,3},{2,0},{3,1},{4,6},{5,7},{6,4},{7,5},{8,10},{9,11},{10,... | collective-permute-start | bytes 589832 | tf_op jit(solution)/shard_map/ppermute | solution.py:700
  15.4 1.5 %collective-permute-start.1 = (bf16[160,512]{1,0:T(8,128)(2,1)S(1)}, bf16[160,512]{1,0:T(8,128)(2,1)S(1)}, u32[]{:S(2)}, u32[]{:S(2)}) collective-permute-start(bf16[160,512]{1,0:T(8,128)(2,1)S(1)} %get-tuple-element.46), channel_id=1, source_target_pairs={{0,8},{4,12},{8,0},{12,4},{16,24},{20,28},{24,16},{28,20},{1,9},{5... | collective-permute-start | bytes 491528 | tf_op jit(solution)/shard_map/ppermute | solution.py:697
  16.9 1.5 %collective-permute-start.2 = (bf16[160,512]{1,0:T(8,128)(2,1)S(1)}, bf16[160,512]{1,0:T(8,128)(2,1)S(1)}, u32[]{:S(2)}, u32[]{:S(2)}) collective-permute-start(bf16[160,512]{1,0:T(8,128)(2,1)S(1)} %get-tuple-element.47), channel_id=1, source_target_pairs={{0,16},{4,20},{8,24},{12,28},{16,0},{20,4},{24,8},{28,12},{1,17},{... | collective-permute-start | bytes 491528 | tf_op jit(solution)/shard_map/ppermute | solution.py:697
  19.0 1.5 %collective-permute-start.4 = (bf16[384,256]{1,0:T(8,128)(2,1)S(1)}, bf16[384,256]{1,0:T(8,128)(2,1)S(1)}, u32[]{:S(2)}, u32[]{:S(2)}) collective-permute-start(bf16[384,256]{1,0:T(8,128)(2,1)S(1)} %halve_weights.1), channel_id=1, source_target_pairs={{0,1},{1,0},{2,3},{3,2},{4,5},{5,4},{6,7},{7,6},{8,9},{9,8},{10,11... | collective-permute-start | bytes 589832 | tf_op jit(solution)/shard_map/ppermute | solution.py:700
  20.5 7.4 %collective-permute-done.5.refs_3_ = bf16[384,256]{1,0:T(8,128)(2,1)S(1)} collective-permute-done((bf16[384,256]{1,0:T(8,128)(2,1)S(1)}, bf16[384,256]{1,0:T(8,128)(2,1)S(1)}, u32[]{:S(2)}, u32[]{:S(2)}) %collective-permute-start.5) | collective-permute-done | bytes 196640 | tf_op jit(solution)/shard_map/ppermute | solution.py:700
  27.9 4.5 %depthwise.1 = (bf16[4,384,512]{2,1,0:T(8,128)(2,1)S(1)}, f32[4,21,64,128]{3,2,1,0:T(8,128)S(1)}, f32[384,256]{1,0:T(8,128)S(1)}, bf16[384,384]{1,0:T(8,128)(2,1)S(1)}, f32[8,128]{1,0:T(8,128)S(1)}) custom-call(s32[4]{0:T(128)S(1)} %copy-done.3, bf16[32,32,128]{2,1,0:T(8,128)(2,1)S(1)} %all-to-all-done.tiles_ref, ...), custom_call_target="tpu_custom_call" | custom-call | flops 2147483648 | bytes 1024 | tf_op jit(solution)/shard_map/depthwise/pallas_call | solution.py:419
  32.4 1.9 %collective-permute-done.6.refs_4_ = bf16[384,256]{1,0:T(8,128)(2,1)S(1)} collective-permute-done((bf16[384,256]{1,0:T(8,128)(2,1)S(1)}, bf16[384,256]{1,0:T(8,128)(2,1)S(1)}, u32[]{:S(2)}, u32[]{:S(2)}) %collective-permute-start.6) | collective-permute-done | bytes 196640 | tf_op jit(solution)/shard_map/ppermute | solution.py:700
  36.3 6.1 %forward_and_backward.1 = (bf16[32,24,128]{2,1,0:T(8,128)(2,1)}, bf16[4,288,256]{2,1,0:T(8,128)(2,1)S(1)}, bf16[4,288,256]{2,1,0:T(8,128)(2,1)S(1)}, bf16[4,384,...) custom-call(s32[4]{0:T(128)S(1)} %copy-done.3, bf16[4,384,512]{2,1,0:T(8,128)(2,1)S(1)} %get-tuple-element.49.dw_out, ...), custom_call_target="tpu_custom_call" | custom-call | flops 2147483648 | bytes 16777216 | tf_op jit(solution)/shard_map/forward_and_backward/pallas_call | solution.py:533
  42.7 1.8 %collective-permute-done.10.other_ref = bf16[4,288,256]{2,1,0:T(8,128)(2,1)S(1)} collective-permute-done((bf16[4,288,256]{2,1,0:T(8,128)(2,1)S(1)}, bf16[4,288,256]{2,1,0:T(8,128)(2,1)S(1)}, u32[]{:S(2)}, u32[]{:S(2)}) %collective-permute-start.10) | collective-permute-done | bytes 589856 | tf_op jit(solution)/shard_map/ppermute | solution.py:697
  44.6 1.5 %collective-permute-start.11 = (bf16[288,256]{1,0:T(8,128)(2,1)S(1)}, bf16[288,256]{1,0:T(8,128)(2,1)S(1)}, u32[]{:S(2)}, u32[]{:S(2)}) collective-permute-start(bf16[288,256]{1,0:T(8,128)(2,1)S(1)} %get-tuple-element.71), channel_id=1, source_target_pairs={{0,8},{4,12},{8,0},{12,4},{16,24},{20,28},{24,16},{28,20},{1,9},{5... | collective-permute-start | bytes 442376 | tf_op jit(solution)/shard_map/ppermute | solution.py:697
  46.1 1.5 %collective-permute-start.12 = (bf16[288,256]{1,0:T(8,128)(2,1)S(1)}, bf16[288,256]{1,0:T(8,128)(2,1)S(1)}, u32[]{:S(2)}, u32[]{:S(2)}) collective-permute-start(bf16[288,256]{1,0:T(8,128)(2,1)S(1)} %get-tuple-element.72), channel_id=1, source_target_pairs={{0,16},{4,20},{8,24},{12,28},{16,0},{20,4},{24,8},{28,12},{1,17},{... | collective-permute-start | bytes 442376 | tf_op jit(solution)/shard_map/ppermute | solution.py:697
  48.1 3.4 %depth_grad.1.depth_ref = bf16[3,32,256]{2,1,0:T(8,128)(2,1)S(1)} custom-call(s32[4]{0:T(128)S(1)} %copy-done.3, bf16[4,384,256]{2,1,0:T(8,128)(2,1)S(1)} %get-tuple-element.67.grad_pre_ref, bf16[4,512,256]{2,1,0:T(8,128)(2,1)S(1)} %get-tuple-element.68.point, f32[4,21,64,128]{3,2,1,0:T(8,128)S(1)} %get-tuple-element.69.spread), custom_call_target="tpu_custom_call" | custom-call | flops 67108864 | bytes 16777216 | tf_op jit(solution)/shard_map/depth_grad/pallas_call | solution.py:593
  51.6 3.4 %collective-permute-done.12.refs_2_ = bf16[288,256]{1,0:T(8,128)(2,1)S(1)} collective-permute-done((bf16[288,256]{1,0:T(8,128)(2,1)S(1)}, bf16[288,256]{1,0:T(8,128)(2,1)S(1)}, u32[]{:S(2)}, u32[]{:S(2)}) %collective-permute-start.12) | collective-permute-done | bytes 147488 | tf_op jit(solution)/shard_map/ppermute | solution.py:697
  56.0 2.4 %collective-permute-start.15 = (bf16[128,256]{1,0:T(8,128)(2,1)S(1)}, bf16[128,256]{1,0:T(8,128)(2,1)S(1)}, u32[]{:S(2)}, u32[]{:S(2)}) collective-permute-start(bf16[128,256]{1,0:T(8,128)(2,1)S(1)} %get-tuple-element.76), channel_id=1, source_target_pairs={{0,2},{1,3},{2,0},{3,1},{4,6},{5,7},{6,4},{7,5},{8,10},{9,11},{10,... | collective-permute-start | bytes 196616 | tf_op jit(solution)/shard_map/ppermute | solution.py:700
  58.3 1.7 %collective-permute-start.16 = (bf16[128,256]{1,0:T(8,128)(2,1)S(1)}, bf16[128,256]{1,0:T(8,128)(2,1)S(1)}, u32[]{:S(2)}, u32[]{:S(2)}) collective-permute-start(bf16[128,256]{1,0:T(8,128)(2,1)S(1)} %get-tuple-element.77), channel_id=1, source_target_pairs={{0,3},{1,2},{2,1},{3,0},{4,7},{5,6},{6,5},{7,4},{8,11},{9,10},{10,... | collective-permute-start | bytes 196616 | tf_op jit(solution)/shard_map/ppermute | solution.py:700
  60.1 3.3 %all-to-all-start.1 = ((bf16[32,24,128]{2,1,0:T(8,128)(2,1)}), bf16[32,24,128]{2,1,0:T(8,128)(2,1)S(1)}, u32[]{:S(2)}, u32[]{:S(2)}) async-start(bf16[32,24,128]{2,1,0:T(8,128)(2,1)} %get-tuple-element.65), calls=%async_computation.1 | async-start | bytes 393216 | tf_op jit(solution)/shard_map/all_to_all | solution.py:704
  64.4 1.8 %collective-permute-start.19 = (bf16[128,256]{1,0:T(8,128)(2,1)S(1)}, bf16[128,256]{1,0:T(8,128)(2,1)S(1)}, u32[]{:S(2)}, u32[]{:S(2)}) collective-permute-start(bf16[128,256]{1,0:T(8,128)(2,1)S(1)} %add_convert_fusion.refs_0_), channel_id=1, source_target_pairs={{0,24},{4,28},{8,16},{12,20},{16,8},{20,12},{24,0},{28,4},{1,25},{... | collective-permute-start | bytes 196616 | tf_op jit(solution)/shard_map/ppermute | solution.py:697
  68.0 2.1 %collective-permute-done.19.refs_3_ = bf16[128,256]{1,0:T(8,128)(2,1)S(1)} collective-permute-done((bf16[128,256]{1,0:T(8,128)(2,1)S(1)}, bf16[128,256]{1,0:T(8,128)(2,1)S(1)}, u32[]{:S(2)}, u32[]{:S(2)}) %collective-permute-start.19) | collective-permute-done | bytes 65568 | tf_op jit(solution)/shard_map/ppermute | solution.py:697
  70.1 1.5 %collective-permute-done.18.refs_2_ = bf16[128,256]{1,0:T(8,128)(2,1)S(1)} collective-permute-done((bf16[128,256]{1,0:T(8,128)(2,1)S(1)}, bf16[128,256]{1,0:T(8,128)(2,1)S(1)}, u32[]{:S(2)}, u32[]{:S(2)}) %collective-permute-start.18) | collective-permute-done | bytes 65568 | tf_op jit(solution)/shard_map/ppermute | solution.py:697
  72.8 1.0 %place_output.1 = (bf16[8,64,192]{2,1,0:T(8,128)(2,1)}, f32[8,128]{1,0:T(8,128)S(1)}) custom-call(bf16[32,24,128]{2,1,0:T(8,128)(2,1)S(1)} %all-to-all-done.1.tiles_ref), custom_call_target="tpu_custom_call" | custom-call | tf_op jit(solution)/shard_map/place_output/pallas_call | solution.py:291
  73.8 1.5 %place_grads.1 = (f32[256,256]{1,0:T(8,128)}, f32[1,512,256]{2,1,0:T(8,128)}, f32[1,9,512]{2,1,0:T(8,128)S(1)}) custom-call(s32[4]{0:T(128)S(1)} %copy-done.3, bf16[128,256]{1,0:T(8,128)(2,1)S(1)} %add_convert_fusion.refs_0_, bf16[128,256]{1,0:T(8,128)(2,1)S(1)} %collective-permute-done.17.refs_1_, bf16[128,256]{1,0:T(8,128)(2,1)S(1)} %collective-permute-done.18.refs_2_, ...), custom_call_target="tpu_custom_call" | custom-call | tf_op jit(solution)/shard_map/place_grads/pallas_call | solution.py:673
  (49 shorter events, 10.4 us)
Async XLA Ops:
  2.7 25.2 %all-to-all-start = ((bf16[32,32,128]{2,1,0:T(8,128)(2,1)}), bf16[32,32,128]{2,1,0:T(8,128)(2,1)S(1)}, u32[]{:S(2)}, u32[]{:S(2)}) async-start(bf16[32,32,128]{2,1,0:T(8,128)(2,1)} %send_cotangent.1), calls=%async_computation | async-start | bytes 524288 | tf_op jit(solution)/shard_map/all_to_all | solution.py:704
  12.1 3.2 %collective-permute-start = (bf16[4,80,512]{2,1,0:T(8,128)(2,1)S(1)}, bf16[4,80,512]{2,1,0:T(8,128)(2,1)S(1)}, u32[]{:S(2)}, u32[]{:S(2)}) collective-permute-start(bf16[4,80,512]{2,1,0:T(8,128)(2,1)S(1)} %get-tuple-element.44), channel_id=1, source_target_pairs={{0,4},{4,0},{8,12},{12,8},{16,20},{20,16},{24,28},{28,24},{1,5},{5... | collective-permute-start | bytes 983048 | tf_op jit(solution)/shard_map/ppermute | solution.py:697
  12.7 15.2 %collective-permute-start.5 = (bf16[384,256]{1,0:T(8,128)(2,1)S(1)}, bf16[384,256]{1,0:T(8,128)(2,1)S(1)}, u32[]{:S(2)}, u32[]{:S(2)}) collective-permute-start(bf16[384,256]{1,0:T(8,128)(2,1)S(1)} %halve_weights.1), channel_id=1, source_target_pairs={{0,2},{1,3},{2,0},{3,1},{4,6},{5,7},{6,4},{7,5},{8,10},{9,11},{10,... | collective-permute-start | bytes 589832 | tf_op jit(solution)/shard_map/ppermute | solution.py:700
  15.4 12.5 %collective-permute-start.1 = (bf16[160,512]{1,0:T(8,128)(2,1)S(1)}, bf16[160,512]{1,0:T(8,128)(2,1)S(1)}, u32[]{:S(2)}, u32[]{:S(2)}) collective-permute-start(bf16[160,512]{1,0:T(8,128)(2,1)S(1)} %get-tuple-element.46), channel_id=1, source_target_pairs={{0,8},{4,12},{8,0},{12,4},{16,24},{20,28},{24,16},{28,20},{1,9},{5... | collective-permute-start | bytes 491528 | tf_op jit(solution)/shard_map/ppermute | solution.py:697
  16.9 10.9 %collective-permute-start.2 = (bf16[160,512]{1,0:T(8,128)(2,1)S(1)}, bf16[160,512]{1,0:T(8,128)(2,1)S(1)}, u32[]{:S(2)}, u32[]{:S(2)}) collective-permute-start(bf16[160,512]{1,0:T(8,128)(2,1)S(1)} %get-tuple-element.47), channel_id=1, source_target_pairs={{0,16},{4,20},{8,24},{12,28},{16,0},{20,4},{24,8},{28,12},{1,17},{... | collective-permute-start | bytes 491528 | tf_op jit(solution)/shard_map/ppermute | solution.py:697
  18.4 9.5 %collective-permute-start.3 = (bf16[160,512]{1,0:T(8,128)(2,1)S(1)}, bf16[160,512]{1,0:T(8,128)(2,1)S(1)}, u32[]{:S(2)}, u32[]{:S(2)}) collective-permute-start(bf16[160,512]{1,0:T(8,128)(2,1)S(1)} %get-tuple-element.48), channel_id=1, source_target_pairs={{0,24},{4,28},{8,16},{12,20},{16,8},{20,12},{24,0},{28,4},{1,25},{... | collective-permute-start | bytes 491528 | tf_op jit(solution)/shard_map/ppermute | solution.py:697
  19.0 13.4 %collective-permute-start.4 = (bf16[384,256]{1,0:T(8,128)(2,1)S(1)}, bf16[384,256]{1,0:T(8,128)(2,1)S(1)}, u32[]{:S(2)}, u32[]{:S(2)}) collective-permute-start(bf16[384,256]{1,0:T(8,128)(2,1)S(1)} %halve_weights.1), channel_id=1, source_target_pairs={{0,1},{1,0},{2,3},{3,2},{4,5},{5,4},{6,7},{7,6},{8,9},{9,8},{10,11... | collective-permute-start | bytes 589832 | tf_op jit(solution)/shard_map/ppermute | solution.py:700
  27.9 6.4 %collective-permute-start.6 = (bf16[384,256]{1,0:T(8,128)(2,1)S(1)}, bf16[384,256]{1,0:T(8,128)(2,1)S(1)}, u32[]{:S(2)}, u32[]{:S(2)}) collective-permute-start(bf16[384,256]{1,0:T(8,128)(2,1)S(1)} %collective-permute-done.5.refs_3_), channel_id=1, source_target_pairs={{0,1},{1,0},{2,3},{3,2},{4,5},{5,4},{6,7},{7,6},{8,9},{9,8},{10,11... | collective-permute-start | bytes 589832 | tf_op jit(solution)/shard_map/ppermute | solution.py:700
  34.3 1.7 %collective-permute-start.8 = (bf16[384,256]{1,0:T(8,128)(2,1)S(1)}, bf16[384,256]{1,0:T(8,128)(2,1)S(1)}, u32[]{:S(2)}, u32[]{:S(2)}) collective-permute-start(bf16[384,256]{1,0:T(8,128)(2,1)S(1)} %collective-permute-done.5.refs_3_), channel_id=1, source_target_pairs={{0,4},{4,0},{8,12},{12,8},{16,20},{20,16},{24,28},{28,24},{1,5},{5... | collective-permute-start | bytes 589832 | tf_op jit(solution)/shard_map/ppermute | solution.py:697
  42.4 2.1 %collective-permute-start.10 = (bf16[4,288,256]{2,1,0:T(8,128)(2,1)S(1)}, bf16[4,288,256]{2,1,0:T(8,128)(2,1)S(1)}, u32[]{:S(2)}, u32[]{:S(2)}) collective-permute-start(bf16[4,288,256]{2,1,0:T(8,128)(2,1)S(1)} %get-tuple-element.58), channel_id=1, source_target_pairs={{0,4},{4,0},{8,12},{12,8},{16,20},{20,16},{24,28},{28,24},{1,5},{5... | collective-permute-start | bytes 1769480 | tf_op jit(solution)/shard_map/ppermute | solution.py:697
  44.6 7.0 %collective-permute-start.11 = (bf16[288,256]{1,0:T(8,128)(2,1)S(1)}, bf16[288,256]{1,0:T(8,128)(2,1)S(1)}, u32[]{:S(2)}, u32[]{:S(2)}) collective-permute-start(bf16[288,256]{1,0:T(8,128)(2,1)S(1)} %get-tuple-element.71), channel_id=1, source_target_pairs={{0,8},{4,12},{8,0},{12,4},{16,24},{20,28},{24,16},{28,20},{1,9},{5... | collective-permute-start | bytes 442376 | tf_op jit(solution)/shard_map/ppermute | solution.py:697
  46.1 8.9 %collective-permute-start.12 = (bf16[288,256]{1,0:T(8,128)(2,1)S(1)}, bf16[288,256]{1,0:T(8,128)(2,1)S(1)}, u32[]{:S(2)}, u32[]{:S(2)}) collective-permute-start(bf16[288,256]{1,0:T(8,128)(2,1)S(1)} %get-tuple-element.72), channel_id=1, source_target_pairs={{0,16},{4,20},{8,24},{12,28},{16,0},{20,4},{24,8},{28,12},{1,17},{... | collective-permute-start | bytes 442376 | tf_op jit(solution)/shard_map/ppermute | solution.py:697
  47.6 7.4 %collective-permute-start.13 = (bf16[288,256]{1,0:T(8,128)(2,1)S(1)}, bf16[288,256]{1,0:T(8,128)(2,1)S(1)}, u32[]{:S(2)}, u32[]{:S(2)}) collective-permute-start(bf16[288,256]{1,0:T(8,128)(2,1)S(1)} %get-tuple-element.73), channel_id=1, source_target_pairs={{0,24},{4,28},{8,16},{12,20},{16,8},{20,12},{24,0},{28,4},{1,25},{... | collective-permute-start | bytes 442376 | tf_op jit(solution)/shard_map/ppermute | solution.py:697
  55.6 7.8 %collective-permute-start.14 = (bf16[128,256]{1,0:T(8,128)(2,1)S(1)}, bf16[128,256]{1,0:T(8,128)(2,1)S(1)}, u32[]{:S(2)}, u32[]{:S(2)}) collective-permute-start(bf16[128,256]{1,0:T(8,128)(2,1)S(1)} %get-tuple-element.75), channel_id=1, source_target_pairs={{0,1},{1,0},{2,3},{3,2},{4,5},{5,4},{6,7},{7,6},{8,9},{9,8},{10,11... | collective-permute-start | bytes 196616 | tf_op jit(solution)/shard_map/ppermute | solution.py:700
  56.0 7.5 %collective-permute-start.15 = (bf16[128,256]{1,0:T(8,128)(2,1)S(1)}, bf16[128,256]{1,0:T(8,128)(2,1)S(1)}, u32[]{:S(2)}, u32[]{:S(2)}) collective-permute-start(bf16[128,256]{1,0:T(8,128)(2,1)S(1)} %get-tuple-element.76), channel_id=1, source_target_pairs={{0,2},{1,3},{2,0},{3,1},{4,6},{5,7},{6,4},{7,5},{8,10},{9,11},{10,... | collective-permute-start | bytes 196616 | tf_op jit(solution)/shard_map/ppermute | solution.py:700
  58.3 6.1 %collective-permute-start.16 = (bf16[128,256]{1,0:T(8,128)(2,1)S(1)}, bf16[128,256]{1,0:T(8,128)(2,1)S(1)}, u32[]{:S(2)}, u32[]{:S(2)}) collective-permute-start(bf16[128,256]{1,0:T(8,128)(2,1)S(1)} %get-tuple-element.77), channel_id=1, source_target_pairs={{0,3},{1,2},{2,1},{3,0},{4,7},{5,6},{6,5},{7,4},{8,11},{9,10},{10,... | collective-permute-start | bytes 196616 | tf_op jit(solution)/shard_map/ppermute | solution.py:700
  60.1 12.7 %all-to-all-start.1 = ((bf16[32,24,128]{2,1,0:T(8,128)(2,1)}), bf16[32,24,128]{2,1,0:T(8,128)(2,1)S(1)}, u32[]{:S(2)}, u32[]{:S(2)}) async-start(bf16[32,24,128]{2,1,0:T(8,128)(2,1)} %get-tuple-element.65), calls=%async_computation.1 | async-start | bytes 393216 | tf_op jit(solution)/shard_map/all_to_all | solution.py:704
  64.4 5.7 %collective-permute-start.19 = (bf16[128,256]{1,0:T(8,128)(2,1)S(1)}, bf16[128,256]{1,0:T(8,128)(2,1)S(1)}, u32[]{:S(2)}, u32[]{:S(2)}) collective-permute-start(bf16[128,256]{1,0:T(8,128)(2,1)S(1)} %add_convert_fusion.refs_0_), channel_id=1, source_target_pairs={{0,24},{4,28},{8,16},{12,20},{16,8},{20,12},{24,0},{28,4},{1,25},{... | collective-permute-start | bytes 196616 | tf_op jit(solution)/shard_map/ppermute | solution.py:697
  66.2 5.3 %collective-permute-start.18 = (bf16[128,256]{1,0:T(8,128)(2,1)S(1)}, bf16[128,256]{1,0:T(8,128)(2,1)S(1)}, u32[]{:S(2)}, u32[]{:S(2)}) collective-permute-start(bf16[128,256]{1,0:T(8,128)(2,1)S(1)} %add_convert_fusion.refs_0_), channel_id=1, source_target_pairs={{0,16},{4,20},{8,24},{12,28},{16,0},{20,4},{24,8},{28,12},{1,17},{... | collective-permute-start | bytes 196616 | tf_op jit(solution)/shard_map/ppermute | solution.py:697
  67.2 4.6 %collective-permute-start.17 = (bf16[128,256]{1,0:T(8,128)(2,1)S(1)}, bf16[128,256]{1,0:T(8,128)(2,1)S(1)}, u32[]{:S(2)}, u32[]{:S(2)}) collective-permute-start(bf16[128,256]{1,0:T(8,128)(2,1)S(1)} %add_convert_fusion.refs_0_), channel_id=1, source_target_pairs={{0,8},{4,12},{8,0},{12,4},{16,24},{20,28},{24,16},{28,20},{1,9},{5... | collective-permute-start | bytes 196616 | tf_op jit(solution)/shard_map/ppermute | solution.py:697
  68.0 5.8 %collective-permute-start.20 = (bf16[128,256]{1,0:T(8,128)(2,1)S(1)}, bf16[128,256]{1,0:T(8,128)(2,1)S(1)}, u32[]{:S(2)}, u32[]{:S(2)}) collective-permute-start(bf16[128,256]{1,0:T(8,128)(2,1)S(1)} %add_convert_fusion.refs_0_), channel_id=1, source_target_pairs={{0,4},{4,0},{8,12},{12,8},{16,20},{20,16},{24,28},{28,24},{1,5},{5... | collective-permute-start | bytes 196616 | tf_op jit(solution)/shard_map/ppermute | solution.py:697
  70.1 3.7 %collective-permute-start.23 = (bf16[128,256]{1,0:T(8,128)(2,1)S(1)}, bf16[128,256]{1,0:T(8,128)(2,1)S(1)}, u32[]{:S(2)}, u32[]{:S(2)}) collective-permute-start(bf16[128,256]{1,0:T(8,128)(2,1)S(1)} %collective-permute-done.19.refs_3_), channel_id=1, source_target_pairs={{0,4},{4,0},{8,12},{12,8},{16,20},{20,16},{24,28},{28,24},{1,5},{5... | collective-permute-start | bytes 196616 | tf_op jit(solution)/shard_map/ppermute | solution.py:697
  71.6 2.2 %collective-permute-start.22 = (bf16[128,256]{1,0:T(8,128)(2,1)S(1)}, bf16[128,256]{1,0:T(8,128)(2,1)S(1)}, u32[]{:S(2)}, u32[]{:S(2)}) collective-permute-start(bf16[128,256]{1,0:T(8,128)(2,1)S(1)} %collective-permute-done.18.refs_2_), channel_id=1, source_target_pairs={{0,4},{4,0},{8,12},{12,8},{16,20},{20,16},{24,28},{28,24},{1,5},{5... | collective-permute-start | bytes 196616 | tf_op jit(solution)/shard_map/ppermute | solution.py:697
  71.8 2.0 %collective-permute-start.21 = (bf16[128,256]{1,0:T(8,128)(2,1)S(1)}, bf16[128,256]{1,0:T(8,128)(2,1)S(1)}, u32[]{:S(2)}, u32[]{:S(2)}) collective-permute-start(bf16[128,256]{1,0:T(8,128)(2,1)S(1)} %collective-permute-done.17.refs_1_), channel_id=1, source_target_pairs={{0,4},{4,0},{8,12},{12,8},{16,20},{20,16},{24,28},{28,24},{1,5},{5... | collective-permute-start | bytes 196616 | tf_op jit(solution)/shard_map/ppermute | solution.py:697
  (6 other events, 53.2 us)
